TPU v7x, 32 devices: a whole 2x2x4 slice. The times are simulated.
32 devices in a mesh: dp: 8 (over y, x, core), tensor: 4 (over z).
Axes of the slice: x: 2, y: 2, z: 4, core: 2. Of those that a mesh axis runs over, the one named last changes fastest.
Arguments:
- inputs: bfloat16 [16384, 1280], P(('dp', 'tensor')), may hold values from -6 to 6
- cotangent: bfloat16 [16384, 1280], P(('dp', 'tensor')), may hold values from -6 to 6
- gain_attn: float32 [1280], replicated, may hold values from 0.1 to 1.9
- gain_mlp: float32 [1280], replicated, may hold values from 0.1 to 1.9
- query_scale: float32 [80], replicated, may hold values from -0.5 to 1.5
- w_query: bfloat16 [1280, 1280], P(None, 'tensor'), may hold values from -0.15625 to 0.15625
- w_key: bfloat16 [1280, 1280], P(None, 'tensor'), may hold values from -0.15625 to 0.15625
- w_value: bfloat16 [1280, 1280], P(None, 'tensor'), may hold values from -0.15625 to 0.15625
- w_out: bfloat16 [1280, 1280], P('tensor'), may hold values from -1 to 1
- w_up: bfloat16 [1280, 1280], P(None, 'tensor'), may hold values from -0.15625 to 0.15625
- w_down: bfloat16 [1280, 1280], P('tensor'), may hold values from -0.15625 to 0.15625
- lengths: int32 [8], P('dp'), may hold values from 1024 to 2048, as said below
- offsets: int32 [8], P('dp'), may hold values from 0 to 1024, as said below
Outputs:
- output: bfloat16 [16384, 1280], P(('dp', 'tensor'))
- grad_input: float32 [16384, 1280], P(('dp', 'tensor'))
- grad_gain_attn: float32 [1280], replicated
- grad_gain_mlp: float32 [1280], replicated
- grad_query_scale: float32 [80], replicated
- grad_query: float32 [1280, 1280], P(None, 'tensor')
- grad_key: float32 [1280, 1280], P(None, 'tensor')
- grad_value: float32 [1280, 1280], P(None, 'tensor')
- grad_out: float32 [1280, 1280], P('tensor')
- grad_up: float32 [1280, 1280], P(None, 'tensor')
- grad_down: float32 [1280, 1280], P('tensor')
Inputs may be any that keep to these rules, and one draw needn't show every extreme that they name: `lengths`: one group's sequence fills all 2048 slots and another's is exactly 1024 long. `offsets`: a sequence never runs past its group's 2048 slots; the group whose length is 1024 starts at 1024.
All inputs are finite; a program needn't handle non-finite values.
Results may differ from a plain program's by a relative error of at most 0.018.
Values may be sent and summed in bfloat16 or wider, within the bound.
A program may use at most 256 MiB of HBM per device.

v0:
```python
import math

import jax
import jax.numpy as jnp
from jax import lax
from jax.sharding import PartitionSpec as P

EPSILON = 1e-06
LOG_TWO_E = 1.4426950408889634


def rms_forward(values, gain):
    inverse = lax.rsqrt(jnp.mean(values * values, axis=-1, keepdims=True) + EPSILON)
    return (values * inverse * gain, inverse)


def rms_backward(values, inverse, gain, grad_normed):
    scaled = values * inverse
    grad_gain = jnp.sum(grad_normed * scaled, axis=0)
    grad_scaled = grad_normed * gain
    grad_values = inverse * (
        grad_scaled - scaled * jnp.mean(grad_scaled * scaled, axis=-1, keepdims=True)
    )
    return (grad_values, grad_gain)


def contract_rows(left, right):
    return lax.dot_general(
        left, right, (((0,), (0,)), ((), ())), preferred_element_type=jnp.float32
    )


def contract_cols(left, right):
    return lax.dot_general(
        left, right, (((1,), (1,)), ((), ())), preferred_element_type=jnp.float32
    )


def silu_slope(values):
    sigmoid_v = jax.nn.sigmoid(values)
    return sigmoid_v * (1.0 + values * (1.0 - sigmoid_v))


def per_device(
    inputs,
    cotangent,
    gain_attn,
    gain_mlp,
    query_scale,
    w_query,
    w_key,
    w_value,
    w_out,
    w_up,
    w_down,
    lengths,
    offsets,
):
    local_rows = inputs.shape[0]
    seq_slots = local_rows * lax.axis_size("tensor")
    width_local = w_query.shape[1]
    head_dim = query_scale.shape[0]
    heads_local = width_local // head_dim
    slot_index = jnp.arange(seq_slots, dtype=jnp.int32)
    length = lengths[0]
    offset = offsets[0]
    key_ok = (slot_index >= offset) & (slot_index < offset + length)
    own_rows = lax.axis_index("tensor") * local_rows + jnp.arange(local_rows, dtype=jnp.int32)
    row_valid = ((own_rows >= offset) & (own_rows < offset + length)).astype(jnp.float32)
    residual = inputs.astype(jnp.float32)
    normed, inverse_one = rms_forward(residual, gain_attn)
    gathered = lax.all_gather(normed.astype(jnp.bfloat16), "tensor", axis=0, tiled=True)
    stacked_w = jnp.concatenate([w_query, w_key, w_value], axis=1)
    projected = jnp.dot(gathered, stacked_w, preferred_element_type=jnp.float32)
    query_raw = projected[:, :width_local]
    scale_const = LOG_TWO_E / math.sqrt(head_dim)
    factor = jnp.tile(jax.nn.softplus(query_scale) * scale_const, heads_local)
    query_low = (query_raw * factor).astype(jnp.bfloat16).reshape(seq_slots, heads_local, head_dim)
    key_low = (
        projected[:, width_local : 2 * width_local]
        .astype(jnp.bfloat16)
        .reshape(seq_slots, heads_local, head_dim)
    )
    value_low = (
        projected[:, 2 * width_local :]
        .astype(jnp.bfloat16)
        .reshape(seq_slots, heads_local, head_dim)
    )
    block_rows = min(512, seq_slots)
    block_count = seq_slots // block_rows

    def block_scores(block_index):
        first_row = block_index * block_rows
        last_row = first_row + block_rows
        query_pos = slot_index[first_row:last_row]
        key_pos = slot_index[:last_row]
        allowed = key_ok[None, :last_row] & (key_pos[None, :] <= query_pos[:, None]) | (
            key_pos[None, :] == query_pos[:, None]
        )
        scores = jnp.einsum(
            "qhe,khe->hqk",
            query_low[first_row:last_row],
            key_low[:last_row],
            preferred_element_type=jnp.float32,
        )
        return jnp.where(allowed[None], scores, -1e30)

    attended_parts = []
    logsum_parts = []
    for block_index in range(block_count):
        last_row = (block_index + 1) * block_rows
        scores = block_scores(block_index)
        highest = jnp.max(scores, axis=-1, keepdims=True)
        expo = jnp.exp(scores - highest)
        summed = jnp.sum(expo, axis=-1, keepdims=True)
        probs = (expo / summed).astype(jnp.bfloat16)
        attended_parts.append(
            jnp.einsum(
                "hqk,khe->qhe", probs, value_low[:last_row], preferred_element_type=jnp.float32
            )
        )
        logsum_parts.append(highest + jnp.log(summed))
    attended = jnp.concatenate(attended_parts, axis=0).reshape(seq_slots, width_local)
    attended_low = attended.astype(jnp.bfloat16)
    hidden_one = residual + lax.psum_scatter(
        jnp.dot(attended_low, w_out, preferred_element_type=jnp.float32).astype(jnp.bfloat16),
        "tensor",
        scatter_dimension=0,
        tiled=True,
    ).astype(jnp.float32)
    second, inverse_two = rms_forward(hidden_one, gain_mlp)
    second_low = second.astype(jnp.bfloat16)
    grad_hidden_out = cotangent.astype(jnp.float32) * row_valid[:, None]
    grad_low = grad_hidden_out.astype(jnp.bfloat16)
    second_all = lax.all_gather(second_low, "tensor", axis=0, tiled=True)
    before_act = jnp.dot(second_all, w_up, preferred_element_type=jnp.float32)
    activated = jax.nn.silu(before_act).astype(jnp.bfloat16)
    output = hidden_one + lax.psum_scatter(
        jnp.dot(activated, w_down, preferred_element_type=jnp.float32).astype(jnp.bfloat16),
        "tensor",
        scatter_dimension=0,
        tiled=True,
    ).astype(jnp.float32)
    grad_all = lax.all_gather(grad_low, "tensor", axis=0, tiled=True)
    grad_down = contract_rows(activated, grad_all)
    grad_act = contract_cols(grad_all, w_down)
    grad_pre = (grad_act * silu_slope(before_act)).astype(jnp.bfloat16)
    grad_up = contract_rows(second_all, grad_pre)
    grad_second = lax.psum_scatter(
        contract_cols(grad_pre, w_up).astype(jnp.bfloat16),
        "tensor",
        scatter_dimension=0,
        tiled=True,
    ).astype(jnp.float32)
    grad_back_two, grad_gain_two = rms_backward(hidden_one, inverse_two, gain_mlp, grad_second)
    grad_hidden = grad_hidden_out + grad_back_two
    branch_all = lax.all_gather(grad_hidden.astype(jnp.bfloat16), "tensor", axis=0, tiled=True)
    grad_w_out = contract_rows(attended_low, branch_all)
    grad_att_low = contract_cols(branch_all, w_out).astype(jnp.bfloat16)
    row_term = jnp.sum(
        (grad_att_low.astype(jnp.float32) * attended).reshape(seq_slots, heads_local, head_dim),
        axis=-1,
    )
    grad_att_heads = grad_att_low.reshape(seq_slots, heads_local, head_dim)
    grad_query_parts = []
    grad_key_acc = jnp.zeros((seq_slots, heads_local, head_dim), jnp.float32)
    grad_value_acc = jnp.zeros((seq_slots, heads_local, head_dim), jnp.float32)
    for block_index in range(block_count):
        first_row = block_index * block_rows
        last_row = first_row + block_rows
        probs_full = jnp.exp(block_scores(block_index) - logsum_parts[block_index])
        grad_att_block = grad_att_heads[first_row:last_row]
        grad_probs = jnp.einsum(
            "qhe,khe->hqk", grad_att_block, value_low[:last_row], preferred_element_type=jnp.float32
        )
        block_term = jnp.transpose(row_term[first_row:last_row])[:, :, None]
        grad_scores = (probs_full * (grad_probs - block_term)).astype(jnp.bfloat16)
        grad_query_parts.append(
            jnp.einsum(
                "hqk,khe->qhe", grad_scores, key_low[:last_row], preferred_element_type=jnp.float32
            )
        )
        grad_key_acc = grad_key_acc.at[:last_row].add(
            jnp.einsum(
                "hqk,qhe->khe",
                grad_scores,
                query_low[first_row:last_row],
                preferred_element_type=jnp.float32,
            )
        )
        grad_value_acc = grad_value_acc.at[:last_row].add(
            jnp.einsum(
                "hqk,qhe->khe",
                probs_full.astype(jnp.bfloat16),
                grad_att_block,
                preferred_element_type=jnp.float32,
            )
        )
    grad_query_scaled = jnp.concatenate(grad_query_parts, axis=0).reshape(seq_slots, width_local)
    grad_factor = jnp.sum(
        (grad_query_scaled * query_raw).reshape(seq_slots, heads_local, head_dim), axis=(0, 1)
    )
    grad_scale = grad_factor * jax.nn.sigmoid(query_scale) * scale_const
    grad_stacked = jnp.concatenate(
        [
            (grad_query_scaled * factor).astype(jnp.bfloat16),
            grad_key_acc.reshape(seq_slots, width_local).astype(jnp.bfloat16),
            grad_value_acc.reshape(seq_slots, width_local).astype(jnp.bfloat16),
        ],
        axis=1,
    )
    grad_stacked_w = contract_rows(gathered, grad_stacked)
    grad_first = lax.psum_scatter(
        contract_cols(grad_stacked, stacked_w).astype(jnp.bfloat16),
        "tensor",
        scatter_dimension=0,
        tiled=True,
    ).astype(jnp.float32)
    grad_back_one, grad_gain_one = rms_backward(residual, inverse_one, gain_attn, grad_first)
    grad_input = grad_hidden + grad_back_one
    small_sums = lax.psum((grad_gain_one, grad_gain_two, grad_scale), ("dp", "tensor"))
    weight_sums = lax.psum(
        (
            grad_stacked_w[:, :width_local],
            grad_stacked_w[:, width_local : 2 * width_local],
            grad_stacked_w[:, 2 * width_local :],
            grad_w_out,
            grad_up,
            grad_down,
        ),
        "dp",
    )
    return (
        output.astype(jnp.bfloat16),
        grad_input,
        small_sums[0],
        small_sums[1],
        small_sums[2],
        weight_sums[0],
        weight_sums[1],
        weight_sums[2],
        weight_sums[3],
        weight_sums[4],
        weight_sums[5],
    )


def solution(mesh):
    return jax.shard_map(
        per_device,
        mesh=mesh,
        in_specs=(
            P(("dp", "tensor"), None),
            P(("dp", "tensor"), None),
            P(),
            P(),
            P(),
            P(None, "tensor"),
            P(None, "tensor"),
            P(None, "tensor"),
            P("tensor", None),
            P(None, "tensor"),
            P("tensor", None),
            P("dp"),
            P("dp"),
        ),
        out_specs=(
            P(("dp", "tensor"), None),
            P(("dp", "tensor"), None),
            P(),
            P(),
            P(),
            P(None, "tensor"),
            P(None, "tensor"),
            P(None, "tensor"),
            P("tensor", None),
            P(None, "tensor"),
            P("tensor", None),
        ),
        check_vma=False,
    )
```

profile of v0, /device:TPU:27, one launch (start us, length us, event | category | flops | bytes accessed | tf_op | source)
XLA Modules:
  0.0 1115.5 jit_solution(5783088377174702782)
XLA Ops:
  9.6 2.8 fusion.64
  21.5 87.6 %all-gather.5.cloned.1.call-done = bf16[2048,1280]{1,0:T(8,128)(2,1)} async-done(((bf16[512,1280]{1,0:T(8,128)(2,1)}), bf16[2048,1280]{1,0:T(8,128)(2,1)}) %all-gather.5.cloned.1.call-update) | async-done | bytes 5242896 | tf_op jit(solution)/shard_map/all_gather | solution.py:72
  109.2 8.4 fusion.121
  127.4 2.2 fusion.10
  130.7 2.6 fusion.91
  133.4 6.7 select_reduce_fusion.1
  140.1 7.7 fusion.2
  147.8 6.3 fusion.93
  154.2 2.8 select_reduce_fusion
  157.0 4.0 fusion
  163.0 4.9 fusion.94
  170.8 4.6 convolution_convert_fusion.3
  175.5 94.2 %reduce-scatter.5.cloned.1.call-done = bf16[512,1280]{1,0:T(8,128)(2,1)} async-done(((bf16[2048,1280]{1,0:T(8,128)(2,1)}), bf16[512,1280]{1,0:T(8,128)(2,1)}) %reduce-scatter.5.cloned.1.call-update) | async-done | bytes 1310736 | tf_op jit(solution)/shard_map/reduce_scatter | solution.py:125
  273.3 2.7 fusion.68
  276.0 93.9 %all-gather.7.cloned.1.call-done = bf16[2048,1280]{1,0:T(8,128)(2,1)} async-done(((bf16[512,1280]{1,0:T(8,128)(2,1)}), bf16[2048,1280]{1,0:T(8,128)(2,1)}) %all-gather.7.cloned.1.call-update) | async-done | bytes 5242896 | tf_op jit(solution)/shard_map/all_gather | solution.py:135
  370.0 6.1 fusion.122
  376.0 92.4 %all-gather.9.cloned.1.call-done = bf16[2048,1280]{1,0:T(8,128)(2,1)} async-done(((bf16[512,1280]{1,0:T(8,128)(2,1)}), bf16[2048,1280]{1,0:T(8,128)(2,1)}) %all-gather.9.cloned.1.call-update) | async-done | bytes 5242896 | tf_op jit(solution)/shard_map/all_gather | solution.py:144
  468.5 5.6 fusion.56
  475.2 4.6 convolution_convert_fusion.1
  480.3 93.8 %reduce-scatter.9.cloned.1.call-done = bf16[512,1280]{1,0:T(8,128)(2,1)} async-done(((bf16[2048,1280]{1,0:T(8,128)(2,1)}), bf16[512,1280]{1,0:T(8,128)(2,1)}) %reduce-scatter.9.cloned.1.call-update) | async-done | bytes 1310736 | tf_op jit(solution)/shard_map/reduce_scatter | solution.py:149
  574.1 2.5 fusion.63
  576.6 2.1 fusion.112
  578.9 96.6 %all-gather.11.cloned.1.call-done = bf16[2048,1280]{1,0:T(8,128)(2,1)} async-done(((bf16[512,1280]{1,0:T(8,128)(2,1)}), bf16[2048,1280]{1,0:T(8,128)(2,1)}) %all-gather.11.cloned.1.call-update) | async-done | bytes 5242896 | tf_op jit(solution)/shard_map/all_gather | solution.py:157
  675.5 6.3 bitcast_multiply_fusion
  684.1 3.4 fusion.88
  692.5 2.4 fusion.85
  694.9 3.3 multiply_convert_fusion.2
  698.3 2.2 convolution_bitcast_fusion.4
  701.6 7.4 fusion.41
  709.1 10.2 multiply_convert_fusion.1
  719.4 7.8 fusion.53
  727.1 9.8 multiply_convert_fusion
  737.0 2.7 convolution_bitcast_fusion.6
  748.2 9.2 convolution_convert_fusion
  759.4 4.9 convolution_convert_fusion.2
  764.3 6.7 fusion.124
  771.1 6.0 fusion.113
  777.1 5.7 fusion.123
  782.8 5.2 fusion.76
  788.1 2.4 fusion.114
  790.5 3.0 multiply_reduce_fusion
  793.6 58.1 %reduce-scatter.11.cloned.1.call-done = bf16[512,1280]{1,0:T(8,128)(2,1)} async-done(((bf16[2048,1280]{1,0:T(8,128)(2,1)}), bf16[512,1280]{1,0:T(8,128)(2,1)}) %reduce-scatter.11.cloned.1.call-update) | async-done | bytes 1310736 | tf_op jit(solution)/shard_map/reduce_scatter | solution.py:213
  851.7 2.2 fusion.66
  853.9 43.0 %all-reduce.2 = (f32[1280]{0:T(1024)}, f32[1280]{0:T(1024)}, f32[80]{0:T(128)}) all-reduce(f32[1280]{0:T(1024)S(1)} %get-tuple-element.125, f32[1280]{0:T(1024)S(1)} %get-tuple-element.123, f32[80]{0:T(128)S(1)} %fusion.101), channel_id=1, replica_groups=mesh['dp'=8,'tensor'=4] {'dp','tensor'}, use_global_device_ids=true, to_apply=%region_18.19 | all-reduce | flops 2640 | bytes 21120 | tf_op jit(solution)/shard_map/psum | solution.py:221
  896.9 52.4 %reduce-scatter.7.cloned.1.call-done = bf16[512,1280]{1,0:T(8,128)(2,1)} async-done(((bf16[2048,1280]{1,0:T(8,128)(2,1)}), bf16[512,1280]{1,0:T(8,128)(2,1)}) %reduce-scatter.7.cloned.1.call-update) | async-done | bytes 1310736 | tf_op jit(solution)/shard_map/reduce_scatter | solution.py:138
  949.3 5.0 fusion.59
  954.3 145.8 %all-reduce.6.cloned.1.call-done = (f32[1280,320]{0,1:T(8,128)}, f32[1280,320]{0,1:T(8,128)}, f32[1280,320]{0,1:T(8,128)}, f32[320,1280]{1,0:T(8,128)}, f32[1280,320]{0,1:T(8,128)}, /*index=5*/f32[320,1280]{1,0:T(8,128)}) async-done(((f32[1280,320]{0,1:T(8,128)}, f32[1280,320]{0,1:T(8,128)}, f32[1280,320]{0,1:T(8,128)}, f32[320,1280]{1,0:T(8,128)}, f32[1280,320]{0,1:T(8,128)}, ...) | async-done | bytes 9830416 | tf_op jit(solution)/shard_map/psum | solution.py:222
  1100.1 2.8 copy.53
  (264 shorter events, 55.9 us)
Async XLA Ops:
  7.2 163.7 %copy-start = (bf16[320,1280]{1,0:T(8,128)(2,1)S(1)}, bf16[320,1280]{1,0:T(8,128)(2,1)}, u32[]{:S(2)}) copy-start(bf16[320,1280]{1,0:T(8,128)(2,1)} %param.41) | copy-start | bytes 2457604
  7.2 6.6 copy-start.77
  7.2 101.9 %all-gather.5.cloned.1.call-start = ((), (), s32[]{:S(2)}) async-start(), calls=%async_computation.4 | async-start | bytes 6553600 | tf_op jit(solution)/shard_map/all_gather | solution.py:72
  9.0 6.0 copy-start.62
  9.6 6.5 copy-start.63
  12.4 257.3 %reduce-scatter.5.cloned.1.call-start = ((), (), s32[]{:S(2)}) async-start(), calls=%async_computation.5 | async-start | bytes 6553600 | tf_op jit(solution)/shard_map/reduce_scatter | solution.py:125
  13.9 106.0 %copy-start.73 = (f32[320]{0:T(512)}, f32[320]{0:T(512)S(1)}, u32[]{:S(2)}) copy-start(f32[320]{0:T(512)S(1)} %mul.171) | copy-start | bytes 3844
  14.3 109.4 %copy-start.29 = (pred[512,512]{0,1:T(8,128)(4,1)}, pred[512,512]{0,1:T(8,128)(4,1)S(1)}, u32[]{:S(2)}) copy-start(pred[512,512]{0,1:T(8,128)(4,1)S(1)} %compare_or_fusion.2) | copy-start | bytes 786436
  14.9 114.6 %copy-start.25 = (pred[512,1024]{1,0:T(8,128)(4,1)}, pred[512,1024]{1,0:T(8,128)(4,1)S(1)}, u32[]{:S(2)}) copy-start(pred[512,1024]{1,0:T(8,128)(4,1)S(1)} %compare_or_fusion.1) | copy-start | bytes 1572868
  20.6 140.4 %copy-start.14 = (pred[512,2048]{1,0:T(8,128)(4,1)}, pred[512,2048]{1,0:T(8,128)(4,1)S(1)}, u32[]{:S(2)}) copy-start(pred[512,2048]{1,0:T(8,128)(4,1)S(1)} %fusion.23) | copy-start | bytes 3145732
  21.5 126.3 %copy-start.19 = (pred[512,1536]{1,0:T(8,128)(4,1)}, pred[512,1536]{1,0:T(8,128)(4,1)S(1)}, u32[]{:S(2)}) copy-start(pred[512,1536]{1,0:T(8,128)(4,1)S(1)} %compare_or_fusion) | copy-start | bytes 2359300
  117.7 6.0 copy-start.67
  117.8 8.0 copy-start.27
  117.8 11.7 %copy-start.64 = (bf16[1024,320]{0,1:T(8,128)(2,1)}, bf16[1024,320]{0,1:T(8,128)(2,1)S(1)}, u32[]{:S(2)}) copy-start(bf16[1024,320]{0,1:T(8,128)(2,1)S(1)} %get-tuple-element.142) | copy-start | bytes 1966084
  118.0 15.4 %copy-start.23 = (bf16[1536,320]{0,1:T(8,128)(2,1)}, bf16[1536,320]{0,1:T(8,128)(2,1)S(1)}, u32[]{:S(2)}) copy-start(bf16[1536,320]{0,1:T(8,128)(2,1)S(1)} %get-tuple-element.143) | copy-start | bytes 2949124
  118.0 29.8 %copy-start.60 = (bf16[1536,320]{0,1:T(8,128)(2,1)}, bf16[1536,320]{0,1:T(8,128)(2,1)S(1)}, u32[]{:S(2)}) copy-start(bf16[1536,320]{0,1:T(8,128)(2,1)S(1)} %get-tuple-element.144) | copy-start | bytes 2949124
  119.9 34.2 %copy-start.17 = (bf16[2048,320]{0,1:T(8,128)(2,1)}, bf16[2048,320]{0,1:T(8,128)(2,1)S(1)}, u32[]{:S(2)}) copy-start(bf16[2048,320]{0,1:T(8,128)(2,1)S(1)} %get-tuple-element.145) | copy-start | bytes 3932164
  121.4 12.0 %copy-start.40 = (bf16[512,320]{0,1:T(8,128)(2,1)}, bf16[512,320]{0,1:T(8,128)(2,1)S(1)}, u32[]{:S(2)}) copy-start(bf16[512,320]{0,1:T(8,128)(2,1)S(1)} %get-tuple-element.155) | copy-start | bytes 983044
  121.4 32.8 %copy-start.31 = (bf16[512,320]{0,1:T(8,128)(2,1)}, bf16[512,320]{0,1:T(8,128)(2,1)S(1)}, u32[]{:S(2)}) copy-start(bf16[512,320]{0,1:T(8,128)(2,1)S(1)} %get-tuple-element.154) | copy-start | bytes 983044
  157.0 6.0 copy-start.2
  157.0 6.0 copy-start.51
  175.4 94.3 %copy-start.3 = (bf16[512,1280]{1,0:T(8,128)(2,1)S(1)}, bf16[512,1280]{1,0:T(8,128)(2,1)}, u32[]{:S(2)}) copy-start(bf16[512,1280]{1,0:T(8,128)(2,1)} %param.33) | copy-start | bytes 3932164
  175.5 96.2 %copy-start.69 = (f32[1280]{0:T(1024)S(1)}, f32[1280]{0:T(1024)}, u32[]{:S(2)}) copy-start(f32[1280]{0:T(1024)} %param.36) | copy-start | bytes 15364
  175.5 194.5 %all-gather.7.cloned.1.call-start = ((), (), s32[]{:S(2)}) async-start(), calls=%async_computation.6 | async-start | bytes 6553600 | tf_op jit(solution)/shard_map/all_gather | solution.py:135
  273.2 195.2 %all-gather.9.cloned.1.call-start = ((), (), s32[]{:S(2)}) async-start(), calls=%async_computation.8 | async-start | bytes 6553600 | tf_op jit(solution)/shard_map/all_gather | solution.py:144
  276.0 298.1 %reduce-scatter.9.cloned.1.call-start = ((), (), s32[]{:S(2)}) async-start(), calls=%async_computation.9 | async-start | bytes 6553600 | tf_op jit(solution)/shard_map/reduce_scatter | solution.py:149
  468.5 6.7 copy-start.75
  479.8 195.7 %all-gather.11.cloned.1.call-start = ((), (), s32[]{:S(2)}) async-start(), calls=%async_computation.10 | async-start | bytes 6553600 | tf_op jit(solution)/shard_map/all_gather | solution.py:157
  578.8 272.9 %reduce-scatter.11.cloned.1.call-start = ((), (), s32[]{:S(2)}) async-start(), calls=%async_computation.11 | async-start | bytes 6553600 | tf_op jit(solution)/shard_map/reduce_scatter | solution.py:213
  684.1 17.4 %copy-start.59 = (bf16[512,320]{0,1:T(8,128)(2,1)}, bf16[512,320]{0,1:T(8,128)(2,1)S(1)}, u32[]{:S(2)}) copy-start(bf16[512,320]{0,1:T(8,128)(2,1)S(1)} %get-tuple-element.150) | copy-start | bytes 983044
  701.5 7.5 copy-start.10
  701.6 7.4 copy-start.61
  701.6 17.7 %slice-start = ((s8[16777216]{0:T(1024)(128)(4,1)}), s8[4194304]{0:T(1024)(128)(4,1)S(1)}, s32[]{:S(2)}) async-start(s8[16777216]{0:T(1024)(128)(4,1)} %bitcast.155), calls=%async_computation.13 | async-start | bytes 8388608
  701.6 17.7 %slice-start.1 = ((s8[16777216]{0:T(1024)(128)(4,1)}), s8[4194304]{0:T(1024)(128)(4,1)S(1)}, s32[]{:S(2)}) async-start(s8[16777216]{0:T(1024)(128)(4,1)} %bitcast.155), calls=%async_computation.14 | async-start | bytes 8388608
  709.1 10.3 copy-start.13
  709.1 10.2 slice-start.2
  709.1 10.2 slice-start.3
  719.4 7.8 copy-start.58
  727.1 9.9 copy-start.18
  746.0 11.4 %copy-start.16 = (f32[2048,4,80]{0,2,1:T(8,128)}, f32[2048,4,80]{0,2,1:T(8,128)S(1)}, u32[]{:S(2)}) copy-start(f32[2048,4,80]{0,2,1:T(8,128)S(1)} %pad_maximum_fusion.2) | copy-start | bytes 7864324
  757.4 191.9 %reduce-scatter.7.cloned.1.call-start = ((), (), s32[]{:S(2)}) async-start(), calls=%async_computation.7 | async-start | bytes 6553600 | tf_op jit(solution)/shard_map/reduce_scatter | solution.py:138
  764.3 335.8 %all-reduce.6.cloned.1.call-start = ((), (), s32[]{:S(2)}) async-start(), calls=%async_computation.12 | async-start | bytes 19660800 | tf_op jit(solution)/shard_map/psum | solution.py:222
  771.1 6.0 copy-start.57
  771.1 11.7 %slice-start.6 = ((s8[5242880]{0:T(1024)(128)(4,1)}), s8[4194304]{0:T(1024)(128)(4,1)S(1)}, s32[]{:S(2)}) async-start(s8[5242880]{0:T(1024)(128)(4,1)} %bitcast.198), calls=%async_computation.19 | async-start | bytes 8388608
  790.5 61.2 %copy-start.4 = (bf16[512,1280]{1,0:T(8,128)(2,1)S(1)}, bf16[512,1280]{1,0:T(8,128)(2,1)}, u32[]{:S(2)}) copy-start(bf16[512,1280]{1,0:T(8,128)(2,1)} %param.33) | copy-start | bytes 3932164
  790.5 61.2 %copy-start.70 = (f32[1280]{0:T(1024)S(1)}, f32[1280]{0:T(1024)}, u32[]{:S(2)}) copy-start(f32[1280]{0:T(1024)} %param.35) | copy-start | bytes 15364
  790.5 61.2 %copy-start.72 = (f32[512]{0:T(512)S(1)}, f32[512]{0:T(512)}, u32[]{:S(2)}) copy-start(f32[512]{0:T(512)} %copy-done.71) | copy-start | bytes 6148
  793.5 155.8 %copy-start.9 = (bf16[512,1280]{1,0:T(8,128)(2,1)S(1)}, bf16[512,1280]{1,0:T(8,128)(2,1)}, u32[]{:S(2)}) copy-start(bf16[512,1280]{1,0:T(8,128)(2,1)} %reduce-scatter.5.cloned.1.call-done) | copy-start | bytes 3932164
  (50 other events, 132.4 us)
Sparse Core Ops, SparseCore 0:
  12.5 96.5 all-gather.4
  175.6 94.1 reduce-scatter.4
  273.4 96.5 all-gather.6
  372.0 96.4 all-gather.8
  479.9 94.0 reduce-scatter.8
  578.9 96.5 all-gather.10
  757.5 94.1 reduce-scatter.10
  854.0 95.2 reduce-scatter.6
  955.1 144.9 all-reduce.5
where the time goes:
time: 1120 us
  waiting for transfers between devices  815 us (73%)
  matrix products  160 us (14%)
  other arithmetic  44.7 us (4%)
  blocking collectives  43 us (4%)
  local copies, waits for them, and re-layouts  35.4 us (3%)
  between operations  16.5 us (1%)
    psum x1, waiting for transfers between devices, per_device(): lax.psum((grad_stacked_w[:, :width_local], grad_stacked_w[:, width_local:...  146 us
    all_gather x1, waiting for transfers between devices, per_device(): lax.all_gather(grad_hidden.astype(jnp.bfloat16), 'tensor', axis=0, tiled=...  96.6 us
    reduce_scatter x1, waiting for transfers between devices, per_device(): lax.psum_scatter(jnp.dot(attended_low, w_out, preferred_element_type=jnp....  94.2 us
    all_gather x1, waiting for transfers between devices, per_device(): second_all = lax.all_gather(second_low, 'tensor', axis=0, tiled=True)  93.9 us
    reduce_scatter x1, waiting for transfers between devices, per_device(): lax.psum_scatter(contract_cols(grad_pre, w_up).astype(jnp.bfloat16), 'ten...  93.8 us
    all_gather x1, waiting for transfers between devices, per_device(): grad_all = lax.all_gather(grad_low, 'tensor', axis=0, tiled=True)  92.4 us
    all_gather x1, waiting for transfers between devices, per_device(): lax.all_gather(normed.astype(jnp.bfloat16), 'tensor', axis=0, tiled=True)  87.6 us
    reduce_scatter x1, waiting for transfers between devices, per_device(): lax.psum_scatter(contract_cols(grad_stacked, stacked_w).astype(jnp.bfloat...  58.1 us
  transfers between devices with their start and end apart: 9, of which 9 were waited for; matrix products, arithmetic and copies ran while one was open for 5% of the time, Pallas kernels for 0%

commit v1 on v0

v1 whole, which is shorter than its diff:
```python
import functools
import math

import jax
import jax.numpy as jnp
from jax import lax
from jax.experimental import pallas as pl
from jax.experimental.pallas import tpu as pltpu
from jax.sharding import PartitionSpec as P

EPSILON = 1e-06
LOG_TWO_E = 1.4426950408889634
MESH_ID = pl.DeviceIdType.MESH
CHUNKS = 4


def rms_forward(values, gain):
    inverse = lax.rsqrt(jnp.mean(values * values, axis=-1, keepdims=True) + EPSILON)
    return (values * inverse * gain, inverse)


def rms_backward(values, inverse, gain, grad_normed):
    scaled = values * inverse
    grad_scaled = grad_normed * gain
    return inverse * (
        grad_scaled - scaled * jnp.mean(grad_scaled * scaled, axis=-1, keepdims=True)
    )


def contract_rows(left, right):
    return lax.dot_general(
        left, right, (((0,), (0,)), ((), ())), preferred_element_type=jnp.float32
    )


def contract_cols(left, right):
    return lax.dot_general(
        left, right, (((1,), (1,)), ((), ())), preferred_element_type=jnp.float32
    )


def silu_slope(values):
    sigmoid_v = jax.nn.sigmoid(values)
    return sigmoid_v * (1.0 + values * (1.0 - sigmoid_v))


class Place:
    def __init__(self):
        self.d = lax.axis_index("dp")
        self.t = lax.axis_index("tensor")
        self.c = lax.rem(self.d, 2)
        self.g = self.t // 2
        self.base = self.d - self.c
        self.main = self.c == self.g
        self.pos = jnp.where(self.c == 0, self.t, 3 - self.t)

    def device(self, seq, pos):
        return (self.base + seq, jnp.where(seq == 0, pos, 3 - pos))

    def partner(self):
        return (self.base + 1 - self.c, self.t)

    def quarter(self):
        return jnp.where(self.main, self.t, lax.rem(self.t + 2, 4))


def pair_barrier(here):
    barrier = pltpu.get_barrier_semaphore()
    for step in range(1, 8):
        code = lax.rem(here.c * 4 + here.t + step, 8)
        pl.semaphore_signal(
            barrier, inc=1, device_id=(here.base + code // 4, lax.rem(code, 4)), device_id_type=MESH_ID
        )
    pl.semaphore_wait(barrier, 7)


def remote(src, dst, send, recv, device):
    return pltpu.make_async_remote_copy(
        src_ref=src, dst_ref=dst, send_sem=send, recv_sem=recv, device_id=device, device_id_type=MESH_ID
    )


def gather_kernel(own, out, send_z, send_c, recv, local_sem):
    here = Place()
    rows = own.shape[0]
    part = rows // CHUNKS
    pair_barrier(here)
    partner = here.partner()

    def place(seq, k, ch):
        block = jnp.where(seq == 0, k, 3 - k)
        return out.at[pl.ds(pl.multiple_of(block * rows + ch * part, part), part)]

    def own_part(ch):
        return own.at[pl.ds(ch * part, part)]

    def copy(src, k, ch, seq, device, send):
        return remote(src, place(seq, k, ch), send.at[k, ch], recv.at[k, ch], device)

    def arrived(k, ch, seq):
        copy(place(seq, k, ch), k, ch, seq, partner, send_z).wait_recv()

    for k in (2, 3):
        @pl.when(here.pos == k)
        def _(k=k):
            target = here.device(here.c, 1)
            for ch in range(CHUNKS):
                copy(own_part(ch), k, ch, here.c, target, send_z).start()
            for ch in range(CHUNKS):
                for kk in range(4):
                    arrived(kk, ch, 1 - here.c)
            for ch in range(CHUNKS):
                copy(own_part(ch), k, ch, here.c, target, send_z).wait_send()

    def keep(k):
        return pltpu.make_async_copy(
            own, out.at[pl.ds(pl.multiple_of(jnp.where(here.c == 0, k, 3 - k) * rows, rows), rows)], local_sem
        )

    @pl.when(here.pos == 1)
    def _():
        seq = here.c
        near = here.device(seq, 0)
        sent = []

        def send(src, k, ch, device, sem):
            copy(src, k, ch, seq, device, sem).start()
            sent.append((src, k, ch, device, sem))

        keep(1).start()
        for ch in range(CHUNKS):
            send(own_part(ch), 1, ch, near, send_z)
            send(own_part(ch), 1, ch, partner, send_c)
        for ch in range(CHUNKS):
            for k in (2, 3):
                arrived(k, ch, seq)
                send(place(seq, k, ch), k, ch, near, send_z)
                send(place(seq, k, ch), k, ch, partner, send_c)
            arrived(0, ch, seq)
            send(place(seq, 0, ch), 0, ch, partner, send_c)
        for src, k, ch, device, sem in sent:
            copy(src, k, ch, seq, device, sem).wait_send()
        keep(1).wait()

    @pl.when(here.pos == 0)
    def _():
        seq = here.c
        far = here.device(seq, 1)
        sent = []

        def send(src, k, ch, device, sem):
            copy(src, k, ch, seq, device, sem).start()
            sent.append((src, k, ch, device, sem))

        keep(0).start()
        for ch in range(CHUNKS):
            send(own_part(ch), 0, ch, far, send_z)
            send(own_part(ch), 0, ch, partner, send_c)
        for ch in range(CHUNKS):
            arrived(1, ch, seq)
            send(place(seq, 1, ch), 1, ch, partner, send_c)
        for ch in range(CHUNKS):
            for k in (2, 3):
                arrived(k, ch, seq)
                send(place(seq, k, ch), k, ch, partner, send_c)
        for src, k, ch, device, sem in sent:
            copy(src, k, ch, seq, device, sem).wait_send()
        keep(0).wait()


def gather_rows(own):
    rows, width = own.shape
    return pl.pallas_call(
        gather_kernel,
        out_shape=jax.ShapeDtypeStruct((4 * rows, width), own.dtype),
        in_specs=[pl.BlockSpec(memory_space=pl.ANY)],
        out_specs=pl.BlockSpec(memory_space=pl.ANY),
        scratch_shapes=[
            pltpu.SemaphoreType.DMA((4, CHUNKS)),
            pltpu.SemaphoreType.DMA((4, CHUNKS)),
            pltpu.SemaphoreType.DMA((4, CHUNKS)),
            pltpu.SemaphoreType.DMA,
        ],
        compiler_params=pltpu.CompilerParams(collective_id=0, has_side_effects=True),
        name="gather_rows",
    )(own)


def heads_to_rows_kernel(heads, out, send, recv, local_sem):
    here = Place()
    rows = out.shape[1]
    pair_barrier(here)
    quarter = here.quarter()
    mine = here.main

    def copy(block):
        return remote(
            heads.at[pl.ds(block * rows, rows)],
            out.at[quarter],
            send.at[block],
            recv.at[quarter],
            (here.base + here.g, block),
        )

    keep = pltpu.make_async_copy(
        heads.at[pl.ds(pl.multiple_of(here.t * rows, rows), rows)], out.at[here.t], local_sem
    )
    for block in range(4):
        @pl.when(mine & (here.t == block))
        def _():
            keep.start()

        @pl.when(jnp.logical_not(mine & (here.t == block)))
        def _(block=block):
            copy(block).start()

    for q in range(4):
        @pl.when(jnp.logical_not(mine & (here.t == q)))
        def _(q=q):
            remote(
                heads.at[pl.ds(0, rows)], out.at[q], send.at[0], recv.at[q], here.partner()
            ).wait_recv()

    for block in range(4):
        @pl.when(mine & (here.t == block))
        def _():
            keep.wait()

        @pl.when(jnp.logical_not(mine & (here.t == block)))
        def _(block=block):
            copy(block).wait_send()


def heads_to_rows(heads):
    rows, width = heads.shape[0] // 4, heads.shape[1]
    return pl.pallas_call(
        heads_to_rows_kernel,
        out_shape=jax.ShapeDtypeStruct((4, rows, width), heads.dtype),
        in_specs=[pl.BlockSpec(memory_space=pl.ANY)],
        out_specs=pl.BlockSpec(memory_space=pl.ANY),
        scratch_shapes=[
            pltpu.SemaphoreType.DMA((4,)),
            pltpu.SemaphoreType.DMA((4,)),
            pltpu.SemaphoreType.DMA,
        ],
        compiler_params=pltpu.CompilerParams(collective_id=1, has_side_effects=True),
        name="heads_to_rows",
    )(heads)


def rows_to_heads_kernel(split, out, send, recv, local_sem):
    here = Place()
    rows = split.shape[1]
    pair_barrier(here)

    def copy(q):
        native = (q // 2) == here.c
        seq = jnp.where(native, here.c, 1 - here.c)
        line = jnp.where(native, q, (q + 2) % 4)
        return remote(
            split.at[q],
            out.at[pl.ds(pl.multiple_of(here.t * rows, rows), rows)],
            send.at[q],
            recv.at[here.t],
            (here.base + seq, line),
        )

    keep = pltpu.make_async_copy(
        split.at[here.t], out.at[pl.ds(pl.multiple_of(here.t * rows, rows), rows)], local_sem
    )
    for q in range(4):
        @pl.when(here.main & (here.t == q))
        def _():
            keep.start()

        @pl.when(jnp.logical_not(here.main & (here.t == q)))
        def _(q=q):
            copy(q).start()

    for block in range(4):
        @pl.when(jnp.logical_not(here.main & (here.t == block)))
        def _(block=block):
            remote(
                split.at[0], out.at[pl.ds(block * rows, rows)], send.at[0], recv.at[block], here.partner()
            ).wait_recv()

    for q in range(4):
        @pl.when(here.main & (here.t == q))
        def _():
            keep.wait()

        @pl.when(jnp.logical_not(here.main & (here.t == q)))
        def _(q=q):
            copy(q).wait_send()


def rows_to_heads(split):
    _, rows, width = split.shape
    return pl.pallas_call(
        rows_to_heads_kernel,
        out_shape=jax.ShapeDtypeStruct((4 * rows, width), split.dtype),
        in_specs=[pl.BlockSpec(memory_space=pl.ANY)],
        out_specs=pl.BlockSpec(memory_space=pl.ANY),
        scratch_shapes=[
            pltpu.SemaphoreType.DMA((4,)),
            pltpu.SemaphoreType.DMA((4,)),
            pltpu.SemaphoreType.DMA,
        ],
        compiler_params=pltpu.CompilerParams(collective_id=2, has_side_effects=True),
        name="rows_to_heads",
    )(split)


def scatter_kernel(partial, out, from_core, from_line, outgoing, send_c, send_z, recv_c, recv_z):
    here = Place()
    rows = out.shape[0]
    part = rows // CHUNKS
    pair_barrier(here)
    partner = here.partner()
    f32 = jnp.float32

    def span(seq, k, ch):
        block = jnp.where(seq == 0, k, 3 - k)
        return pl.ds(pl.multiple_of(block * rows + ch * part, part), part)

    def piece(k, ch):
        return pl.ds(k * rows + ch * part, part)

    def line(ch):
        return pl.ds(ch * part, part)

    order = (3, 2, 1, 0)

    for k in (2, 3):
        @pl.when(here.pos == k)
        def _(k=k):
            seq = 1 - here.c
            copies = []
            for kk in order:
                for ch in range(CHUNKS):
                    cp = remote(
                        partial.at[span(seq, kk, ch)],
                        from_core.at[piece(kk, ch)],
                        send_c.at[kk, ch],
                        recv_c.at[kk, ch],
                        partner,
                    )
                    cp.start()
                    copies.append(cp)
            for ch in range(CHUNKS):
                remote(
                    outgoing.at[piece(0, ch)], out.at[line(ch)], send_z.at[0, ch], recv_z.at[k, ch], partner
                ).wait_recv()
            for cp in copies:
                cp.wait_send()

    def core_sum(k, ch):
        remote(
            partial.at[piece(k, ch)], from_core.at[piece(k, ch)], send_c.at[k, ch], recv_c.at[k, ch], partner
        ).wait_recv()
        return partial[span(here.c, k, ch)].astype(f32) + from_core[piece(k, ch)].astype(f32)

    def line_wait(k, ch):
        remote(
            outgoing.at[piece(k, ch)], from_line.at[piece(k, ch)], send_z.at[k, ch], recv_z.at[k, ch], partner
        ).wait_recv()
        return from_line[piece(k, ch)].astype(f32)

    @pl.when(here.pos == 0)
    def _():
        copies = []
        for k in (3, 2, 1):
            for ch in range(CHUNKS):
                outgoing[piece(k, ch)] = core_sum(k, ch).astype(outgoing.dtype)
                cp = remote(
                    outgoing.at[piece(k, ch)],
                    from_line.at[piece(k, ch)],
                    send_z.at[k, ch],
                    recv_z.at[k, ch],
                    here.device(here.c, 1),
                )
                cp.start()
                copies.append(cp)
        for ch in range(CHUNKS):
            total = core_sum(0, ch)
            out[line(ch)] = (total + line_wait(0, ch)).astype(out.dtype)
        for cp in copies:
            cp.wait_send()

    @pl.when(here.pos == 1)
    def _():
        copies = []
        for ch in range(CHUNKS):
            outgoing[piece(0, ch)] = core_sum(0, ch).astype(outgoing.dtype)
            cp = remote(
                outgoing.at[piece(0, ch)],
                from_line.at[piece(0, ch)],
                send_z.at[0, ch],
                recv_z.at[0, ch],
                here.device(here.c, 0),
            )
            cp.start()
            copies.append(cp)
        for k in (3, 2):
            for ch in range(CHUNKS):
                total = core_sum(k, ch)
                outgoing[piece(k, ch)] = (total + line_wait(k, ch)).astype(outgoing.dtype)
                cp = remote(
                    outgoing.at[piece(k, ch)],
                    out.at[line(ch)],
                    send_z.at[k, ch],
                    recv_z.at[k, ch],
                    here.device(here.c, k),
                )
                cp.start()
                copies.append(cp)
        for ch in range(CHUNKS):
            total = core_sum(1, ch)
            out[line(ch)] = (total + line_wait(1, ch)).astype(out.dtype)
        for cp in copies:
            cp.wait_send()


def scatter_rows(partial):
    rows, width = partial.shape[0] // 4, partial.shape[1]
    vmem = pl.BlockSpec(memory_space=pltpu.VMEM)
    return pl.pallas_call(
        scatter_kernel,
        out_shape=jax.ShapeDtypeStruct((rows, width), partial.dtype),
        in_specs=[vmem],
        out_specs=vmem,
        scratch_shapes=[
            pltpu.VMEM((4 * rows, width), partial.dtype),
            pltpu.VMEM((4 * rows, width), partial.dtype),
            pltpu.VMEM((4 * rows, width), partial.dtype),
            pltpu.SemaphoreType.DMA((4, CHUNKS)),
            pltpu.SemaphoreType.DMA((4, CHUNKS)),
            pltpu.SemaphoreType.DMA((4, CHUNKS)),
            pltpu.SemaphoreType.DMA((4, CHUNKS)),
        ],
        compiler_params=pltpu.CompilerParams(
            collective_id=3, has_side_effects=True, vmem_limit_bytes=40 * 1024 * 1024
        ),
        name="scatter_rows",
    )(partial)


def attention_forward(query_low, key_low, value_low, key_ok):
    seq_slots, heads_local, head_dim = query_low.shape
    slot_index = jnp.arange(seq_slots, dtype=jnp.int32)
    block_rows = min(512, seq_slots)
    block_count = seq_slots // block_rows

    def block_scores(block_index):
        first_row = block_index * block_rows
        last_row = first_row + block_rows
        query_pos = slot_index[first_row:last_row]
        key_pos = slot_index[:last_row]
        allowed = key_ok[None, :last_row] & (key_pos[None, :] <= query_pos[:, None]) | (
            key_pos[None, :] == query_pos[:, None]
        )
        scores = jnp.einsum(
            "qhe,khe->hqk",
            query_low[first_row:last_row],
            key_low[:last_row],
            preferred_element_type=jnp.float32,
        )
        return jnp.where(allowed[None], scores, -1e30)

    attended_parts = []
    logsum_parts = []
    for block_index in range(block_count):
        last_row = (block_index + 1) * block_rows
        scores = block_scores(block_index)
        highest = jnp.max(scores, axis=-1, keepdims=True)
        expo = jnp.exp(scores - highest)
        summed = jnp.sum(expo, axis=-1, keepdims=True)
        probs = (expo / summed).astype(jnp.bfloat16)
        attended_parts.append(
            jnp.einsum(
                "hqk,khe->qhe", probs, value_low[:last_row], preferred_element_type=jnp.float32
            )
        )
        logsum_parts.append(highest + jnp.log(summed))
    attended = jnp.concatenate(attended_parts, axis=0).reshape(seq_slots, -1)
    return attended, (block_scores, logsum_parts)


def attention_backward(query_low, key_low, value_low, attended, grad_att_low, saved):
    block_scores, logsum_parts = saved
    seq_slots, heads_local, head_dim = query_low.shape
    block_rows = min(512, seq_slots)
    block_count = seq_slots // block_rows
    row_term = jnp.sum(
        (grad_att_low.astype(jnp.float32) * attended).reshape(seq_slots, heads_local, head_dim),
        axis=-1,
    )
    grad_att_heads = grad_att_low.reshape(seq_slots, heads_local, head_dim)
    grad_query_parts = []
    grad_key_acc = jnp.zeros((seq_slots, heads_local, head_dim), jnp.float32)
    grad_value_acc = jnp.zeros((seq_slots, heads_local, head_dim), jnp.float32)
    for block_index in range(block_count):
        first_row = block_index * block_rows
        last_row = first_row + block_rows
        probs_full = jnp.exp(block_scores(block_index) - logsum_parts[block_index])
        grad_att_block = grad_att_heads[first_row:last_row]
        grad_probs = jnp.einsum(
            "qhe,khe->hqk", grad_att_block, value_low[:last_row], preferred_element_type=jnp.float32
        )
        block_term = jnp.transpose(row_term[first_row:last_row])[:, :, None]
        grad_scores = (probs_full * (grad_probs - block_term)).astype(jnp.bfloat16)
        grad_query_parts.append(
            jnp.einsum(
                "hqk,khe->qhe", grad_scores, key_low[:last_row], preferred_element_type=jnp.float32
            )
        )
        grad_key_acc = grad_key_acc.at[:last_row].add(
            jnp.einsum(
                "hqk,qhe->khe",
                grad_scores,
                query_low[first_row:last_row],
                preferred_element_type=jnp.float32,
            )
        )
        grad_value_acc = grad_value_acc.at[:last_row].add(
            jnp.einsum(
                "hqk,qhe->khe",
                probs_full.astype(jnp.bfloat16),
                grad_att_block,
                preferred_element_type=jnp.float32,
            )
        )
    return (
        jnp.concatenate(grad_query_parts, axis=0).reshape(seq_slots, -1),
        grad_key_acc.reshape(seq_slots, -1),
        grad_value_acc.reshape(seq_slots, -1),
    )


def per_device(
    inputs,
    cotangent,
    gain_attn,
    gain_mlp,
    query_scale,
    w_query,
    w_key,
    w_value,
    w_out,
    w_up,
    w_down,
    lengths,
    offsets,
):
    low = jnp.bfloat16
    f32 = jnp.float32
    here = Place()
    n_dp = lax.axis_size("dp")
    local_rows, model = inputs.shape
    seq_slots = local_rows * 4
    width_local = w_query.shape[1]
    head_dim = query_scale.shape[0]
    heads_local = width_local // head_dim
    slot_index = jnp.arange(seq_slots, dtype=jnp.int32)
    swap_core = [(i, i ^ 1) for i in range(n_dp)]
    swap_line = [(i, (i + 2) % 4) for i in range(4)]

    slice_rows = w_out.shape[0] // n_dp

    def own_slice(weight):
        return lax.dynamic_slice_in_dim(weight, here.d * slice_rows, slice_rows, 0)

    def gather_weight(weight):
        return lax.all_gather(own_slice(weight), ("tensor", "dp"), axis=0, tiled=True)

    up_slice = jnp.transpose(
        lax.dynamic_slice_in_dim(w_up, here.d * slice_rows, slice_rows, 1)
    )
    native_w = jnp.concatenate([w_query, w_key, w_value], axis=1)
    qkv_rows = model // n_dp
    foreign_slice = lax.ppermute(
        lax.dynamic_slice_in_dim(native_w, here.d * qkv_rows, qkv_rows, 0), "tensor", swap_line
    )
    foreign_w = lax.all_gather(foreign_slice, "dp", axis=0, tiled=True)
    stacked_w = jnp.where(here.main, native_w, foreign_w)
    own_span = jnp.concatenate([lengths, offsets])
    other_span = lax.ppermute(own_span, "dp", swap_core)
    group_span = jnp.where(here.main, own_span, other_span)

    key_ok = (slot_index >= group_span[1]) & (slot_index < group_span[1] + group_span[0])
    own_rows = here.t * local_rows + jnp.arange(local_rows, dtype=jnp.int32)
    row_valid = ((own_rows >= offsets[0]) & (own_rows < offsets[0] + lengths[0])).astype(f32)

    residual = inputs.astype(f32)
    normed, inverse_one = rms_forward(residual, gain_attn)
    gathered = gather_rows(normed.astype(low))
    w_out_all = gather_weight(w_out)
    w_up_all = lax.all_gather(up_slice, ("tensor", "dp"), axis=0, tiled=True)
    w_down_all = gather_weight(w_down)

    projected = jnp.dot(gathered, stacked_w, preferred_element_type=f32)
    scale_const = LOG_TWO_E / math.sqrt(head_dim)
    soft = jax.nn.softplus(query_scale)
    factor = jnp.tile(soft * scale_const, heads_local)
    shape = (seq_slots, heads_local, head_dim)
    query_low = (projected[:, :width_local] * factor).astype(low).reshape(shape)
    key_low = projected[:, width_local : 2 * width_local].astype(low).reshape(shape)
    value_low = projected[:, 2 * width_local :].astype(low).reshape(shape)
    attended, saved = attention_forward(query_low, key_low, value_low, key_ok)

    attended_rows = heads_to_rows(attended.astype(low))
    w_out_split = w_out_all.reshape(4, width_local, model)
    hidden_one = residual + jnp.einsum(
        "qre,qed->rd", attended_rows, w_out_split, preferred_element_type=f32
    )
    second, inverse_two = rms_forward(hidden_one, gain_mlp)
    second_low = second.astype(low)
    before_act = contract_cols(second_low, w_up_all)
    activated = jax.nn.silu(before_act).astype(low)
    output = hidden_one + jnp.dot(activated, w_down_all, preferred_element_type=f32)
    grad_hidden_out = cotangent.astype(f32) * row_valid[:, None]
    grad_low = grad_hidden_out.astype(low)
    grad_act = contract_cols(grad_low, w_down_all)
    grad_pre = (grad_act * silu_slope(before_act)).astype(low)
    grad_second = jnp.dot(grad_pre, w_up_all, preferred_element_type=f32)
    grad_hidden = grad_hidden_out + rms_backward(hidden_one, inverse_two, gain_mlp, grad_second)
    branch_low = grad_hidden.astype(low)
    grad_att_rows = jnp.einsum(
        "rd,qed->qre", branch_low, w_out_split, preferred_element_type=f32
    ).astype(low)
    grad_att_low = rows_to_heads(grad_att_rows)

    grad_w_down = contract_rows(activated, grad_low)
    grad_w_up_t = contract_rows(grad_pre, second_low)
    grad_w_out = jnp.einsum(
        "qre,rd->qed", attended_rows, branch_low, preferred_element_type=f32
    ).reshape(model, model)
    gain_two_part = jnp.sum(grad_w_up_t * w_up_all.astype(f32), axis=0)

    def reduce_weight(grad):
        split = jnp.transpose(grad.astype(low).reshape(4, n_dp, slice_rows, model), (1, 0, 2, 3))
        return split

    mlp_split = jnp.concatenate(
        [reduce_weight(grad_w_out), reduce_weight(grad_w_up_t), reduce_weight(grad_w_down)], axis=2
    ).reshape(n_dp * 12 * slice_rows, model)
    mlp_part = lax.psum_scatter(mlp_split, "dp", scatter_dimension=0, tiled=True)
    mlp_part = lax.psum_scatter(mlp_part, "tensor", scatter_dimension=0, tiled=True)
    mlp_all = lax.all_gather(mlp_part, "dp", axis=0, tiled=True).astype(f32)
    mlp_all = mlp_all.reshape(n_dp, 3, slice_rows, model)
    grad_out_final = mlp_all[:, 0].reshape(width_local, model)
    grad_up_final = jnp.transpose(mlp_all[:, 1].reshape(width_local, model))
    grad_down_final = mlp_all[:, 2].reshape(width_local, model)

    grad_query, grad_key, grad_value = attention_backward(
        query_low, key_low, value_low, attended, grad_att_low, saved
    )
    grad_stacked = jnp.concatenate(
        [(grad_query * factor).astype(low), grad_key.astype(low), grad_value.astype(low)], axis=1
    )
    grad_stacked_w = contract_rows(gathered, grad_stacked)
    grad_first = scatter_rows(contract_cols(grad_stacked, stacked_w).astype(low)).astype(f32)
    grad_input = grad_hidden + rms_backward(residual, inverse_one, gain_attn, grad_first)

    weighted = grad_stacked_w * stacked_w.astype(f32)
    gain_one_part = jnp.sum(weighted, axis=1)
    scale_part = jnp.sum(
        jnp.sum(weighted[:, :width_local], axis=0).reshape(heads_local, head_dim), axis=0
    )
    small = lax.psum(
        jnp.concatenate([gain_one_part, gain_two_part, scale_part]), ("dp", "tensor")
    )
    grad_gain_one = small[:model] / gain_attn
    grad_gain_two = small[model : 2 * model] / gain_mlp
    grad_scale = small[2 * model :] * jax.nn.sigmoid(query_scale) / soft

    same_core = [[i for i in range(n_dp) if i % 2 == k] for k in range(2)]
    qkv_part = lax.psum_scatter(
        grad_stacked_w.astype(low), "dp", scatter_dimension=0, tiled=True, axis_index_groups=same_core
    )
    qkv_sum = qkv_part.astype(f32) + lax.ppermute(qkv_part, "tensor", swap_line).astype(f32)
    qkv_sum = qkv_sum.astype(low)
    qkv_sum = jnp.where(here.main, qkv_sum, lax.ppermute(qkv_sum, "dp", swap_core))
    qkv_all = lax.all_gather(
        qkv_sum, "dp", axis=0, tiled=True, axis_index_groups=same_core
    ).astype(f32)
    return (
        output.astype(low),
        grad_input,
        grad_gain_one,
        grad_gain_two,
        grad_scale,
        qkv_all[:, :width_local],
        qkv_all[:, width_local : 2 * width_local],
        qkv_all[:, 2 * width_local :],
        grad_out_final,
        grad_up_final,
        grad_down_final,
    )


def solution(mesh):
    rows = P(("dp", "tensor"), None)
    cols_t = P(None, "tensor")
    rows_t = P("tensor", None)
    return jax.shard_map(
        per_device,
        mesh=mesh,
        in_specs=(
            rows, rows, P(), P(), P(), cols_t, cols_t, cols_t, rows_t, cols_t, rows_t, P("dp"), P("dp"),
        ),
        out_specs=(
            rows, rows, P(), P(), P(), cols_t, cols_t, cols_t, rows_t, cols_t, rows_t,
        ),
        check_vma=False,
    )
```

time: 1120 us -> 679 us (0.61)
  waiting for transfers between devices: 815 us -> 161 us
  Pallas kernels: 0 us -> 170 us
  local copies, waits for them, and re-layouts: 35.4 us -> 77.3 us
    all_gather x4 -> x6, waiting for transfers between devices: 371 us -> 45.2 us  [the longest x2 45.2 us: gather_weight(): lax.all_gather(own_slice(weight), ('tensor', 'dp'), axis=0, tiled=True)]
    reduce_scatter x4 -> x3, waiting for transfers between devices: 298 us -> 38.5 us  [the longest x1 38.4 us: per_device(): lax.psum_scatter(grad_stacked_w.astype(low), 'dp', scatter_dimension=0, t...]
    pallas_call x0 -> x4, Pallas kernels: none -> 170 us  [the longest x1 49.3 us: gather_rows(): pl.pallas_call(gather_kernel, out_shape=jax.ShapeDtypeStruct((4 * rows, w...]
    psum x1 -> x0, waiting for transfers between devices: 146 us -> none  [per_device(): lax.psum((grad_stacked_w[:, :width_local], grad_stacked_w[:, width_local:...]
    ppermute x0 -> x4, waiting for transfers between devices: none -> 76.1 us  [the longest x1 50 us: per_device(): lax.ppermute(qkv_part, 'tensor', swap_line).astype(f32)]
    slice x3 -> x9, local copies, waits for them, and re-layouts: 6.31 us -> 18.4 us  [the longest x5 8.11 us: attention_backward(): grad_att_block = grad_att_heads[first_row:last_row]]
    dot_general x24 -> x26, matrix products: 98.8 us -> 109 us  [the longest x4 25.3 us: attention_backward(): jnp.einsum('hqk,qhe->khe', probs_full.astype(jnp.bfloat16), grad_att_bloc...]
    dot_general x4 -> x3, matrix products: 25.7 us -> 18.7 us  [contract_cols(): lax.dot_general(left, right, (((1,), (1,)), ((), ())), preferred_element_...]
  transfers between devices with their start and end apart: 9 -> 13, of which waited for: 9 -> 5; matrix products, arithmetic and copies ran while one was open for 5% -> 35% of each run, Pallas kernels for 0% -> 25%
where the time goes in v1:
time: 679 us; the launch traced here: 672 us
  Pallas kernels  170 us (25%)
  waiting for transfers between devices  161 us (24%)
  matrix products  158 us (23%)
  local copies, waits for them, and re-layouts  77.3 us (11%)
  other arithmetic  42.6 us (6%)
  blocking collectives  41.8 us (6%)
  between operations  18.3 us (3%)
    ppermute x1, waiting for transfers between devices, per_device(): lax.ppermute(qkv_part, 'tensor', swap_line).astype(f32)  50 us
    pallas_call x1, Pallas kernels, gather_rows(): pl.pallas_call(gather_kernel, out_shape=jax.ShapeDtypeStruct((4 * rows, w...  49.3 us
    pallas_call x1, Pallas kernels, scatter_rows(): pl.pallas_call(scatter_kernel, out_shape=jax.ShapeDtypeStruct((rows, widt...  45.4 us
    all_gather x2, waiting for transfers between devices, gather_weight(): lax.all_gather(own_slice(weight), ('tensor', 'dp'), axis=0, tiled=True)  45.2 us
    psum x1, blocking collectives, per_device(): lax.psum(jnp.concatenate([gain_one_part, gain_two_part, scale_part]), ('d...  41.8 us
    reduce_scatter x1, waiting for transfers between devices, per_device(): lax.psum_scatter(grad_stacked_w.astype(low), 'dp', scatter_dimension=0, t...  38.4 us
    pallas_call x1, Pallas kernels, heads_to_rows(): pl.pallas_call(heads_to_rows_kernel, out_shape=jax.ShapeDtypeStruct((4, r...  38.2 us
    pallas_call x1, Pallas kernels, rows_to_heads(): pl.pallas_call(rows_to_heads_kernel, out_shape=jax.ShapeDtypeStruct((4 *...  37.5 us
  transfers between devices with their start and end apart: 13, of which 5 were waited for; matrix products, arithmetic and copies ran while one was open for 35% of the time, Pallas kernels for 25%

profile of v1, /device:TPU:27, one launch (start us, length us, event | category | flops | bytes accessed | tf_op | source)
XLA Modules:
  0.0 671.8 jit_solution(15566171375856178736)
XLA Ops:
  14.0 24.4 %collective-permute-done = bf16[160,960]{0,1:T(8,128)(2,1)S(1)} collective-permute-done((bf16[160,960]{0,1:T(8,128)(2,1)S(1)}, bf16[160,960]{0,1:T(8,128)(2,1)S(1)}, u32[]{:S(2)}, u32[]{:S(2)}) %collective-permute-start) | collective-permute-done | bytes 307232 | tf_op jit(solution)/shard_map/ppermute | solution.py:581
  47.1 49.3 %gather_rows.1 = bf16[2048,1280]{1,0:T(8,128)(2,1)} custom-call(bf16[512,1280]{1,0:T(8,128)(2,1)} %fusion.55.own), custom_call_target="tpu_custom_call" | custom-call | tf_op jit(solution)/shard_map/gather_rows/pallas_call | solution.py:173
  102.6 4.5 copy.116
  110.4 5.3 fusion.124
  119.9 2.8 select_reduce_fusion
  122.7 4.4 fusion
  128.6 6.7 select_reduce_fusion.1
  135.3 7.8 %fusion.2 = f32[4,512]{1,0:T(4,128)S(1)} fusion(f32[4,512,1536]{2,1,0:T(8,128)} %get-tuple-element.196, f32[4,512]{1,0:T(4,128)S(1)} %get-tuple-element.195, pred[512,1536]{1,0:T(8,128)(4,1)S(1)} %compare_or_fusion), kind=kLoop, calls=%fused_computation.11 | loop fusion | flops 9435136 | bytes 13385728 | tf_op jit(solution)/shard_map/reduce_sum | solution.py:477
  143.1 6.3 fusion.89
  162.7 5.4 fusion.90
  170.6 2.7 copy.118.heads
  173.3 38.2 %heads_to_rows.1 = bf16[4,512,320]{2,1,0:T(8,128)(2,1)} custom-call(bf16[2048,320]{1,0:T(8,128)(2,1)} %copy.118.heads), custom_call_target="tpu_custom_call" | custom-call | tf_op jit(solution)/shard_map/heads_to_rows/pallas_call | solution.py:236
  211.5 6.2 multiply_reduce_fusion.2
  217.7 4.7 fusion.112
  224.0 3.8 convolution_convert_fusion.1
  227.8 45.2 %all-gather.13.cloned.1.call-done = bf16[1280,1280]{1,0:T(8,128)(2,1)} async-done(((bf16[40,1280]{1,0:T(8,128)(2,1)}), bf16[1280,1280]{1,0:T(8,128)(2,1)}) %all-gather.13.cloned.1.call-update) | async-done | bytes 3276816 | tf_op jit(solution)/shard_map/all_gather | solution.py:574
  273.1 5.5 fusion.32
  284.3 2.6 fusion.114
  287.6 4.5 pad_maximum_fusion
  294.5 4.6 convolution_convert_fusion.3
  300.7 37.5 %rows_to_heads.1 = bf16[2048,320]{1,0:T(8,128)(2,1)} custom-call(bf16[4,512,320]{2,1,0:T(8,128)(2,1)} %bitcast.204), custom_call_target="tpu_custom_call" | custom-call | tf_op jit(solution)/shard_map/rows_to_heads/pallas_call | solution.py:299
  338.3 2.5 fusion.121
  346.4 3.9 convert_multiply_fusion.3
  352.6 4.2 fusion.84
  358.9 4.1 multiply_convert_fusion.3
  367.0 3.1 multiply_convert_fusion.2
  372.6 4.3 multiply_convert_fusion.1
  377.0 2.9 convolution_bitcast_fusion.4
  379.9 9.4 %multiply_convert_fusion = bf16[4,512,2048]{2,1,0:T(8,128)(2,1)S(1)} fusion(f32[4,512,2048]{2,1,0:T(8,128)} %copy-done.2, f32[4,512]{1,0:T(4,128)S(1)} %get-tuple-element.183, f32[4,512]{1,0:T(4,128)S(1)} %log_add_fusion, pred[512,2048]{1,0:T(8,128)(4,1)S(1)} %copy-done.6, bf16[512,4,80]{0,2,1:T(8,128)(2,1)S(1)} %bitcast.234, bf16[2048,4,80]{0,2,1:T(8,128)(2,1)} %bitcast.227), kind=kOutput, calls=%fused_computation | convolution fusion | flops 692060160 | bytes 27869184 | tf_op jit(solution)/shard_map/qhe,khe->hqk/dot_general | solution.py:507
  389.3 2.7 convolution_bitcast_fusion.7
  394.2 3.5 fusion.75
  397.8 4.2 fusion.47
  403.3 5.0 fusion.54
  408.4 4.7 fusion.79
  413.1 8.6 %fusion.39 = f32[2048,4,80]{0,2,1:T(8,128)} fusion(f32[2048,4,80]{0,2,1:T(8,128)} %fusion.79, bf16[512,4,80]{0,2,1:T(8,128)(2,1)S(1)} %bitcast.236, f32[4,512,1536]{2,1,0:T(8,128)} %get-tuple-element.196, f32[4,512]{1,0:T(4,128)S(1)} %log_add_fusion.1, pred[512,1536]{1,0:T(8,128)(4,1)S(1)} %compare_or_fusion), kind=kOutput, calls=%fused_computation.73 | convolution fusion | flops 513245184 | bytes 17637376 | tf_op jit(solution)/shard_map/hqk,qhe->khe/dot_general | solution.py:526
  421.8 7.7 %fusion.51 = bf16[2048,4,80]{0,2,1:T(8,128)(2,1)} fusion(f32[2048,4,80]{0,2,1:T(8,128)} %fusion.39, bf16[512,4,80]{0,2,1:T(8,128)(2,1)} %bitcast.233, f32[4,512,2048]{2,1,0:T(8,128)S(1)} %bitcast.186, f32[4,512]{1,0:T(4,128)S(1)} %log_add_fusion, pred[512,2048]{1,0:T(8,128)(4,1)} %copy-done.5), kind=kOutput, calls=%fused_computation.81 | convolution fusion | flops 684982272 | bytes 22093824 | tf_op jit(solution)/shard_map/hqk,qhe->khe/dot_general | solution.py:526
  429.6 11.8 %fusion.113 = (f32[1280]{0:T(1024)S(1)}, f32[1280,960]{0,1:T(8,128)}, bf16[1280,960]{0,1:T(8,128)(2,1)S(1)}) fusion(bf16[1280,960]{0,1:T(8,128)(2,1)} %copy-done.42, bf16[2048,1280]{1,0:T(8,128)(2,1)} %gather_rows.1, bf16[2048,320]{0,1:T(8,128)(2,1)} %bitcast.223, bf16[2048,320]{0,1:T(8,128)(2,1)} %bitcast.229, bf16[2048,320]{0,1:T(8,128)(2,1)} %fusion.62), kind=kOutput, calls=%fused_computation.192 | convolution fusion | flops 5049875456 | bytes 19010560 | tf_op jit(solution)/shard_map/dot_general | solution.py:31
  441.3 3.5 copy.150
  445.7 38.4 %reduce-scatter.10.cloned.1.call-done = bf16[320,960]{1,0:T(8,128)(2,1)} async-done(((bf16[1280,960]{1,0:T(8,128)(2,1)}), bf16[320,960]{1,0:T(8,128)(2,1)}) %reduce-scatter.10.cloned.1.call-update) | async-done | bytes 614416 | tf_op jit(solution)/shard_map/reduce_scatter | solution.py:678
  485.9 50.0 %collective-permute-done.2 = bf16[320,960]{1,0:T(8,128)(2,1)S(1)} collective-permute-done((bf16[320,960]{1,0:T(8,128)(2,1)}, bf16[320,960]{1,0:T(8,128)(2,1)S(1)}, u32[]{:S(2)}, u32[]{:S(2)}) %collective-permute-start.2) | collective-permute-done | bytes 614432 | tf_op jit(solution)/shard_map/ppermute | solution.py:681
  541.3 8.5 %convolution_convert_fusion.partial = bf16[2048,1280]{1,0:T(8,128)(2,1)S(1)} fusion(bf16[1280,960]{0,1:T(8,128)(2,1)} %copy-done.42, bf16[2048,320]{0,1:T(8,128)(2,1)} %bitcast.224, bf16[2048,320]{0,1:T(8,128)(2,1)} %bitcast.230, bf16[2048,320]{0,1:T(8,128)(2,1)} %fusion.62), kind=kOutput, calls=%fused_computation.24 | convolution fusion | flops 5047582720 | bytes 11632640 | tf_op jit(solution)/shard_map/dot_general | solution.py:37
  549.8 45.4 %scatter_rows.1 = bf16[512,1280]{1,0:T(8,128)(2,1)S(1)} custom-call(bf16[2048,1280]{1,0:T(8,128)(2,1)S(1)} %convolution_convert_fusion.partial), custom_call_target="tpu_custom_call" | custom-call | tf_op jit(solution)/shard_map/scatter_rows/pallas_call | solution.py:427
  597.0 41.8 %psum.7 = f32[2640]{0:T(1024)S(1)} all-reduce(f32[2640]{0:T(1024)S(1)} %pad_maximum_fusion.6), channel_id=1, replica_groups=mesh['dp'=8,'tensor'=4] {'dp','tensor'}, use_global_device_ids=true, to_apply=%region_17.18 | all-reduce | flops 2640 | bytes 21120 | tf_op jit(solution)/shard_map/psum | solution.py:670
  644.3 5.0 fusion.31
  649.3 4.3 fusion.119
  653.5 2.7 copy.140
  656.2 2.7 copy.141
  660.7 4.1 fusion.120
  (301 shorter events, 91.8 us)
Async XLA Ops:
  7.2 32.2 %copy-start = (bf16[320,1280]{1,0:T(8,128)(2,1)S(1)}, bf16[320,1280]{1,0:T(8,128)(2,1)}, u32[]{:S(2)}) copy-start(bf16[320,1280]{1,0:T(8,128)(2,1)} %param.41) | copy-start | bytes 2457604
  7.2 95.4 %all-gather.7.cloned.1.call-start = ((), (), s32[]{:S(2)}) async-start(), calls=%async_computation.3 | async-start | bytes 2949120 | tf_op jit(solution)/shard_map/all_gather | solution.py:584
  11.5 33.7 %copy-start.10 = (bf16[512,1280]{1,0:T(8,128)(2,1)S(1)}, bf16[512,1280]{1,0:T(8,128)(2,1)}, u32[]{:S(2)}) copy-start(bf16[512,1280]{1,0:T(8,128)(2,1)} %param.33) | copy-start | bytes 3932164
  12.5 33.1 %copy-start.58 = (f32[1280]{0:T(1024)S(1)}, f32[1280]{0:T(1024)}, u32[]{:S(2)}) copy-start(f32[1280]{0:T(1024)} %param.35) | copy-start | bytes 15364
  13.8 24.5 %collective-permute-start = (bf16[160,960]{0,1:T(8,128)(2,1)S(1)}, bf16[160,960]{0,1:T(8,128)(2,1)S(1)}, u32[]{:S(2)}, u32[]{:S(2)}) collective-permute-start(bf16[160,960]{0,1:T(8,128)(2,1)S(1)} %constant_dynamic-slice_fusion.2), channel_id=1, source_target_pairs={{0,2},{1,3},{2,0},{3,1},{4,6},{5,7},{6,4},{7,5},{8,10},{9,11},{10,... | collective-permute-start | bytes 921608 | tf_op jit(solution)/shard_map/ppermute | solution.py:581
  39.3 172.2 %all-gather.9.cloned.1.call-start = ((), (), s32[]{:S(2)}) async-start(), calls=%async_computation.4 | async-start | bytes 3379200 | tf_op jit(solution)/shard_map/all_gather | solution.py:574
  40.0 177.7 %all-gather.11.cloned.1.call-start = ((), (), s32[]{:S(2)}) async-start(), calls=%async_computation.5 | async-start | bytes 3379200 | tf_op jit(solution)/shard_map/all_gather | solution.py:598
  41.7 231.4 %all-gather.13.cloned.1.call-start = ((), (), s32[]{:S(2)}) async-start(), calls=%async_computation.6 | async-start | bytes 3379200 | tf_op jit(solution)/shard_map/all_gather | solution.py:574
  43.1 53.4 %collective-permute-start.1 = (s32[2]{0:T(128)S(1)}, s32[2]{0:T(128)S(1)}, u32[]{:S(2)}, u32[]{:S(2)}) collective-permute-start(s32[2]{0:T(128)S(1)} %pad_add_fusion), channel_id=1, source_target_pairs={{0,4},{4,0},{8,12},{12,8},{16,20},{20,16},{24,28},{28,24},{1,5},{5... | collective-permute-start | bytes 32 | tf_op jit(solution)/shard_map/ppermute | solution.py:587
  45.1 399.8 %reduce-scatter.6.cloned.1.call-start = ((), (), s32[]{:S(2)}) async-start(), calls=%async_computation.8 | async-start | bytes 11059200 | tf_op jit(solution)/shard_map/reduce_scatter | solution.py:647
  45.6 50.7 %copy-start.60 = (f32[512]{0:T(512)}, f32[512]{0:T(512)S(1)}, u32[]{:S(2)}) copy-start(f32[512]{0:T(512)S(1)} %add_rsqrt_fusion.1) | copy-start | bytes 6148
  47.1 49.3 %copy-start.67 = (f32[80]{0:T(128)S(1)}, f32[80]{0:T(128)}, u32[]{:S(2)}) copy-start(f32[80]{0:T(128)} %param.37) | copy-start | bytes 964
  96.5 23.0 %copy-start.62 = (f32[320]{0:T(512)}, f32[320]{0:T(512)S(1)}, u32[]{:S(2)}) copy-start(f32[320]{0:T(512)S(1)} %mul.178) | copy-start | bytes 3844
  100.7 60.7 %copy-start.5 = (pred[512,2048]{1,0:T(8,128)(4,1)}, pred[512,2048]{1,0:T(8,128)(4,1)S(1)}, u32[]{:S(2)}) copy-start(pred[512,2048]{1,0:T(8,128)(4,1)S(1)} %fusion.23) | copy-start | bytes 3145732
  101.0 57.4 %copy-start.25 = (pred[512,512]{0,1:T(8,128)(4,1)}, pred[512,512]{0,1:T(8,128)(4,1)S(1)}, u32[]{:S(2)}) copy-start(pred[512,512]{0,1:T(8,128)(4,1)S(1)} %compare_or_fusion.2) | copy-start | bytes 786436
  102.6 50.6 %copy-start.19 = (pred[512,1024]{1,0:T(8,128)(4,1)}, pred[512,1024]{1,0:T(8,128)(4,1)S(1)}, u32[]{:S(2)}) copy-start(pred[512,1024]{1,0:T(8,128)(4,1)S(1)} %compare_or_fusion.1) | copy-start | bytes 1572868
  118.4 10.2 %copy-start.17 = (bf16[1536,320]{0,1:T(8,128)(2,1)}, bf16[1536,320]{0,1:T(8,128)(2,1)S(1)}, u32[]{:S(2)}) copy-start(bf16[1536,320]{0,1:T(8,128)(2,1)S(1)} %get-tuple-element.165) | copy-start | bytes 2949124
  118.5 30.9 %copy-start.22 = (bf16[1024,320]{0,1:T(8,128)(2,1)}, bf16[1024,320]{0,1:T(8,128)(2,1)S(1)}, u32[]{:S(2)}) copy-start(bf16[1024,320]{0,1:T(8,128)(2,1)S(1)} %get-tuple-element.163) | copy-start | bytes 1966084
  118.5 34.7 %copy-start.55 = (bf16[1024,320]{0,1:T(8,128)(2,1)}, bf16[1024,320]{0,1:T(8,128)(2,1)S(1)}, u32[]{:S(2)}) copy-start(bf16[1024,320]{0,1:T(8,128)(2,1)S(1)} %get-tuple-element.164) | copy-start | bytes 1966084
  119.5 37.3 %copy-start.31 = (bf16[512,320]{0,1:T(8,128)(2,1)}, bf16[512,320]{0,1:T(8,128)(2,1)S(1)}, u32[]{:S(2)}) copy-start(bf16[512,320]{0,1:T(8,128)(2,1)S(1)} %get-tuple-element.161) | copy-start | bytes 983044
  119.8 8.8 %copy-start.35 = (bf16[512,320]{0,1:T(8,128)(2,1)}, bf16[512,320]{0,1:T(8,128)(2,1)S(1)}, u32[]{:S(2)}) copy-start(bf16[512,320]{0,1:T(8,128)(2,1)S(1)} %get-tuple-element.181) | copy-start | bytes 983044
  119.8 29.6 %copy-start.28 = (bf16[512,320]{0,1:T(8,128)(2,1)}, bf16[512,320]{0,1:T(8,128)(2,1)S(1)}, u32[]{:S(2)}) copy-start(bf16[512,320]{0,1:T(8,128)(2,1)S(1)} %get-tuple-element.182) | copy-start | bytes 983044
  119.8 36.9 %copy-start.33 = (bf16[512,320]{0,1:T(8,128)(2,1)}, bf16[512,320]{0,1:T(8,128)(2,1)S(1)}, u32[]{:S(2)}) copy-start(bf16[512,320]{0,1:T(8,128)(2,1)S(1)} %get-tuple-element.179) | copy-start | bytes 983044
  135.3 7.8 %copy-start.52 = (bf16[1536,320]{0,1:T(8,128)(2,1)S(1)}, bf16[1536,320]{0,1:T(8,128)(2,1)}, u32[]{:S(2)}) copy-start(bf16[1536,320]{0,1:T(8,128)(2,1)} %get-tuple-element.166) | copy-start | bytes 2949124
  154.4 7.0 %slice-start = ((s8[16777216]{0:T(1024)(128)(4,1)}), s8[4194304]{0:T(1024)(128)(4,1)S(1)}, s32[]{:S(2)}) async-start(s8[16777216]{0:T(1024)(128)(4,1)} %bitcast.183), calls=%async_computation.12 | async-start | bytes 8388608
  154.4 7.0 %slice-start.1 = ((s8[16777216]{0:T(1024)(128)(4,1)}), s8[4194304]{0:T(1024)(128)(4,1)S(1)}, s32[]{:S(2)}) async-start(s8[16777216]{0:T(1024)(128)(4,1)} %bitcast.183), calls=%async_computation.13 | async-start | bytes 8388608
  154.4 7.0 %slice-start.2 = ((s8[16777216]{0:T(1024)(128)(4,1)}), s8[4194304]{0:T(1024)(128)(4,1)S(1)}, s32[]{:S(2)}) async-start(s8[16777216]{0:T(1024)(128)(4,1)} %bitcast.183), calls=%async_computation.14 | async-start | bytes 8388608
  292.1 192.0 %reduce-scatter.10.cloned.1.call-start = ((), (), s32[]{:S(2)}) async-start(), calls=%async_computation.11 | async-start | bytes 3276800 | tf_op jit(solution)/shard_map/reduce_scatter | solution.py:678
  338.3 8.1 %copy-start.14 = (bf16[2048,320]{1,0:T(8,128)(2,1)S(1)}, bf16[2048,320]{1,0:T(8,128)(2,1)}, u32[]{:S(2)}) copy-start(bf16[2048,320]{1,0:T(8,128)(2,1)} %rows_to_heads.1) | copy-start | bytes 3932164
  358.9 8.1 %slice-start.11 = ((s8[8388608]{0:T(1024)(128)(4,1)}), s8[4194304]{0:T(1024)(128)(4,1)S(1)}, s32[]{:S(2)}) async-start(s8[8388608]{0:T(1024)(128)(4,1)} %bitcast.189), calls=%async_computation.23 | async-start | bytes 8388608
  358.9 8.1 %copy-start.44 = (bf16[512,320]{0,1:T(8,128)(2,1)S(1)}, bf16[512,320]{0,1:T(8,128)(2,1)}, u32[]{:S(2)}) copy-start(bf16[512,320]{0,1:T(8,128)(2,1)} %copy.126) | copy-start | bytes 983044
  358.9 8.1 %copy-start.56 = (bf16[1024,320]{0,1:T(8,128)(2,1)S(1)}, bf16[1024,320]{0,1:T(8,128)(2,1)}, u32[]{:S(2)}) copy-start(bf16[1024,320]{0,1:T(8,128)(2,1)} %copy-done.55) | copy-start | bytes 1966084
  363.8 8.7 %slice-start.8 = ((s8[12582912]{0:T(1024)(128)(4,1)}), s8[4194304]{0:T(1024)(128)(4,1)S(1)}, s32[]{:S(2)}) async-start(s8[12582912]{0:T(1024)(128)(4,1)} %bitcast.187), calls=%async_computation.20 | async-start | bytes 8388608
  379.9 9.4 %copy-start.13 = (bf16[2048,320]{0,1:T(8,128)(2,1)S(1)}, bf16[2048,320]{0,1:T(8,128)(2,1)}, u32[]{:S(2)}) copy-start(bf16[2048,320]{0,1:T(8,128)(2,1)} %copy-done.12) | copy-start | bytes 3932164
  397.8 10.6 %slice-start.13 = ((s8[8388608]{0:T(1024)(128)(4,1)}), s8[4194304]{0:T(1024)(128)(4,1)S(1)}, s32[]{:S(2)}) async-start(s8[8388608]{0:T(1024)(128)(4,1)} %bitcast.191), calls=%async_computation.25 | async-start | bytes 8388608
  403.3 18.5 %slice-start.4 = ((s8[16777216]{0:T(1024)(128)(4,1)}), s8[4194304]{0:T(1024)(128)(4,1)S(1)}, s32[]{:S(2)}) async-start(s8[16777216]{0:T(1024)(128)(4,1)} %bitcast.185), calls=%async_computation.16 | async-start | bytes 8388608
  403.3 18.5 %slice-start.5 = ((s8[16777216]{0:T(1024)(128)(4,1)}), s8[4194304]{0:T(1024)(128)(4,1)S(1)}, s32[]{:S(2)}) async-start(s8[16777216]{0:T(1024)(128)(4,1)} %bitcast.185), calls=%async_computation.17 | async-start | bytes 8388608
  408.4 13.4 %slice-start.6 = ((s8[16777216]{0:T(1024)(128)(4,1)}), s8[4194304]{0:T(1024)(128)(4,1)S(1)}, s32[]{:S(2)}) async-start(s8[16777216]{0:T(1024)(128)(4,1)} %bitcast.185), calls=%async_computation.18 | async-start | bytes 8388608
  413.1 8.7 %slice-start.7 = ((s8[16777216]{0:T(1024)(128)(4,1)}), s8[4194304]{0:T(1024)(128)(4,1)S(1)}, s32[]{:S(2)}) async-start(s8[16777216]{0:T(1024)(128)(4,1)} %bitcast.185), calls=%async_computation.19 | async-start | bytes 8388608
  444.9 95.7 %reduce-scatter.8.cloned.1.call-start = ((), (), s32[]{:S(2)}) async-start(), calls=%async_computation.9 | async-start | bytes 1536000 | tf_op jit(solution)/shard_map/reduce_scatter | solution.py:648
  445.6 203.6 %all-gather.15.cloned.1.call-start = ((), (), s32[]{:S(2)}) async-start(), calls=%async_computation.7 | async-start | bytes 3276800 | tf_op jit(solution)/shard_map/all_gather | solution.py:684
  484.1 51.7 %collective-permute-start.2 = (bf16[320,960]{1,0:T(8,128)(2,1)}, bf16[320,960]{1,0:T(8,128)(2,1)S(1)}, u32[]{:S(2)}, u32[]{:S(2)}) collective-permute-start(bf16[320,960]{1,0:T(8,128)(2,1)} %reduce-scatter.10.cloned.1.call-done), channel_id=1, source_target_pairs={{0,2},{1,3},{2,0},{3,1},{4,6},{5,7},{6,4},{7,5},{8,10},{9,11},{10,... | collective-permute-start | bytes 1843208 | tf_op jit(solution)/shard_map/ppermute | solution.py:681
  536.7 2.3 collective-permute-start.3
  540.5 120.1 %all-gather.17.cloned.1.call-start = ((), (), s32[]{:S(2)}) async-start(), calls=%async_computation.10 | async-start | bytes 2764800 | tf_op jit(solution)/shard_map/all_gather | solution.py:649
  549.8 89.0 %copy-start.11 = (bf16[512,1280]{1,0:T(8,128)(2,1)S(1)}, bf16[512,1280]{1,0:T(8,128)(2,1)}, u32[]{:S(2)}) copy-start(bf16[512,1280]{1,0:T(8,128)(2,1)} %param.33) | copy-start | bytes 3932164
  549.8 89.0 %copy-start.59 = (f32[1280]{0:T(1024)S(1)}, f32[1280]{0:T(1024)}, u32[]{:S(2)}) copy-start(f32[1280]{0:T(1024)} %param.35) | copy-start | bytes 15364
  549.8 89.0 %copy-start.61 = (f32[512]{0:T(512)S(1)}, f32[512]{0:T(512)}, u32[]{:S(2)}) copy-start(f32[512]{0:T(512)} %copy-done.60) | copy-start | bytes 6148
  595.2 44.2 %copy-start.68 = (f32[80]{0:T(128)S(1)}, f32[80]{0:T(128)}, u32[]{:S(2)}) copy-start(f32[80]{0:T(128)} %param.37) | copy-start | bytes 964
  (52 other events, 188.6 us)
Sparse Core Ops, SparseCore 0:
  39.4 31.2 all-gather.6
  73.5 58.2 all-gather.8
  134.7 67.3 all-gather.10
  204.8 68.2 all-gather.12
  292.2 77.7 reduce-scatter.5
  445.0 39.0 reduce-scatter.9
  486.4 42.6 reduce-scatter.7
  540.7 39.3 all-gather.14
  582.1 30.3 all-gather.16

commit v2 on v1

v2 whole, which is shorter than its diff:
```python
import functools
import math

import jax
import jax.numpy as jnp
from jax import lax
from jax.experimental import pallas as pl
from jax.experimental.pallas import tpu as pltpu
from jax.sharding import PartitionSpec as P

EPSILON = 1e-06
LOG_TWO_E = 1.4426950408889634
MESH_ID = pl.DeviceIdType.MESH
CHUNKS = 4


def rms_forward(values, gain):
    inverse = lax.rsqrt(jnp.mean(values * values, axis=-1, keepdims=True) + EPSILON)
    return (values * inverse * gain, inverse)


def rms_backward(values, inverse, gain, grad_normed):
    scaled = values * inverse
    grad_scaled = grad_normed * gain
    return inverse * (
        grad_scaled - scaled * jnp.mean(grad_scaled * scaled, axis=-1, keepdims=True)
    )


def contract_rows(left, right):
    return lax.dot_general(
        left, right, (((0,), (0,)), ((), ())), preferred_element_type=jnp.float32
    )


def contract_cols(left, right):
    return lax.dot_general(
        left, right, (((1,), (1,)), ((), ())), preferred_element_type=jnp.float32
    )


def silu_slope(values):
    sigmoid_v = jax.nn.sigmoid(values)
    return sigmoid_v * (1.0 + values * (1.0 - sigmoid_v))


class Place:
    def __init__(self):
        self.d = lax.axis_index("dp")
        self.t = lax.axis_index("tensor")
        self.c = lax.rem(self.d, 2)
        self.g = self.t // 2
        self.base = self.d - self.c
        self.pairs = lax.axis_size("dp") // 2
        self.pair = self.d // 2
        self.main = self.c == self.g
        self.pos = jnp.where(self.c == 0, self.t, 3 - self.t)

    def device(self, seq, pos):
        return (self.base + seq, jnp.where(seq == 0, pos, 3 - pos))

    def across(self, step):
        return (2 * lax.rem(self.pair + step, self.pairs) + self.c, self.t)

    def partner(self):
        return (self.base + 1 - self.c, self.t)

    def quarter(self):
        return jnp.where(self.main, self.t, lax.rem(self.t + 2, 4))


def pair_barrier(here, plane=False):
    barrier = pltpu.get_barrier_semaphore()
    others = []
    for step in range(1, 8):
        code = lax.rem(here.c * 4 + here.t + step, 8)
        others.append((here.base + code // 4, lax.rem(code, 4)))
    if plane:
        others += [here.across(step) for step in range(1, here.pairs)]
    for device in others:
        pl.semaphore_signal(barrier, inc=1, device_id=device, device_id_type=MESH_ID)
    pl.semaphore_wait(barrier, len(others))


def remote(src, dst, send, recv, device):
    return pltpu.make_async_remote_copy(
        src_ref=src, dst_ref=dst, send_sem=send, recv_sem=recv, device_id=device, device_id_type=MESH_ID
    )


def gather_kernel(
    own, native, out, foreign, send_z, send_c, recv, local_sem, send_w, spread_w, recv_w
):
    here = Place()
    rows = own.shape[0]
    part = rows // CHUNKS
    pair_barrier(here, plane=True)
    partner = here.partner()
    members = native.shape[0]
    line = lax.rem(here.t + 2, 4)
    weight_copy = remote(
        native.at[here.d],
        foreign.at[here.d],
        send_w,
        recv_w.at[here.d],
        (here.base + 1 - line // 2, line),
    )
    weight_copy.start()

    def weight_arrived(member):
        remote(native.at[0], foreign.at[member], send_w, recv_w.at[member], partner).wait_recv()

    def spread(core, step):
        member = here.base + core
        return remote(
            foreign.at[member],
            foreign.at[member],
            spread_w.at[core, step],
            recv_w.at[member],
            here.across(step),
        )

    def place(seq, k, ch):
        block = jnp.where(seq == 0, k, 3 - k)
        return out.at[pl.ds(pl.multiple_of(block * rows + ch * part, part), part)]

    def own_part(ch):
        return own.at[pl.ds(ch * part, part)]

    def copy(src, k, ch, seq, device, send):
        return remote(src, place(seq, k, ch), send.at[k, ch], recv.at[k, ch], device)

    def arrived(k, ch, seq):
        copy(place(seq, k, ch), k, ch, seq, partner, send_z).wait_recv()

    for k in (2, 3):
        @pl.when(here.pos == k)
        def _(k=k):
            target = here.device(here.c, 1)
            for ch in range(CHUNKS):
                copy(own_part(ch), k, ch, here.c, target, send_z).start()
            for core in range(2):
                weight_arrived(here.base + core)
                for step in range(1, here.pairs):
                    spread(core, step).start()
            for step in range(1, here.pairs):
                for core in range(2):
                    weight_arrived(2 * lax.rem(here.pair + step, here.pairs) + core)
            for ch in range(CHUNKS):
                for kk in range(4):
                    arrived(kk, ch, 1 - here.c)
            for ch in range(CHUNKS):
                copy(own_part(ch), k, ch, here.c, target, send_z).wait_send()
            for core in range(2):
                for step in range(1, here.pairs):
                    spread(core, step).wait_send()

    def keep(k):
        return pltpu.make_async_copy(
            own, out.at[pl.ds(pl.multiple_of(jnp.where(here.c == 0, k, 3 - k) * rows, rows), rows)], local_sem
        )

    @pl.when(here.pos == 1)
    def _():
        seq = here.c
        near = here.device(seq, 0)
        sent = []

        def send(src, k, ch, device, sem):
            copy(src, k, ch, seq, device, sem).start()
            sent.append((src, k, ch, device, sem))

        keep(1).start()
        for ch in range(CHUNKS):
            send(own_part(ch), 1, ch, near, send_z)
            send(own_part(ch), 1, ch, partner, send_c)
        for ch in range(CHUNKS):
            for k in (2, 3):
                arrived(k, ch, seq)
                send(place(seq, k, ch), k, ch, near, send_z)
                send(place(seq, k, ch), k, ch, partner, send_c)
            arrived(0, ch, seq)
            send(place(seq, 0, ch), 0, ch, partner, send_c)
        for src, k, ch, device, sem in sent:
            copy(src, k, ch, seq, device, sem).wait_send()
        keep(1).wait()

    @pl.when(here.pos == 0)
    def _():
        seq = here.c
        far = here.device(seq, 1)
        sent = []

        def send(src, k, ch, device, sem):
            copy(src, k, ch, seq, device, sem).start()
            sent.append((src, k, ch, device, sem))

        keep(0).start()
        for ch in range(CHUNKS):
            send(own_part(ch), 0, ch, far, send_z)
            send(own_part(ch), 0, ch, partner, send_c)
        for ch in range(CHUNKS):
            arrived(1, ch, seq)
            send(place(seq, 1, ch), 1, ch, partner, send_c)
        for ch in range(CHUNKS):
            for k in (2, 3):
                arrived(k, ch, seq)
                send(place(seq, k, ch), k, ch, partner, send_c)
        for src, k, ch, device, sem in sent:
            copy(src, k, ch, seq, device, sem).wait_send()
        keep(0).wait()

    weight_copy.wait_send()


def gather_rows(own, native):
    rows, width = own.shape
    members = native.shape[0]
    hbm = pl.BlockSpec(memory_space=pl.ANY)
    return pl.pallas_call(
        gather_kernel,
        out_shape=(
            jax.ShapeDtypeStruct((4 * rows, width), own.dtype),
            jax.ShapeDtypeStruct(native.shape, native.dtype),
        ),
        in_specs=[hbm, hbm],
        out_specs=(hbm, hbm),
        scratch_shapes=[
            pltpu.SemaphoreType.DMA((4, CHUNKS)),
            pltpu.SemaphoreType.DMA((4, CHUNKS)),
            pltpu.SemaphoreType.DMA((4, CHUNKS)),
            pltpu.SemaphoreType.DMA,
            pltpu.SemaphoreType.DMA,
            pltpu.SemaphoreType.DMA((2, members // 2)),
            pltpu.SemaphoreType.DMA((members,)),
        ],
        compiler_params=pltpu.CompilerParams(collective_id=0, has_side_effects=True),
        name="gather_rows",
    )(own, native)


def dg(left, right, left_dim, right_dim):
    return lax.dot_general(
        left, right, (((left_dim,), (right_dim,)), ((), ())), preferred_element_type=jnp.float32
    )


TILE = 512
MASKED = -1e30


def readable(span, first_key, first_query):
    shape = (TILE, TILE)
    key = first_key + lax.broadcasted_iota(jnp.int32, shape, 0)
    query = first_query + lax.broadcasted_iota(jnp.int32, shape, 1)
    valid = (key >= span[1]) & (key < span[1] + span[0])
    return (valid & (key <= query)) | (key == query)


def key_bias(span, first_key):
    key = first_key + lax.broadcasted_iota(jnp.int32, (TILE, 1), 0)
    return jnp.where((key >= span[1]) & (key < span[1] + span[0]), 0.0, MASKED)


def forward_kernel(span, qkv, out, logsum, rows_out, highest, summed, total, send, recv, local_sem):
    heads = logsum.shape[0]
    width, slots = out.shape
    dim = width // heads
    here = Place()
    pair_barrier(here)
    quarter = here.quarter()

    def into(q):
        return rows_out.at[pl.ds(pl.multiple_of(q * width, width), width)]

    def columns(i):
        return out.at[:, pl.ds(pl.multiple_of(i * TILE, TILE), TILE)]

    def copy(i):
        return remote(columns(i), into(quarter), send.at[i], recv.at[quarter], (here.base + here.g, i))

    keep = pltpu.make_async_copy(columns(here.t), into(here.t), local_sem)

    @pl.loop(0, slots // TILE)
    def _(s):
        i = slots // TILE - 1 - s
        qs = pl.ds(pl.multiple_of(i * TILE, TILE), TILE)
        highest[...] = jnp.full_like(highest, MASKED)
        summed[...] = jnp.zeros_like(summed)
        total[...] = jnp.zeros_like(total)

        def tile(j, diagonal):
            ks = pl.ds(pl.multiple_of(j * TILE, TILE), TILE)
            if diagonal:
                allowed = readable(span, j * TILE, i * TILE)
            else:
                bias = key_bias(span, j * TILE)
            for h in range(heads):
                hs = pl.ds(h * dim, dim)
                scores = dg(qkv[pl.ds(width + h * dim, dim), ks], qkv[hs, qs], 0, 0)
                scores = jnp.where(allowed, scores, MASKED) if diagonal else scores + bias
                before = highest[h : h + 1]
                after = jnp.maximum(before, jnp.max(scores, axis=0, keepdims=True))
                expo = jnp.exp(scores - after)
                scale = jnp.exp(before - after)
                summed[h : h + 1] = summed[h : h + 1] * scale + jnp.sum(expo, axis=0, keepdims=True)
                highest[h : h + 1] = after
                total[hs] = total[hs] * scale + dg(
                    qkv[pl.ds(2 * width + h * dim, dim), ks], expo.astype(qkv.dtype), 1, 0
                )

        @pl.loop(0, i)
        def _(j):
            tile(j, False)

        tile(i, True)
        for h in range(heads):
            hs = pl.ds(h * dim, dim)
            out[hs, qs] = (total[hs] / summed[h : h + 1]).astype(out.dtype)
            logsum[h : h + 1, qs] = highest[h : h + 1] + jnp.log(summed[h : h + 1])
        stays = here.main & (here.t == i)

        @pl.when(stays)
        def _():
            keep.start()

        @pl.when(jnp.logical_not(stays))
        def _():
            copy(i).start()

    for block in range(4):
        stays = here.main & (here.t == block)

        @pl.when(stays)
        def _():
            keep.wait()

        @pl.when(jnp.logical_not(stays))
        def _(block=block):
            copy(block).wait_send()
            remote(columns(0), into(block), send.at[0], recv.at[block], here.partner()).wait_recv()


def attention_forward(span, qkv, heads):
    width, slots = qkv.shape[0] // 3, qkv.shape[1]
    vmem = pl.BlockSpec(memory_space=pltpu.VMEM)
    return pl.pallas_call(
        forward_kernel,
        out_shape=(
            jax.ShapeDtypeStruct((width, slots), qkv.dtype),
            jax.ShapeDtypeStruct((heads, slots), jnp.float32),
            jax.ShapeDtypeStruct((4 * width, slots // 4), qkv.dtype),
        ),
        in_specs=[pl.BlockSpec(memory_space=pltpu.SMEM), vmem],
        out_specs=(vmem, vmem, pl.BlockSpec(memory_space=pl.ANY)),
        scratch_shapes=[
            pltpu.VMEM((heads, TILE), jnp.float32),
            pltpu.VMEM((heads, TILE), jnp.float32),
            pltpu.VMEM((width, TILE), jnp.float32),
            pltpu.SemaphoreType.DMA((4,)),
            pltpu.SemaphoreType.DMA((4,)),
            pltpu.SemaphoreType.DMA,
        ],
        compiler_params=pltpu.CompilerParams(
            collective_id=1, has_side_effects=True, vmem_limit_bytes=50 * 1024 * 1024
        ),
        name="attention_forward",
    )(span, qkv)


def backward_kernel(
    span, qkv, out, logsum, factor, weights, split, grad_out, grad_up, grad_down,
    result, rows_grad, plane_sum,
    grad, query_sum, key_sum, value_sum, term,
    partial, from_core, from_line, keep_in, chip_sum, plane_in,
    split_sent, split_got, local_sem, keep_sem,
    give_sent, give_got, plane_sent, plane_got,
    send_c, send_z, recv_c, recv_z,
):
    heads = logsum.shape[0]
    width, slots = out.shape
    dim = width // heads
    low, f32 = qkv.dtype, jnp.float32
    here = Place()
    pairs = here.pairs
    rows = split.shape[1]
    part = rows // CHUNKS
    partner = here.partner()
    pair_barrier(here, plane=True)
    blocks = slots // TILE

    def of(q):
        return split.at[pl.ds(pl.multiple_of(q * width, width), width)]

    def into(block):
        return grad.at[:, pl.ds(pl.multiple_of(block * rows, rows), rows)]

    def split_copy(q):
        native = (q // 2) == here.c
        seq = jnp.where(native, here.c, 1 - here.c)
        line = jnp.where(native, q, (q + 2) % 4)
        return remote(of(q), into(here.t), split_sent.at[q], split_got.at[here.t], (here.base + seq, line))

    keep = pltpu.make_async_copy(of(here.t), into(here.t), local_sem)
    for q in range(4):
        stays = here.main & (here.t == q)

        @pl.when(stays)
        def _():
            keep.start()

        @pl.when(jnp.logical_not(stays))
        def _(q=q):
            split_copy(q).start()

    sources = (grad_out, grad_up, grad_down)
    columns = chip_sum.shape[-1]

    def half(core):
        return pl.ds(pl.multiple_of(core * columns, columns), columns)

    def give(w):
        return remote(
            sources[w].at[:, :, :, half(1 - here.c)], chip_sum.at[w], give_sent.at[w], give_got.at[w], partner
        )

    def own_half(w, q):
        slot = (4 * w + q) % 2
        return pltpu.make_async_copy(
            sources[w].at[q, :, :, half(here.c)], keep_in.at[slot], keep_sem.at[slot]
        )

    def plane_copy(w, step):
        return remote(
            chip_sum.at[w, :, lax.rem(here.pair + step, pairs)],
            plane_in.at[step - 1, w],
            plane_sent.at[w, step - 1],
            plane_got.at[w, step - 1],
            here.across(step),
        )

    for w in range(3):
        give(w).start()
    own_half(0, 0).start()
    query_sum[...] = jnp.zeros_like(query_sum)
    key_sum[...] = jnp.zeros_like(key_sum)
    value_sum[...] = jnp.zeros_like(value_sum)
    for w in range(3):
        give(w).wait_recv()
        for q in range(4):
            own_half(w, q).wait()
            if q < 3:
                own_half(w, q + 1).start()
            elif w < 2:
                own_half(w + 1, 0).start()

            @pl.loop(0, pairs)
            def _(p, w=w, q=q):
                chip_sum[w, q, p] = (chip_sum[w, q, p].astype(f32) + keep_in[q % 2, p].astype(f32)).astype(low)

        for step in range(1, pairs):
            plane_copy(w, step).start()

    for block in range(4):
        stays = here.main & (here.t == block)

        @pl.when(stays)
        def _():
            keep.wait()

        @pl.when(jnp.logical_not(stays))
        def _(block=block):
            remote(of(0), into(block), split_sent.at[0], split_got.at[block], partner).wait_recv()

    for h in range(heads):
        hs = pl.ds(h * dim, dim)
        term[h : h + 1] = jnp.sum(grad[hs].astype(f32) * out[hs].astype(f32), axis=0, keepdims=True)

    def span_of(seq, k, ch):
        block = jnp.where(seq == 0, k, 3 - k)
        return pl.ds(pl.multiple_of(block * rows + ch * part, part), part)

    def piece(k, ch):
        return pl.ds(pl.multiple_of(k * rows + ch * part, part), part)

    def line_rows(ch):
        return pl.ds(ch * part, part)

    def core_copy(k, ch):
        at = span_of(here.g, k, ch)
        return remote(partial.at[at], from_core.at[piece(k, ch)], send_c.at[k, ch], recv_c.at[k, ch], partner)

    def line_copy(k, ch):
        at = span_of(here.g, k, ch)
        return remote(
            partial.at[at],
            from_line.at[piece((k % 3 if isinstance(k, int) else lax.rem(k, 3)), ch)],
            send_z.at[k, ch],
            recv_z.at[k, ch],
            here.device(here.c, jnp.where(here.pos == 0, 1, 0)),
        )

    def home_copy(k, ch):
        at = span_of(here.g, k, ch)
        return remote(
            partial.at[at], rows_grad.at[line_rows(ch)], send_z.at[k, ch], recv_z.at[k, ch], here.device(here.c, k)
        )

    def core_sum(k, ch):
        core_copy(k, ch).wait_recv()
        return partial[span_of(here.g, k, ch)].astype(f32) + from_core[piece(k, ch)].astype(f32)

    def with_line(k, ch):
        line_copy(k, ch).wait_recv()
        return core_sum(k, ch) + from_line[piece((k % 3 if isinstance(k, int) else lax.rem(k, 3)), ch)].astype(f32)

    def pass_on(k):
        for ch in range(CHUNKS):
            partial[span_of(here.g, k, ch)] = core_sum(k, ch).astype(low)
            line_copy(k, ch).start()

    def send_home(k):
        for ch in range(CHUNKS):
            partial[span_of(here.g, k, ch)] = with_line(k, ch).astype(low)
            home_copy(k, ch).start()

    @pl.loop(0, blocks)
    def _(s):
        b = jnp.where(here.g == 0, blocks - 1 - s, s)

        def tile(i, j, diagonal):
            qs = pl.ds(pl.multiple_of(i * TILE, TILE), TILE)
            ks = pl.ds(pl.multiple_of(j * TILE, TILE), TILE)
            if diagonal:
                allowed = readable(span, j * TILE, i * TILE)
            else:
                bias = key_bias(span, j * TILE)
            for h in range(heads):
                hs = pl.ds(h * dim, dim)
                ke = pl.ds(width + h * dim, dim)
                va = pl.ds(2 * width + h * dim, dim)
                scores = dg(qkv[ke, ks], qkv[hs, qs], 0, 0)
                scores = jnp.where(allowed, scores, MASKED) if diagonal else scores + bias
                probs = jnp.exp(scores - logsum[h : h + 1, qs])
                grad_probs = dg(qkv[va, ks], grad[hs, qs], 0, 0)
                grad_scores = (probs * (grad_probs - term[h : h + 1, qs])).astype(low)
                value_sum[hs, ks] += dg(grad[hs, qs], probs.astype(low), 1, 1)
                key_sum[hs, ks] += dg(qkv[hs, qs], grad_scores, 1, 1)
                query_sum[hs, qs] += dg(qkv[ke, ks], grad_scores, 1, 0)

        @pl.loop(0, blocks - 1 - s)
        def _(n):
            tile(jnp.where(here.g == 0, b, b + 1 + n), jnp.where(here.g == 0, n, b), False)

        tile(b, b, True)
        bs = pl.ds(pl.multiple_of(b * TILE, TILE), TILE)
        result[pl.ds(0, width), bs] = (query_sum[:, bs] * factor[...]).astype(low)
        result[pl.ds(width, width), bs] = key_sum[:, bs].astype(low)
        result[pl.ds(2 * width, width), bs] = value_sum[:, bs].astype(low)
        k = blocks - 1 - s
        partial[bs] = dg(result[:, bs], weights[...], 0, 1).astype(low)

        @pl.when(jnp.logical_not(here.main))
        def _():
            for ch in range(CHUNKS):
                core_copy(k, ch).start()

        @pl.when((here.pos == 0) & (s >= 1))
        def _():
            pass_on(k + 1)

        @pl.when((here.pos == 1) & (s >= 2))
        def _():
            send_home(k + 2)

    for w in range(3):
        for step in range(1, pairs):
            plane_copy(w, step).wait_recv()

        @pl.loop(0, 4)
        def _(q, w=w):
            total = chip_sum[w, q, here.pair].astype(f32)
            for step in range(1, pairs):
                total += plane_in[step - 1, w, q].astype(f32)
            plane_sum[q, w] = total.astype(low)

    @pl.when(here.pos == 0)
    def _():
        for ch in range(CHUNKS):
            rows_grad[line_rows(ch)] = with_line(0, ch).astype(low)
        for k in (1, 2, 3):
            for ch in range(CHUNKS):
                line_copy(k, ch).wait_send()

    @pl.when(here.pos == 1)
    def _():
        pass_on(0)
        for ch in range(CHUNKS):
            rows_grad[line_rows(ch)] = with_line(1, ch).astype(low)
        for ch in range(CHUNKS):
            line_copy(0, ch).wait_send()
            for k in (2, 3):
                home_copy(k, ch).wait_send()

    for k in (2, 3):
        @pl.when(here.pos == k)
        def _(k=k):
            for ch in range(CHUNKS):
                remote(
                    partial.at[piece(0, ch)], rows_grad.at[line_rows(ch)], send_z.at[0, ch], recv_z.at[k, ch], partner
                ).wait_recv()

    @pl.when(jnp.logical_not(here.main))
    def _():
        for k in range(4):
            for ch in range(CHUNKS):
                core_copy(k, ch).wait_send()

    for q in range(4):
        @pl.when(jnp.logical_not(here.main & (here.t == q)))
        def _(q=q):
            split_copy(q).wait_send()

    for w in range(3):
        give(w).wait_send()
        for step in range(1, pairs):
            plane_copy(w, step).wait_send()


def attention_backward(span, qkv, out, logsum, factor, weights, split, grad_out, grad_up, grad_down):
    width, slots = out.shape
    heads = logsum.shape[0]
    rows, model = split.shape[1], weights.shape[0]
    low, f32 = qkv.dtype, jnp.float32
    pairs, slice_rows = grad_out.shape[1], grad_out.shape[2]
    columns = model // 2
    vmem = pl.BlockSpec(memory_space=pltpu.VMEM)
    hbm = pl.BlockSpec(memory_space=pl.ANY)
    dma = pltpu.SemaphoreType.DMA
    return pl.pallas_call(
        backward_kernel,
        out_shape=(
            jax.ShapeDtypeStruct(qkv.shape, low),
            jax.ShapeDtypeStruct((rows, model), low),
            jax.ShapeDtypeStruct((4, 3, slice_rows, columns), low),
        ),
        in_specs=[pl.BlockSpec(memory_space=pltpu.SMEM)] + [vmem] * 5 + [hbm] * 4,
        out_specs=(vmem,) * 3,
        scratch_shapes=[
            pltpu.VMEM((width, slots), low),
            pltpu.VMEM((width, slots), f32),
            pltpu.VMEM((width, slots), f32),
            pltpu.VMEM((width, slots), f32),
            pltpu.VMEM((heads, slots), f32),
            pltpu.VMEM((slots, model), low),
            pltpu.VMEM((slots, model), low),
            pltpu.VMEM((3 * rows, model), low),
            pltpu.VMEM((2, pairs, slice_rows, columns), low),
            pltpu.VMEM((3, 4, pairs, slice_rows, columns), low),
            pltpu.VMEM((pairs - 1, 3, 4, slice_rows, columns), low),
            dma((4,)),
            dma((4,)),
            dma,
            dma((2,)),
            dma((3,)),
            dma((3,)),
            dma((3, pairs - 1)),
            dma((3, pairs - 1)),
            dma((4, CHUNKS)),
            dma((4, CHUNKS)),
            dma((4, CHUNKS)),
            dma((4, CHUNKS)),
        ],
        compiler_params=pltpu.CompilerParams(
            collective_id=2, has_side_effects=True, vmem_limit_bytes=60 * 1024 * 1024
        ),
        name="attention_backward",
    )(span, qkv, out, logsum, factor, weights, split, grad_out, grad_up, grad_down)


def weights_kernel(
    mlp, qkv, small, mlp_all, qkv_all, small_all, mlp_in, qkv_in, qkv_swap, small_pair, small_plane, small_line,
    mlp_sent, mlp_got, mlp_spread, mlp_share, mlp_have,
    qkv_sent, qkv_got, qkv_cross, qkv_crossed, qkv_spread, qkv_share, qkv_have,
    small_sent, small_got, plane_sent, plane_got, line_sent, line_got,
):
    here = Place()
    pairs = here.pairs
    pair_barrier(here, plane=True)
    partner = here.partner()
    f32 = jnp.float32

    def mlp_send(step):
        line = lax.rem(here.t + step, 4)
        return remote(
            mlp.at[line], mlp_in.at[step - 1], mlp_sent.at[step - 1], mlp_got.at[step - 1], (here.d, line)
        )

    def qkv_send(step):
        return remote(
            qkv.at[lax.rem(here.pair + step, pairs)],
            qkv_in.at[step - 1],
            qkv_sent.at[step - 1],
            qkv_got.at[step - 1],
            here.across(step),
        )

    small_copy = remote(small, small_pair, small_sent, small_got, partner)
    small_copy.start()
    for step in range(1, pairs):
        qkv_send(step).start()
    for step in range(1, 4):
        mlp_send(step).start()
    small_copy.wait_recv()
    small_plane[here.pair] = small[...] + small_pair[...]

    def small_across(step):
        return remote(
            small_plane.at[here.pair], small_plane.at[here.pair], plane_sent.at[step], plane_got.at[here.pair],
            here.across(step),
        )

    def small_along(step):
        return remote(
            small_line.at[here.t], small_line.at[here.t], line_sent.at[step], line_got.at[here.t],
            (here.d, lax.rem(here.t + step, 4)),
        )

    for step in range(1, pairs):
        small_across(step).start()
    for step in range(1, pairs):
        pair = lax.rem(here.pair + step, pairs)
        remote(
            small_plane.at[pair], small_plane.at[pair], plane_sent.at[0], plane_got.at[pair], partner
        ).wait_recv()
    plane_total = small_plane[0]
    for pair in range(1, pairs):
        plane_total += small_plane[pair]
    small_line[here.t] = plane_total
    for step in range(1, 4):
        small_along(step).start()

    for step in range(1, pairs):
        qkv_send(step).wait_recv()
    total = qkv[here.pair].astype(f32)
    for step in range(1, pairs):
        total += qkv_in[step - 1].astype(f32)
    qkv_swap[0] = total.astype(qkv_swap.dtype)
    line = lax.rem(here.t + 2, 4)
    cross = remote(
        qkv_swap.at[0], qkv_swap.at[1], qkv_cross, qkv_crossed, (here.base + line // 2, line)
    )

    def qkv_piece(step):
        return qkv_all.at[lax.rem(here.pair + step, pairs)]

    def qkv_out(step):
        return remote(
            qkv_all.at[here.pair], qkv_all.at[here.pair], qkv_spread.at[step], qkv_have.at[here.pair],
            here.across(step),
        )

    def qkv_core(step):
        piece = lax.rem(here.pair + step, pairs)
        return remote(
            qkv_all.at[piece], qkv_all.at[piece], qkv_share.at[step], qkv_have.at[piece], partner
        )

    @pl.when(jnp.logical_not(here.main))
    def _():
        cross.start()

    for step in range(1, 4):
        mlp_send(step).wait_recv()
    mlp_total = mlp[here.t].astype(f32)
    for step in range(1, 4):
        mlp_total += mlp_in[step - 1].astype(f32)
    mlp_all[here.d] = mlp_total.astype(mlp_all.dtype)

    def mlp_out(step):
        return remote(
            mlp_all.at[here.d], mlp_all.at[here.d], mlp_spread.at[step], mlp_have.at[here.d],
            here.across(step),
        )

    def mlp_core(step):
        member = 2 * lax.rem(here.pair + step, pairs) + here.c
        return remote(
            mlp_all.at[member], mlp_all.at[member], mlp_share.at[step], mlp_have.at[member], partner
        )

    def mlp_arrived(member):
        remote(
            mlp_all.at[member], mlp_all.at[member], mlp_share.at[0], mlp_have.at[member], partner
        ).wait_recv()

    for step in range(1, pairs):
        mlp_out(step).start()
    mlp_core(0).start()

    @pl.when(here.main)
    def _():
        cross.wait_recv()
        whole = qkv_swap[0].astype(f32) + qkv_swap[1].astype(f32)
        qkv_all[here.pair] = whole.astype(qkv_all.dtype)
        for step in range(1, pairs):
            qkv_out(step).start()
        qkv_core(0).start()

    for step in range(1, pairs):
        mlp_arrived(2 * lax.rem(here.pair + step, pairs) + here.c)
        mlp_core(step).start()

    @pl.when(here.main)
    def _():
        for step in range(1, pairs):
            qkv_core(step).wait_recv()
            qkv_core(step).start()
        for step in range(1, pairs):
            qkv_out(step).wait_send()
        for step in range(pairs):
            qkv_core(step).wait_send()

    @pl.when(jnp.logical_not(here.main))
    def _():
        for step in range(pairs):
            qkv_core(step).wait_recv()
        cross.wait_send()

    for step in range(pairs):
        mlp_arrived(2 * lax.rem(here.pair + step, pairs) + 1 - here.c)
    for step in range(1, 4):
        mlp_send(step).wait_send()
    for step in range(1, pairs):
        qkv_send(step).wait_send()
        mlp_out(step).wait_send()
    for step in range(pairs):
        mlp_core(step).wait_send()
    for step in range(1, 4):
        line = lax.rem(here.t + step, 4)
        remote(small_line.at[line], small_line.at[line], line_sent.at[0], line_got.at[line], partner).wait_recv()
    small_all[...] = (small_line[0] + small_line[1]) + (small_line[2] + small_line[3])
    small_copy.wait_send()
    for step in range(1, pairs):
        small_across(step).wait_send()
    for step in range(1, 4):
        small_along(step).wait_send()


def weight_sums(mlp, qkv, small):
    vmem = pl.BlockSpec(memory_space=pltpu.VMEM)
    low = mlp.dtype
    pairs = qkv.shape[0]
    dma = pltpu.SemaphoreType.DMA
    return pl.pallas_call(
        weights_kernel,
        out_shape=(
            jax.ShapeDtypeStruct((2 * pairs,) + mlp.shape[1:], low),
            jax.ShapeDtypeStruct(qkv.shape, low),
            jax.ShapeDtypeStruct(small.shape, small.dtype),
        ),
        in_specs=[vmem] * 3,
        out_specs=(vmem,) * 3,
        scratch_shapes=[
            pltpu.VMEM((3,) + mlp.shape[1:], low),
            pltpu.VMEM((pairs - 1,) + qkv.shape[1:], low),
            pltpu.VMEM((2,) + qkv.shape[1:], low),
            pltpu.VMEM(small.shape, small.dtype),
            pltpu.VMEM((pairs,) + small.shape, small.dtype),
            pltpu.VMEM((4,) + small.shape, small.dtype),
            dma((3,)),
            dma((3,)),
            dma((pairs,)),
            dma((pairs,)),
            dma((2 * pairs,)),
            dma((pairs - 1,)),
            dma((pairs - 1,)),
            dma,
            dma,
            dma((pairs,)),
            dma((pairs,)),
            dma((pairs,)),
            dma,
            dma,
            dma((pairs,)),
            dma((pairs,)),
            dma((4,)),
            dma((4,)),
        ],
        compiler_params=pltpu.CompilerParams(
            collective_id=3, has_side_effects=True, vmem_limit_bytes=56 * 1024 * 1024
        ),
        name="weight_sums",
    )(mlp, qkv, small)


def per_device(
    inputs,
    cotangent,
    gain_attn,
    gain_mlp,
    query_scale,
    w_query,
    w_key,
    w_value,
    w_out,
    w_up,
    w_down,
    lengths,
    offsets,
):
    low = jnp.bfloat16
    f32 = jnp.float32
    here = Place()
    n_dp = lax.axis_size("dp")
    local_rows, model = inputs.shape
    seq_slots = local_rows * 4
    width_local = w_query.shape[1]
    head_dim = query_scale.shape[0]
    heads_local = width_local // head_dim
    pairs = n_dp // 2
    swap_core = [(i, i ^ 1) for i in range(n_dp)]

    slice_rows = w_out.shape[0] // n_dp
    own_slice = jnp.stack(
        [
            lax.dynamic_slice_in_dim(w_out, here.d * slice_rows, slice_rows, 0),
            jnp.transpose(lax.dynamic_slice_in_dim(w_up, here.d * slice_rows, slice_rows, 1)),
            lax.dynamic_slice_in_dim(w_down, here.d * slice_rows, slice_rows, 0),
        ]
    )
    line_w = lax.all_gather(own_slice, "tensor", axis=0, tiled=False)
    mlp_w = lax.all_gather(line_w, "dp", axis=0, tiled=False)

    def whole_weight(w):
        return jnp.transpose(mlp_w[:, :, w], (1, 0, 2, 3)).reshape(model, model)

    w_out_all, w_up_all, w_down_all = whole_weight(0), whole_weight(1), whole_weight(2)

    own_span = jnp.concatenate([lengths, offsets])
    other_span = lax.ppermute(own_span, "dp", swap_core)
    group_span = jnp.where(here.main, own_span, other_span)
    own_rows = here.t * local_rows + jnp.arange(local_rows, dtype=jnp.int32)
    row_valid = ((own_rows >= offsets[0]) & (own_rows < offsets[0] + lengths[0])).astype(f32)

    residual = inputs.astype(f32)
    normed, inverse_one = rms_forward(residual, gain_attn)
    native_w = jnp.concatenate([w_query, w_key, w_value], axis=1)
    gathered, foreign_w = gather_rows(
        normed.astype(low), native_w.reshape(n_dp, model // n_dp, 3 * width_local)
    )
    stacked_w = jnp.where(here.main, native_w, foreign_w.reshape(model, 3 * width_local))

    scale_const = LOG_TWO_E / math.sqrt(head_dim)
    soft = jax.nn.softplus(query_scale)
    factor = jnp.tile(soft * scale_const, heads_local)[:, None]
    projected = dg(stacked_w, gathered, 0, 1)
    qkv = (projected * jnp.concatenate([factor, jnp.ones((2 * width_local, 1), f32)])).astype(low)
    attended, logsum, attended_rows = attention_forward(group_span, qkv, heads_local)

    hidden_one = residual + contract_rows(attended_rows, w_out_all)
    second, inverse_two = rms_forward(hidden_one, gain_mlp)
    second_low = second.astype(low)
    before_act = contract_cols(second_low, w_up_all)
    activated = jax.nn.silu(before_act).astype(low)
    output = hidden_one + jnp.dot(activated, w_down_all, preferred_element_type=f32)
    grad_hidden_out = cotangent.astype(f32) * row_valid[:, None]
    grad_low = grad_hidden_out.astype(low)
    grad_act = contract_cols(grad_low, w_down_all)
    grad_pre = (grad_act * silu_slope(before_act)).astype(low)
    grad_second = jnp.dot(grad_pre, w_up_all, preferred_element_type=f32)
    grad_hidden = grad_hidden_out + rms_backward(hidden_one, inverse_two, gain_mlp, grad_second)
    branch_low = grad_hidden.astype(low)
    grad_att_rows = contract_cols(w_out_all, branch_low).astype(low)

    grad_w_down = contract_rows(activated, grad_low)
    grad_w_up_t = contract_rows(grad_pre, second_low)
    grad_w_out = jnp.dot(attended_rows, branch_low, preferred_element_type=f32)
    gain_two_part = jnp.sum(grad_w_up_t * w_up_all.astype(f32), axis=0)

    def by_member(grad):
        return grad.astype(low).reshape(4, pairs, width_local // pairs, model)

    grad_stacked, grad_first, plane_sum = attention_backward(
        group_span, qkv, attended, logsum, factor, stacked_w, grad_att_rows,
        by_member(grad_w_out), by_member(grad_w_up_t), by_member(grad_w_down),
    )
    grad_stacked_w = dg(gathered, grad_stacked, 0, 1)
    weighted = grad_stacked_w * stacked_w.astype(f32)
    gain_one_part = jnp.sum(weighted, axis=1)
    scale_part = jnp.sum(
        jnp.sum(weighted[:, :width_local], axis=0).reshape(heads_local, head_dim), axis=0
    )
    small = jnp.concatenate([gain_one_part, gain_two_part, scale_part])
    lanes = 128
    small = jnp.pad(small, (0, -small.size % (8 * lanes))).reshape(-1, lanes)
    mlp_all, qkv_all, small = weight_sums(
        plane_sum,
        grad_stacked_w.astype(low).reshape(pairs, model // pairs, 3 * width_local),
        small,
    )
    small = small.reshape(-1)
    grad_input = grad_hidden + rms_backward(
        residual, inverse_one, gain_attn, grad_first.astype(f32)
    )
    grad_gain_one = small[:model] / gain_attn
    grad_gain_two = small[model : 2 * model] / gain_mlp
    grad_scale = small[2 * model : 2 * model + head_dim] * jax.nn.sigmoid(query_scale) / soft
    mlp_all = mlp_all.astype(f32).reshape(pairs, 2, 3, width_local // pairs, model // 2)

    def final_weight(w):
        return jnp.transpose(mlp_all[:, :, w], (0, 2, 1, 3)).reshape(width_local, model)

    grad_out_final = final_weight(0)
    grad_up_final = jnp.transpose(final_weight(1))
    grad_down_final = final_weight(2)
    qkv_all = qkv_all.astype(f32).reshape(model, 3 * width_local)
    return (
        output.astype(low),
        grad_input,
        grad_gain_one,
        grad_gain_two,
        grad_scale,
        qkv_all[:, :width_local],
        qkv_all[:, width_local : 2 * width_local],
        qkv_all[:, 2 * width_local :],
        grad_out_final,
        grad_up_final,
        grad_down_final,
    )


def solution(mesh):
    rows = P(("dp", "tensor"), None)
    cols_t = P(None, "tensor")
    rows_t = P("tensor", None)
    return jax.shard_map(
        per_device,
        mesh=mesh,
        in_specs=(
            rows, rows, P(), P(), P(), cols_t, cols_t, cols_t, rows_t, cols_t, rows_t, P("dp"), P("dp"),
        ),
        out_specs=(
            rows, rows, P(), P(), P(), cols_t, cols_t, cols_t, rows_t, cols_t, rows_t,
        ),
        check_vma=False,
    )
```

time: 679 us -> 472 us (0.70)
  Pallas kernels: 170 us -> 303 us
  waiting for transfers between devices: 161 us -> 30.7 us
  matrix products: 158 us -> 43.5 us
  blocking collectives: 41.8 us -> 0 us
  local copies, waits for them, and re-layouts: 77.3 us -> 41.8 us
  other arithmetic: 42.6 us -> 27.9 us
    pallas_call x4, Pallas kernels: 170 us -> 303 us  [the longest x1 122 us: attention_backward(): pl.pallas_call(backward_kernel, out_shape=(jax.ShapeDtypeStruct(qkv.shape...]
    dot_general x28 -> x3, matrix products: 114 us -> 20.9 us  [the longest x2 17.1 us: dg(): lax.dot_general(left, right, (((left_dim,), (right_dim,)), ((), ())), pre...]
    ppermute x3 -> x0, waiting for transfers between devices: 76.1 us -> none  [the longest x1 50 us: per_device(): lax.ppermute(qkv_part, 'tensor', swap_line).astype(f32)]
    psum x1 -> x0, blocking collectives: 41.8 us -> none  [per_device(): lax.psum(jnp.concatenate([gain_one_part, gain_two_part, scale_part]), ('d...]
    reduce_scatter x3 -> x0, waiting for transfers between devices: 38.5 us -> none  [the longest x1 38.4 us: per_device(): lax.psum_scatter(grad_stacked_w.astype(low), 'dp', scatter_dimension=0, t...]
    slice x14 -> x0, local copies, waits for them, and re-layouts: 16.7 us -> none  [the longest x5 8.11 us: attention_backward(): grad_att_block = grad_att_heads[first_row:last_row]]
    all_gather x6 -> x2, waiting for transfers between devices: 45.2 us -> 30.7 us  [the longest x1 30.7 us: per_device(): line_w = lax.all_gather(own_slice, 'tensor', axis=0, tiled=False)]
    reduce_sum x5 -> x1, other arithmetic: 15.4 us -> 3.09 us  [per_device(): gain_one_part = jnp.sum(weighted, axis=1)]
  transfers between devices with their start and end apart: 13 -> 3, of which waited for: 5 -> 1; matrix products, arithmetic and copies ran while one was open for 35% -> 5% of each run, Pallas kernels for 25% -> 23%
where the time goes in v2:
time: 472 us; the launch traced here: 463 us
  Pallas kernels  303 us (64%)
  matrix products  43.5 us (9%)
  local copies, waits for them, and re-layouts  41.8 us (9%)
  waiting for transfers between devices  30.7 us (7%)
  other arithmetic  27.9 us (6%)
  between operations  15.9 us (3%)
    pallas_call x1, Pallas kernels, attention_backward(): pl.pallas_call(backward_kernel, out_shape=(jax.ShapeDtypeStruct(qkv.shape...  122 us
    pallas_call x1, Pallas kernels, weight_sums(): pl.pallas_call(weights_kernel, out_shape=(jax.ShapeDtypeStruct((2 * pairs...  74.3 us
    pallas_call x1, Pallas kernels, gather_rows(): pl.pallas_call(gather_kernel, out_shape=(jax.ShapeDtypeStruct((4 * rows,...  64.4 us
    pallas_call x1, Pallas kernels, attention_forward(): pl.pallas_call(forward_kernel, out_shape=(jax.ShapeDtypeStruct((width, sl...  41.8 us
    all_gather x1, waiting for transfers between devices, per_device(): line_w = lax.all_gather(own_slice, 'tensor', axis=0, tiled=False)  30.7 us
    unnamed x43, local copies, waits for them, and re-layouts  19 us
    dot_general x2, matrix products, dg(): lax.dot_general(left, right, (((left_dim,), (right_dim,)), ((), ())), pre...  17.1 us
    dot_general x3, matrix products, contract_rows(): lax.dot_general(left, right, (((0,), (0,)), ((), ())), preferred_element_...  10 us
  transfers between devices with their start and end apart: 3, of which 1 were waited for; matrix products, arithmetic and copies ran while one was open for 5% of the time, Pallas kernels for 23%

profile of v2, /device:TPU:27, one launch (start us, length us, event | category | flops | bytes accessed | tf_op | source)
XLA Modules:
  0.0 463.2 jit_solution(2682926639248821060)
XLA Ops:
  7.2 1.1 copy-done
  8.4 1.0 dynamic-slice_bitcast_fusion
  9.4 0.8 pad_maximum_fusion.1
  10.2 30.7 %all-gather.5.cloned.1.call-done = bf16[12,40,1280]{2,1,0:T(8,128)(2,1)} async-done(((bf16[3,40,1280]{2,1,0:T(8,128)(2,1)}), bf16[12,40,1280]{2,1,0:T(8,128)(2,1)}) %all-gather.5.cloned.1.call-update) | async-done | bytes 1228816 | tf_op jit(solution)/shard_map/all_gather | solution.py:932
  42.8 0.6 copy.80
  43.4 2.2 copy.79
  45.6 2.2 copy.78
  48.0 0.8 copy.84.factor
  49.1 4.0 pad_maximum_fusion
  53.1 1.4 fusion.5.own
  54.5 64.4 %gather_rows.1 = (bf16[2048,1280]{1,0:T(8,128)(2,1)}, bf16[8,160,960]{2,1,0:T(8,128)(2,1)}) custom-call(bf16[512,1280]{1,0:T(8,128)(2,1)} %fusion.5.own, bf16[8,160,960]{2,1,0:T(8,128)(2,1)} %bitcast.91), custom_call_target="tpu_custom_call" | custom-call | tf_op jit(solution)/shard_map/gather_rows/pallas_call | solution.py:220
  119.0 3.7 bitcast_select_fusion.weights
  122.9 7.5 %multiply_convert_fusion.qkv = bf16[960,2048]{1,0:T(8,128)(2,1)} fusion(bf16[1280,960]{1,0:T(8,128)(2,1)S(1)} %bitcast_select_fusion.weights, bf16[2048,1280]{1,0:T(8,128)(2,1)S(1)} %copy-done.14, f32[960]{0:T(1024)S(1)} %bitcast.109), kind=kOutput, calls=%fused_computation | convolution fusion | flops 5037096960 | bytes 11636480 | tf_op jit(solution)/shard_map/dot_general | solution.py:243
  130.4 41.8 %attention_forward.1 = (bf16[320,2048]{1,0:T(8,128)(2,1)S(1)}, f32[4,2048]{1,0:T(4,128)S(1)}, bf16[1280,512]{1,0:T(8,128)(2,1)S(1)}) custom-call(s32[2]{0:T(128)S(1)} %broadcast_select_fusion.span, bf16[960,2048]{1,0:T(8,128)(2,1)} %multiply_convert_fusion.qkv), custom_call_target="tpu_custom_call" | custom-call | tf_op jit(solution)/shard_map/attention_forward/pallas_call | solution.py:347
  172.2 1.0 copy-done.2
  173.9 4.8 %slice_bitcast_fusion.1 = (bf16[4,8,40,1280]{3,2,0,1:T(8,128)(2,1)S(1)}, bf16[4,8,40,1280]{3,2,0,1:T(8,128)(2,1)S(1)}, bf16[4,8,40,1280]{3,2,0,1:T(8,128)(2,1)S(1)}) fusion(bf16[8,4,3,40,1280]{4,3,2,1,0:T(8,128)(2,1)} %bitcast.92), kind=kLoop, calls=%fused_computation.15 | loop fusion | bytes 19660800 | tf_op jit(solution)/shard_map/transpose | solution.py:936
  179.4 2.2 multiply_reduce_fusion.2
  181.5 1.9 fusion.23
  183.5 3.3 fusion.3
  186.8 2.3 fusion.4
  189.1 2.1 multiply_reduce_fusion.1
  191.2 0.7 multiply_add_fusion
  191.9 3.0 convolution_convert_fusion.2.split
  194.9 3.7 convolution_convert_fusion.1
  198.6 4.0 multiply_reduce_fusion
  202.6 3.9 convolution_convert_fusion
  206.5 122.4 %attention_backward.1 = (bf16[960,2048]{1,0:T(8,128)(2,1)}, bf16[512,1280]{1,0:T(8,128)(2,1)}, bf16[4,3,80,640]{3,2,1,0:T(8,128)(2,1)}) custom-call(s32[2]{0:T(128)} %copy-done.4, bf16[960,2048]{1,0:T(8,128)(2,1)} %multiply_convert_fusion.qkv, bf16[320,2048]{1,0:T(8,128)(2,1)} %copy-done.2, f32[4,2048]{1,0:T(4,128)} %copy-done.3, f32[320,1]{1,0:T(8,128)} %copy.84.factor, ...), custom_call_target="tpu_custom_call" | custom-call | tf_op jit(solution)/shard_map/attention_backward/pallas_call | solution.py:640
  329.0 2.1 fusion.6
  331.1 3.7 fusion.9
  334.8 9.7 %fusion.26 = (bf16[1280,960]{0,1:T(8,128)(2,1)S(1)}, f32[1280,960]{0,1:T(8,128)}) fusion(bf16[960,2048]{1,0:T(8,128)(2,1)S(1)} %copy-done.15, bf16[2048,1280]{1,0:T(8,128)(2,1)} %get-tuple-element.23), kind=kOutput, calls=%fused_computation.73 | convolution fusion | flops 5034393600 | bytes 16547840 | tf_op jit(solution)/shard_map/dot_general | solution.py:243
  344.4 3.5 copy.85
  348.0 6.0 %copy.86 = f32[1280,960]{1,0:T(8,128)} copy(f32[1280,960]{0,1:T(8,128)} %get-tuple-element.54) | data formatting | bytes 9830400 | tf_op jit(solution)/shard_map/dot_general | solution.py:243
  354.0 3.1 fusion.24
  358.1 74.3 %weight_sums.1 = (bf16[8,3,80,640]{3,2,1,0:T(8,128)(2,1)}, bf16[4,320,960]{2,1,0:T(8,128)(2,1)}, f32[24,128]{1,0:T(8,128)}) custom-call(bf16[4,3,80,640]{3,2,1,0:T(8,128)(2,1)} %get-tuple-element.28.mlp, bf16[4,320,960]{2,1,0:T(8,128)(2,1)} %bitcast.90, f32[24,128]{1,0:T(8,128)} %fusion.16.small), custom_call_target="tpu_custom_call" | custom-call | tf_op jit(solution)/shard_map/weight_sums/pallas_call | solution.py:855
  432.4 1.4 bitcast_divide_fusion
  433.8 1.2 fusion.21
  435.0 2.4 bitcast_convert_fusion
  437.4 2.8 fusion.25
  440.2 2.7 copy.93
  442.9 2.7 copy.94
  445.6 1.7 copy.95
  447.3 2.1 convert.3
  449.8 0.8 copy.90
  450.7 1.3 copy.96
  451.9 0.8 copy.91
  452.8 1.3 copy.97
  454.1 0.8 copy.92
  454.9 1.3 copy.98
  (60 shorter events, 4.1 us)
Async XLA Ops:
  7.2 1.2 copy-start
  7.2 33.7 %all-gather.5.cloned.1.call-start = ((), (), s32[]{:S(2)}) async-start(), calls=%async_computation | async-start | bytes 1536000 | tf_op jit(solution)/shard_map/all_gather | solution.py:932
  8.3 34.5 %copy-start.11 = (bf16[1280,320]{0,1:T(8,128)(2,1)S(1)}, bf16[1280,320]{0,1:T(8,128)(2,1)}, u32[]{:S(2)}) copy-start(bf16[1280,320]{0,1:T(8,128)(2,1)} %param.20) | copy-start | bytes 2457604
  10.2 163.7 %all-gather.7.cloned.1.call-start = ((), (), s32[]{:S(2)}) async-start(), calls=%async_computation.1 | async-start | bytes 11059200 | tf_op jit(solution)/shard_map/all_gather | solution.py:933
  42.3 88.1 %collective-permute-start = (s32[2]{0:T(128)S(1)}, s32[2]{0:T(128)S(1)}, u32[]{:S(2)}, u32[]{:S(2)}) collective-permute-start(s32[2]{0:T(128)S(1)} %pad_add_fusion), channel_id=1, source_target_pairs={{0,4},{4,0},{8,12},{12,8},{16,20},{20,16},{24,28},{28,24},{1,5},{5... | collective-permute-start | bytes 32 | tf_op jit(solution)/shard_map/ppermute | solution.py:941
  42.8 5.1 %copy-start.16 = (f32[80]{0:T(128)S(1)}, f32[80]{0:T(128)}, u32[]{:S(2)}) copy-start(f32[80]{0:T(128)} %param.17) | copy-start | bytes 964
  42.8 6.0 %copy-start.5 = (bf16[512,1280]{1,0:T(8,128)(2,1)S(1)}, bf16[512,1280]{1,0:T(8,128)(2,1)}, u32[]{:S(2)}) copy-start(bf16[512,1280]{1,0:T(8,128)(2,1)} %param.13) | copy-start | bytes 3932164
  49.1 4.0 copy-start.12
  119.0 3.9 copy-start.14
  122.7 7.6 %copy-start.6 = (bf16[1280,960]{1,0:T(8,128)(2,1)}, bf16[1280,960]{1,0:T(8,128)(2,1)S(1)}, u32[]{:S(2)}) copy-start(bf16[1280,960]{1,0:T(8,128)(2,1)S(1)} %bitcast_select_fusion.weights) | copy-start | bytes 7372804
  130.4 48.2 %copy-start.4 = (s32[2]{0:T(128)}, s32[2]{0:T(128)S(1)}, u32[]{:S(2)}) copy-start(s32[2]{0:T(128)S(1)} %broadcast_select_fusion.span) | copy-start | bytes 28
  172.2 1.1 copy-start.2
  173.3 0.6 copy-start.3
  179.3 2.2 copy-start.13
  183.5 3.3 copy-start.10
  191.9 3.0 copy-start.8
  328.9 2.1 copy-start.9
  331.1 3.7 copy-start.15
  348.0 6.1 %copy-start.7 = (bf16[1280,960]{1,0:T(8,128)(2,1)S(1)}, bf16[1280,960]{1,0:T(8,128)(2,1)}, u32[]{:S(2)}) copy-start(bf16[1280,960]{1,0:T(8,128)(2,1)} %copy-done.6) | copy-start | bytes 7372804
  454.1 2.1 copy-start.1
Sparse Core Ops, SparseCore 0:
  10.3 30.5 all-gather.4
  42.8 72.1 all-gather.6

commit v3 on v2

--- a/solution.py
+++ b/solution.py
@@ -369,13 +369,18 @@
 
 
 def backward_kernel(
-    span, qkv, out, logsum, factor, weights, split, grad_out, grad_up, grad_down,
-    result, rows_grad, plane_sum,
-    grad, query_sum, key_sum, value_sum, term,
+    span, qkv, out, logsum, factor, weights, small, split, grad_out, grad_up, grad_down, gathered,
+    rows_grad, mlp_all, qkv_all, small_all,
+    result, grad, query_sum, key_sum, value_sum, term,
     partial, from_core, from_line, keep_in, chip_sum, plane_in,
+    normed, weight_grad, qkv_in, qkv_swap, mlp_in, mlp_sum,
+    small_own, small_pair, small_plane, small_line,
     split_sent, split_got, local_sem, keep_sem,
     give_sent, give_got, plane_sent, plane_got,
     send_c, send_z, recv_c, recv_z,
+    out_sem, normed_sem, qkv_sent, qkv_got, cross_sent, cross_got, qkv_spread, qkv_share, qkv_have, qkv_local,
+    line_sent, line_got, mlp_spread, mlp_share, mlp_have, mlp_local,
+    small_sems, small_across_sent, small_across_got, small_along_sent, small_along_got,
 ):
     heads = logsum.shape[0]
     width, slots = out.shape
@@ -442,6 +447,8 @@
     for w in range(3):
         give(w).start()
     own_half(0, 0).start()
+    out_copy = pltpu.make_async_copy(out, result.at[pl.ds(0, width)], out_sem)
+    out_copy.start()
     query_sum[...] = jnp.zeros_like(query_sum)
     key_sum[...] = jnp.zeros_like(key_sum)
     value_sum[...] = jnp.zeros_like(value_sum)
@@ -472,9 +479,10 @@
         def _(block=block):
             remote(of(0), into(block), split_sent.at[0], split_got.at[block], partner).wait_recv()
 
+    out_copy.wait()
     for h in range(heads):
         hs = pl.ds(h * dim, dim)
-        term[h : h + 1] = jnp.sum(grad[hs].astype(f32) * out[hs].astype(f32), axis=0, keepdims=True)
+        term[h : h + 1] = jnp.sum(grad[hs].astype(f32) * result[hs].astype(f32), axis=0, keepdims=True)
 
     def span_of(seq, k, ch):
         block = jnp.where(seq == 0, k, 3 - k)
@@ -483,6 +491,9 @@
     def piece(k, ch):
         return pl.ds(pl.multiple_of(k * rows + ch * part, part), part)
 
+    def line_piece(k, ch):
+        return piece(k % 3 if isinstance(k, int) else lax.rem(k, 3), ch)
+
     def line_rows(ch):
         return pl.ds(ch * part, part)
 
@@ -494,7 +505,7 @@
         at = span_of(here.g, k, ch)
         return remote(
             partial.at[at],
-            from_line.at[piece((k % 3 if isinstance(k, int) else lax.rem(k, 3)), ch)],
+            from_line.at[line_piece(k, ch)],
             send_z.at[k, ch],
             recv_z.at[k, ch],
             here.device(here.c, jnp.where(here.pos == 0, 1, 0)),
@@ -512,7 +523,7 @@
 
     def with_line(k, ch):
         line_copy(k, ch).wait_recv()
-        return core_sum(k, ch) + from_line[piece((k % 3 if isinstance(k, int) else lax.rem(k, 3)), ch)].astype(f32)
+        return core_sum(k, ch) + from_line[line_piece(k, ch)].astype(f32)
 
     def pass_on(k):
         for ch in range(CHUNKS):
@@ -527,6 +538,7 @@
     @pl.loop(0, blocks)
     def _(s):
         b = jnp.where(here.g == 0, blocks - 1 - s, s)
+        k = blocks - 1 - s
 
         def tile(i, j, diagonal):
             qs = pl.ds(pl.multiple_of(i * TILE, TILE), TILE)
@@ -548,16 +560,20 @@
                 key_sum[hs, ks] += dg(qkv[hs, qs], grad_scores, 1, 1)
                 query_sum[hs, qs] += dg(qkv[ke, ks], grad_scores, 1, 0)
 
+        tile(b, b, True)
+
+        @pl.when((here.pos == 0) & (s >= 1))
+        def _():
+            pass_on(k + 1)
+
         @pl.loop(0, blocks - 1 - s)
         def _(n):
             tile(jnp.where(here.g == 0, b, b + 1 + n), jnp.where(here.g == 0, n, b), False)
 
-        tile(b, b, True)
         bs = pl.ds(pl.multiple_of(b * TILE, TILE), TILE)
         result[pl.ds(0, width), bs] = (query_sum[:, bs] * factor[...]).astype(low)
         result[pl.ds(width, width), bs] = key_sum[:, bs].astype(low)
         result[pl.ds(2 * width, width), bs] = value_sum[:, bs].astype(low)
-        k = blocks - 1 - s
         partial[bs] = dg(result[:, bs], weights[...], 0, 1).astype(low)
 
         @pl.when(jnp.logical_not(here.main))
@@ -565,13 +581,72 @@
             for ch in range(CHUNKS):
                 core_copy(k, ch).start()
 
-        @pl.when((here.pos == 0) & (s >= 1))
+    @pl.when(here.pos == 1)
+    def _():
+        send_home(3)
+
+    chunks, _, share, _ = weight_grad.shape
+    depth = pairs * share
+
+    half_slots = slots // 2
+
+    def load(i, part_of):
+        return pltpu.make_async_copy(
+            gathered.at[
+                pl.ds(part_of * half_slots, half_slots), pl.ds(pl.multiple_of(i * depth, depth), depth)
+            ],
+            normed.at[part_of],
+            normed_sem.at[part_of],
+        )
+
+    def qkv_send(i, step):
+        return remote(
+            weight_grad.at[i, lax.rem(here.pair + step, pairs)],
+            qkv_in.at[i, step - 1],
+            qkv_sent.at[i, step - 1],
+            qkv_got.at[i, step - 1],
+            here.across(step),
+        )
+
+    small_own[...] = small[...]
+    load(0, 0).start()
+    load(0, 1).start()
+
+    @pl.loop(0, chunks)
+    def _(i):
+        at = pl.ds(pl.multiple_of(i * depth, depth), depth)
+        load(i, 0).wait()
+        grads = dg(normed[0], result[:, :half_slots], 0, 1)
+
+        @pl.when(i + 1 < chunks)
         def _():
-            pass_on(k + 1)
-
-        @pl.when((here.pos == 1) & (s >= 2))
+            load(i + 1, 0).start()
+
+        load(i, 1).wait()
+        grads += dg(normed[1], result[:, half_slots:], 0, 1)
+
+        @pl.when(i + 1 < chunks)
         def _():
-            send_home(k + 2)
+            load(i + 1, 1).start()
+
+        for p in range(pairs):
+            weight_grad[i, p] = grads[p * share : (p + 1) * share].astype(low)
+        for step in range(1, pairs):
+            qkv_send(i, step).start()
+        weighted = grads * weights[at].astype(f32)
+        by_row = jnp.sum(weighted, axis=1, keepdims=True)
+        small_own[0:1, at] = jnp.transpose(jnp.broadcast_to(by_row, (depth, 128)))[0:1]
+        small_own[2:3, pl.ds(0, 3 * width)] += jnp.sum(weighted, axis=0, keepdims=True)
+
+    small_copy = remote(small_own, small_pair, small_sems.at[0], small_sems.at[1], partner)
+    small_copy.start()
+
+    def mlp_line(step):
+        line = lax.rem(here.t + step, 4)
+        return remote(
+            chip_sum.at[:, line, here.pair], mlp_in.at[step - 1], line_sent.at[step - 1], line_got.at[step - 1],
+            (here.d, line),
+        )
 
     for w in range(3):
         for step in range(1, pairs):
@@ -582,7 +657,130 @@
             total = chip_sum[w, q, here.pair].astype(f32)
             for step in range(1, pairs):
                 total += plane_in[step - 1, w, q].astype(f32)
-            plane_sum[q, w] = total.astype(low)
+            chip_sum[w, q, here.pair] = total.astype(low)
+
+    for step in range(1, 4):
+        mlp_line(step).start()
+
+    @pl.when(here.pos == 1)
+    def _():
+        pass_on(0)
+        send_home(2)
+
+    line = lax.rem(here.t + 2, 4)
+
+    def cross(i):
+        return remote(
+            qkv_swap.at[0, i], qkv_swap.at[1, i], cross_sent.at[i], cross_got.at[i],
+            (here.base + line // 2, line),
+        )
+
+    def qkv_out(i, step):
+        return remote(
+            qkv_swap.at[0, i], qkv_all.at[i, here.pair], qkv_spread.at[i, step], qkv_have.at[i, here.pair],
+            here.across(step),
+        )
+
+    def qkv_own(i):
+        return remote(
+            qkv_swap.at[0, i], qkv_all.at[i, here.pair], qkv_share.at[i, 0], qkv_have.at[i, here.pair], partner
+        )
+
+    def qkv_keep(i):
+        return pltpu.make_async_copy(qkv_swap.at[0, i], qkv_all.at[i, here.pair], qkv_local.at[i])
+
+    def qkv_core(i, step):
+        pair = lax.rem(here.pair + step, pairs)
+        return remote(
+            qkv_all.at[i, pair], qkv_all.at[i, pair], qkv_share.at[i, step], qkv_have.at[i, pair], partner
+        )
+
+    def finish(i):
+        @pl.when(here.main)
+        def _():
+            cross(i).wait_recv()
+            qkv_swap[0, i] = (qkv_swap[0, i].astype(f32) + qkv_swap[1, i].astype(f32)).astype(low)
+            qkv_keep(i).start()
+            for step in range(1, pairs):
+                qkv_out(i, step).start()
+            qkv_own(i).start()
+
+    @pl.loop(0, chunks)
+    def _(i):
+        total = weight_grad[i, here.pair].astype(f32)
+        for step in range(1, pairs):
+            qkv_send(i, step).wait_recv()
+            total += qkv_in[i, step - 1].astype(f32)
+        qkv_swap[0, i] = total.astype(low)
+
+        @pl.when(jnp.logical_not(here.main))
+        def _():
+            cross(i).start()
+
+        @pl.when(i >= 1)
+        def _():
+            finish(i - 1)
+
+    finish(chunks - 1)
+
+    small_copy.wait_recv()
+    small_plane[here.pair] = small_own[...] + small_pair[...]
+
+    def small_across(step):
+        return remote(
+            small_plane.at[here.pair], small_plane.at[here.pair], small_across_sent.at[step],
+            small_across_got.at[here.pair], here.across(step),
+        )
+
+    def small_along(step):
+        return remote(
+            small_line.at[here.t], small_line.at[here.t], small_along_sent.at[step], small_along_got.at[here.t],
+            (here.d, lax.rem(here.t + step, 4)),
+        )
+
+    for step in range(1, pairs):
+        small_across(step).start()
+
+    for step in range(1, 4):
+        mlp_line(step).wait_recv()
+    mlp_total = chip_sum[:, here.t, here.pair].astype(f32)
+    for step in range(1, 4):
+        mlp_total += mlp_in[step - 1].astype(f32)
+    mlp_sum[...] = mlp_total.astype(low)
+
+    def mlp_out(step):
+        return remote(
+            mlp_sum, mlp_all.at[here.d], mlp_spread.at[step], mlp_have.at[here.d], here.across(step)
+        )
+
+    mlp_own = remote(mlp_sum, mlp_all.at[here.d], mlp_share.at[0], mlp_have.at[here.d], partner)
+    mlp_keep = pltpu.make_async_copy(mlp_sum, mlp_all.at[here.d], mlp_local)
+
+    def mlp_core(step):
+        member = 2 * lax.rem(here.pair + step, pairs) + here.c
+        return remote(
+            mlp_all.at[member], mlp_all.at[member], mlp_share.at[step], mlp_have.at[member], partner
+        )
+
+    def mlp_arrived(member):
+        remote(mlp_sum, mlp_all.at[member], mlp_share.at[0], mlp_have.at[member], partner).wait_recv()
+
+    for step in range(1, pairs):
+        mlp_out(step).start()
+    mlp_own.start()
+    mlp_keep.start()
+
+    for step in range(1, pairs):
+        pair = lax.rem(here.pair + step, pairs)
+        remote(
+            small_own, small_plane.at[pair], small_across_sent.at[0], small_across_got.at[pair], partner
+        ).wait_recv()
+    plane_total = small_plane[0]
+    for pair in range(1, pairs):
+        plane_total += small_plane[pair]
+    small_line[here.t] = plane_total
+    for step in range(1, 4):
+        small_along(step).start()
 
     @pl.when(here.pos == 0)
     def _():
@@ -594,7 +792,6 @@
 
     @pl.when(here.pos == 1)
     def _():
-        pass_on(0)
         for ch in range(CHUNKS):
             rows_grad[line_rows(ch)] = with_line(1, ch).astype(low)
         for ch in range(CHUNKS):
@@ -610,11 +807,51 @@
                     partial.at[piece(0, ch)], rows_grad.at[line_rows(ch)], send_z.at[0, ch], recv_z.at[k, ch], partner
                 ).wait_recv()
 
+    for step in range(1, 4):
+        other = lax.rem(here.t + step, 4)
+        remote(
+            small_own, small_line.at[other], small_along_sent.at[0], small_along_got.at[other], partner
+        ).wait_recv()
+    small_all[...] = (small_line[0] + small_line[1]) + (small_line[2] + small_line[3])
+
+    @pl.when(here.main)
+    def _():
+        @pl.loop(0, chunks)
+        def _(i):
+            for step in range(1, pairs):
+                qkv_core(i, step).wait_recv()
+                qkv_core(i, step).start()
+
+    for step in range(1, pairs):
+        mlp_arrived(2 * lax.rem(here.pair + step, pairs) + here.c)
+        mlp_core(step).start()
+
+    @pl.when(here.main)
+    def _():
+        @pl.loop(0, chunks)
+        def _(i):
+            qkv_keep(i).wait()
+            qkv_own(i).wait_send()
+            for step in range(1, pairs):
+                qkv_out(i, step).wait_send()
+                qkv_core(i, step).wait_send()
+
     @pl.when(jnp.logical_not(here.main))
     def _():
+        @pl.loop(0, chunks)
+        def _(i):
+            cross(i).wait_send()
+            for step in range(pairs):
+                qkv_core(i, step).wait_recv()
+
         for k in range(4):
             for ch in range(CHUNKS):
                 core_copy(k, ch).wait_send()
+
+    for step in range(pairs):
+        mlp_arrived(2 * lax.rem(here.pair + step, pairs) + 1 - here.c)
+    mlp_keep.wait()
+    mlp_own.wait_send()
 
     for q in range(4):
         @pl.when(jnp.logical_not(here.main & (here.t == q)))
@@ -626,38 +863,71 @@
         for step in range(1, pairs):
             plane_copy(w, step).wait_send()
 
-
-def attention_backward(span, qkv, out, logsum, factor, weights, split, grad_out, grad_up, grad_down):
+    @pl.loop(0, chunks)
+    def _(i):
+        for step in range(1, pairs):
+            qkv_send(i, step).wait_send()
+
+    for step in range(1, pairs):
+        mlp_out(step).wait_send()
+        mlp_core(step).wait_send()
+        small_across(step).wait_send()
+    for step in range(1, 4):
+        mlp_line(step).wait_send()
+        small_along(step).wait_send()
+    small_copy.wait_send()
+
+
+DEPTH = 256
+
+
+def attention_backward(
+    span, qkv, out, logsum, factor, weights, small, split, grad_out, grad_up, grad_down, gathered
+):
     width, slots = out.shape
     heads = logsum.shape[0]
     rows, model = split.shape[1], weights.shape[0]
     low, f32 = qkv.dtype, jnp.float32
     pairs, slice_rows = grad_out.shape[1], grad_out.shape[2]
     columns = model // 2
+    chunks, share = model // DEPTH, DEPTH // pairs
     vmem = pl.BlockSpec(memory_space=pltpu.VMEM)
     hbm = pl.BlockSpec(memory_space=pl.ANY)
     dma = pltpu.SemaphoreType.DMA
+    buffer = pltpu.VMEM
     return pl.pallas_call(
         backward_kernel,
         out_shape=(
-            jax.ShapeDtypeStruct(qkv.shape, low),
             jax.ShapeDtypeStruct((rows, model), low),
-            jax.ShapeDtypeStruct((4, 3, slice_rows, columns), low),
+            jax.ShapeDtypeStruct((2 * pairs, 3, slice_rows, columns), low),
+            jax.ShapeDtypeStruct((chunks, pairs, share, 3 * width), low),
+            jax.ShapeDtypeStruct(small.shape, f32),
         ),
-        in_specs=[pl.BlockSpec(memory_space=pltpu.SMEM)] + [vmem] * 5 + [hbm] * 4,
-        out_specs=(vmem,) * 3,
+        in_specs=[pl.BlockSpec(memory_space=pltpu.SMEM), vmem, hbm] + [vmem] * 4 + [hbm] * 5,
+        out_specs=(vmem, hbm, hbm, vmem),
         scratch_shapes=[
-            pltpu.VMEM((width, slots), low),
-            pltpu.VMEM((width, slots), f32),
-            pltpu.VMEM((width, slots), f32),
-            pltpu.VMEM((width, slots), f32),
-            pltpu.VMEM((heads, slots), f32),
-            pltpu.VMEM((slots, model), low),
-            pltpu.VMEM((slots, model), low),
-            pltpu.VMEM((3 * rows, model), low),
-            pltpu.VMEM((2, pairs, slice_rows, columns), low),
-            pltpu.VMEM((3, 4, pairs, slice_rows, columns), low),
-            pltpu.VMEM((pairs - 1, 3, 4, slice_rows, columns), low),
+            buffer(qkv.shape, low),
+            buffer((width, slots), low),
+            buffer((width, slots), f32),
+            buffer((width, slots), f32),
+            buffer((width, slots), f32),
+            buffer((heads, slots), f32),
+            buffer((slots, model), low),
+            buffer((slots, model), low),
+            buffer((3 * rows, model), low),
+            buffer((2, pairs, slice_rows, columns), low),
+            buffer((3, 4, pairs, slice_rows, columns), low),
+            buffer((pairs - 1, 3, 4, slice_rows, columns), low),
+            buffer((2, slots // 2, DEPTH), low),
+            buffer((chunks, pairs, share, 3 * width), low),
+            buffer((chunks, pairs - 1, share, 3 * width), low),
+            buffer((2, chunks, share, 3 * width), low),
+            buffer((3, 3, slice_rows, columns), low),
+            buffer((3, slice_rows, columns), low),
+            buffer(small.shape, f32),
+            buffer(small.shape, f32),
+            buffer((pairs,) + small.shape, f32),
+            buffer((4,) + small.shape, f32),
             dma((4,)),
             dma((4,)),
             dma,
@@ -670,228 +940,33 @@
             dma((4, CHUNKS)),
             dma((4, CHUNKS)),
             dma((4, CHUNKS)),
-        ],
-        compiler_params=pltpu.CompilerParams(
-            collective_id=2, has_side_effects=True, vmem_limit_bytes=60 * 1024 * 1024
-        ),
-        name="attention_backward",
-    )(span, qkv, out, logsum, factor, weights, split, grad_out, grad_up, grad_down)
-
-
-def weights_kernel(
-    mlp, qkv, small, mlp_all, qkv_all, small_all, mlp_in, qkv_in, qkv_swap, small_pair, small_plane, small_line,
-    mlp_sent, mlp_got, mlp_spread, mlp_share, mlp_have,
-    qkv_sent, qkv_got, qkv_cross, qkv_crossed, qkv_spread, qkv_share, qkv_have,
-    small_sent, small_got, plane_sent, plane_got, line_sent, line_got,
-):
-    here = Place()
-    pairs = here.pairs
-    pair_barrier(here, plane=True)
-    partner = here.partner()
-    f32 = jnp.float32
-
-    def mlp_send(step):
-        line = lax.rem(here.t + step, 4)
-        return remote(
-            mlp.at[line], mlp_in.at[step - 1], mlp_sent.at[step - 1], mlp_got.at[step - 1], (here.d, line)
-        )
-
-    def qkv_send(step):
-        return remote(
-            qkv.at[lax.rem(here.pair + step, pairs)],
-            qkv_in.at[step - 1],
-            qkv_sent.at[step - 1],
-            qkv_got.at[step - 1],
-            here.across(step),
-        )
-
-    small_copy = remote(small, small_pair, small_sent, small_got, partner)
-    small_copy.start()
-    for step in range(1, pairs):
-        qkv_send(step).start()
-    for step in range(1, 4):
-        mlp_send(step).start()
-    small_copy.wait_recv()
-    small_plane[here.pair] = small[...] + small_pair[...]
-
-    def small_across(step):
-        return remote(
-            small_plane.at[here.pair], small_plane.at[here.pair], plane_sent.at[step], plane_got.at[here.pair],
-            here.across(step),
-        )
-
-    def small_along(step):
-        return remote(
-            small_line.at[here.t], small_line.at[here.t], line_sent.at[step], line_got.at[here.t],
-            (here.d, lax.rem(here.t + step, 4)),
-        )
-
-    for step in range(1, pairs):
-        small_across(step).start()
-    for step in range(1, pairs):
-        pair = lax.rem(here.pair + step, pairs)
-        remote(
-            small_plane.at[pair], small_plane.at[pair], plane_sent.at[0], plane_got.at[pair], partner
-        ).wait_recv()
-    plane_total = small_plane[0]
-    for pair in range(1, pairs):
-        plane_total += small_plane[pair]
-    small_line[here.t] = plane_total
-    for step in range(1, 4):
-        small_along(step).start()
-
-    for step in range(1, pairs):
-        qkv_send(step).wait_recv()
-    total = qkv[here.pair].astype(f32)
-    for step in range(1, pairs):
-        total += qkv_in[step - 1].astype(f32)
-    qkv_swap[0] = total.astype(qkv_swap.dtype)
-    line = lax.rem(here.t + 2, 4)
-    cross = remote(
-        qkv_swap.at[0], qkv_swap.at[1], qkv_cross, qkv_crossed, (here.base + line // 2, line)
-    )
-
-    def qkv_piece(step):
-        return qkv_all.at[lax.rem(here.pair + step, pairs)]
-
-    def qkv_out(step):
-        return remote(
-            qkv_all.at[here.pair], qkv_all.at[here.pair], qkv_spread.at[step], qkv_have.at[here.pair],
-            here.across(step),
-        )
-
-    def qkv_core(step):
-        piece = lax.rem(here.pair + step, pairs)
-        return remote(
-            qkv_all.at[piece], qkv_all.at[piece], qkv_share.at[step], qkv_have.at[piece], partner
-        )
-
-    @pl.when(jnp.logical_not(here.main))
-    def _():
-        cross.start()
-
-    for step in range(1, 4):
-        mlp_send(step).wait_recv()
-    mlp_total = mlp[here.t].astype(f32)
-    for step in range(1, 4):
-        mlp_total += mlp_in[step - 1].astype(f32)
-    mlp_all[here.d] = mlp_total.astype(mlp_all.dtype)
-
-    def mlp_out(step):
-        return remote(
-            mlp_all.at[here.d], mlp_all.at[here.d], mlp_spread.at[step], mlp_have.at[here.d],
-            here.across(step),
-        )
-
-    def mlp_core(step):
-        member = 2 * lax.rem(here.pair + step, pairs) + here.c
-        return remote(
-            mlp_all.at[member], mlp_all.at[member], mlp_share.at[step], mlp_have.at[member], partner
-        )
-
-    def mlp_arrived(member):
-        remote(
-            mlp_all.at[member], mlp_all.at[member], mlp_share.at[0], mlp_have.at[member], partner
-        ).wait_recv()
-
-    for step in range(1, pairs):
-        mlp_out(step).start()
-    mlp_core(0).start()
-
-    @pl.when(here.main)
-    def _():
-        cross.wait_recv()
-        whole = qkv_swap[0].astype(f32) + qkv_swap[1].astype(f32)
-        qkv_all[here.pair] = whole.astype(qkv_all.dtype)
-        for step in range(1, pairs):
-            qkv_out(step).start()
-        qkv_core(0).start()
-
-    for step in range(1, pairs):
-        mlp_arrived(2 * lax.rem(here.pair + step, pairs) + here.c)
-        mlp_core(step).start()
-
-    @pl.when(here.main)
-    def _():
-        for step in range(1, pairs):
-            qkv_core(step).wait_recv()
-            qkv_core(step).start()
-        for step in range(1, pairs):
-            qkv_out(step).wait_send()
-        for step in range(pairs):
-            qkv_core(step).wait_send()
-
-    @pl.when(jnp.logical_not(here.main))
-    def _():
-        for step in range(pairs):
-            qkv_core(step).wait_recv()
-        cross.wait_send()
-
-    for step in range(pairs):
-        mlp_arrived(2 * lax.rem(here.pair + step, pairs) + 1 - here.c)
-    for step in range(1, 4):
-        mlp_send(step).wait_send()
-    for step in range(1, pairs):
-        qkv_send(step).wait_send()
-        mlp_out(step).wait_send()
-    for step in range(pairs):
-        mlp_core(step).wait_send()
-    for step in range(1, 4):
-        line = lax.rem(here.t + step, 4)
-        remote(small_line.at[line], small_line.at[line], line_sent.at[0], line_got.at[line], partner).wait_recv()
-    small_all[...] = (small_line[0] + small_line[1]) + (small_line[2] + small_line[3])
-    small_copy.wait_send()
-    for step in range(1, pairs):
-        small_across(step).wait_send()
-    for step in range(1, 4):
-        small_along(step).wait_send()
-
-
-def weight_sums(mlp, qkv, small):
-    vmem = pl.BlockSpec(memory_space=pltpu.VMEM)
-    low = mlp.dtype
-    pairs = qkv.shape[0]
-    dma = pltpu.SemaphoreType.DMA
-    return pl.pallas_call(
-        weights_kernel,
-        out_shape=(
-            jax.ShapeDtypeStruct((2 * pairs,) + mlp.shape[1:], low),
-            jax.ShapeDtypeStruct(qkv.shape, low),
-            jax.ShapeDtypeStruct(small.shape, small.dtype),
-        ),
-        in_specs=[vmem] * 3,
-        out_specs=(vmem,) * 3,
-        scratch_shapes=[
-            pltpu.VMEM((3,) + mlp.shape[1:], low),
-            pltpu.VMEM((pairs - 1,) + qkv.shape[1:], low),
-            pltpu.VMEM((2,) + qkv.shape[1:], low),
-            pltpu.VMEM(small.shape, small.dtype),
-            pltpu.VMEM((pairs,) + small.shape, small.dtype),
-            pltpu.VMEM((4,) + small.shape, small.dtype),
+            dma,
+            dma((2,)),
+            dma((chunks, pairs - 1)),
+            dma((chunks, pairs - 1)),
+            dma((chunks,)),
+            dma((chunks,)),
+            dma((chunks, pairs)),
+            dma((chunks, pairs)),
+            dma((chunks, pairs)),
+            dma((chunks,)),
             dma((3,)),
             dma((3,)),
             dma((pairs,)),
             dma((pairs,)),
             dma((2 * pairs,)),
-            dma((pairs - 1,)),
-            dma((pairs - 1,)),
             dma,
-            dma,
-            dma((pairs,)),
-            dma((pairs,)),
-            dma((pairs,)),
-            dma,
-            dma,
+            dma((2,)),
             dma((pairs,)),
             dma((pairs,)),
             dma((4,)),
             dma((4,)),
         ],
         compiler_params=pltpu.CompilerParams(
-            collective_id=3, has_side_effects=True, vmem_limit_bytes=56 * 1024 * 1024
+            collective_id=2, has_side_effects=True, vmem_limit_bytes=65_500_000
         ),
-        name="weight_sums",
-    )(mlp, qkv, small)
+        name="attention_backward",
+    )(span, qkv, out, logsum, factor, weights, small, split, grad_out, grad_up, grad_down, gathered)
 
 
 def per_device(
@@ -981,31 +1056,20 @@
     def by_member(grad):
         return grad.astype(low).reshape(4, pairs, width_local // pairs, model)
 
-    grad_stacked, grad_first, plane_sum = attention_backward(
-        group_span, qkv, attended, logsum, factor, stacked_w, grad_att_rows,
-        by_member(grad_w_out), by_member(grad_w_up_t), by_member(grad_w_down),
-    )
-    grad_stacked_w = dg(gathered, grad_stacked, 0, 1)
-    weighted = grad_stacked_w * stacked_w.astype(f32)
-    gain_one_part = jnp.sum(weighted, axis=1)
-    scale_part = jnp.sum(
-        jnp.sum(weighted[:, :width_local], axis=0).reshape(heads_local, head_dim), axis=0
-    )
-    small = jnp.concatenate([gain_one_part, gain_two_part, scale_part])
-    lanes = 128
-    small = jnp.pad(small, (0, -small.size % (8 * lanes))).reshape(-1, lanes)
-    mlp_all, qkv_all, small = weight_sums(
-        plane_sum,
-        grad_stacked_w.astype(low).reshape(pairs, model // pairs, 3 * width_local),
-        small,
-    )
-    small = small.reshape(-1)
+    small = jnp.concatenate(
+        [jnp.zeros((1, model), f32), gain_two_part[None], jnp.zeros((6, model), f32)]
+    )
+    grad_first, mlp_all, qkv_all, small = attention_backward(
+        group_span, qkv, attended, logsum, factor, stacked_w, small, grad_att_rows,
+        by_member(grad_w_out), by_member(grad_w_up_t), by_member(grad_w_down), gathered,
+    )
     grad_input = grad_hidden + rms_backward(
         residual, inverse_one, gain_attn, grad_first.astype(f32)
     )
-    grad_gain_one = small[:model] / gain_attn
-    grad_gain_two = small[model : 2 * model] / gain_mlp
-    grad_scale = small[2 * model : 2 * model + head_dim] * jax.nn.sigmoid(query_scale) / soft
+    grad_gain_one = small[0] / gain_attn
+    grad_gain_two = small[1] / gain_mlp
+    scale_sum = jnp.sum(small[2, :width_local].reshape(heads_local, head_dim), axis=0)
+    grad_scale = scale_sum * jax.nn.sigmoid(query_scale) / soft
     mlp_all = mlp_all.astype(f32).reshape(pairs, 2, 3, width_local // pairs, model // 2)
 
     def final_weight(w):

time: 472 us -> 417 us (0.88)
  Pallas kernels: 303 us -> 275 us
  matrix products: 43.5 us -> 33.8 us
  local copies, waits for them, and re-layouts: 41.8 us -> 33.1 us
  other arithmetic: 27.9 us -> 23 us
    pallas_call x2 -> x1, Pallas kernels: 197 us -> 169 us  [attention_backward(): pl.pallas_call(backward_kernel, out_shape=(jax.ShapeDtypeStruct((rows, mo...]
    dot_general x2 -> x1, matrix products: 17.1 us -> 7.46 us  [dg(): lax.dot_general(left, right, (((left_dim,), (right_dim,)), ((), ())), pre...]
    dot_general x1 -> x0, local copies, waits for them, and re-layouts: 6.05 us -> none  [dg(): lax.dot_general(left, right, (((left_dim,), (right_dim,)), ((), ())), pre...]
    unnamed x43 -> x39, local copies, waits for them, and re-layouts: 19 us -> 18.3 us
  transfers between devices with their start and end apart: 3 -> 3, of which waited for: 1 -> 1; matrix products, arithmetic and copies ran while one was open for 5% -> 5% of each run, Pallas kernels for 23% -> 26%
where the time goes in v3:
time: 417 us; the launch traced here: 412 us
  Pallas kernels  275 us (66%)
  matrix products  33.8 us (8%)
  local copies, waits for them, and re-layouts  33.1 us (8%)
  waiting for transfers between devices  30.7 us (7%)
  other arithmetic  23 us (6%)
  between operations  15.9 us (4%)
    pallas_call x1, Pallas kernels, attention_backward(): pl.pallas_call(backward_kernel, out_shape=(jax.ShapeDtypeStruct((rows, mo...  169 us
    pallas_call x1, Pallas kernels, gather_rows(): pl.pallas_call(gather_kernel, out_shape=(jax.ShapeDtypeStruct((4 * rows,...  64.6 us
    pallas_call x1, Pallas kernels, attention_forward(): pl.pallas_call(forward_kernel, out_shape=(jax.ShapeDtypeStruct((width, sl...  41.4 us
    all_gather x1, waiting for transfers between devices, per_device(): line_w = lax.all_gather(own_slice, 'tensor', axis=0, tiled=False)  30.7 us
    unnamed x39, local copies, waits for them, and re-layouts  18.3 us
    dot_general x3, matrix products, contract_rows(): lax.dot_general(left, right, (((0,), (0,)), ((), ())), preferred_element_...  9.99 us
  transfers between devices with their start and end apart: 3, of which 1 were waited for; matrix products, arithmetic and copies ran while one was open for 5% of the time, Pallas kernels for 26%

profile of v3, /device:TPU:27, one launch (start us, length us, event | category | flops | bytes accessed | tf_op | source)
XLA Modules:
  0.0 412.3 jit_solution(8744607171665274955)
XLA Ops:
  7.3 1.1 copy-done
  8.3 1.0 dynamic-slice_bitcast_fusion
  9.3 0.8 pad_maximum_fusion.1
  10.1 30.7 %all-gather.5.cloned.1.call-done = bf16[12,40,1280]{2,1,0:T(8,128)(2,1)} async-done(((bf16[3,40,1280]{2,1,0:T(8,128)(2,1)}), bf16[12,40,1280]{2,1,0:T(8,128)(2,1)}) %all-gather.5.cloned.1.call-update) | async-done | bytes 1228816 | tf_op jit(solution)/shard_map/all_gather | solution.py:1007
  42.7 0.6 copy.59
  43.3 1.6 copy.58
  44.9 2.2 copy.57
  47.2 0.8 copy.63.factor
  48.5 3.6 pad_maximum_fusion
  52.2 1.4 fusion.5.own
  53.6 64.6 %gather_rows.1 = (bf16[2048,1280]{1,0:T(8,128)(2,1)}, bf16[8,160,960]{2,1,0:T(8,128)(2,1)}) custom-call(bf16[512,1280]{1,0:T(8,128)(2,1)} %fusion.5.own, bf16[8,160,960]{2,1,0:T(8,128)(2,1)} %bitcast.81), custom_call_target="tpu_custom_call" | custom-call | tf_op jit(solution)/shard_map/gather_rows/pallas_call | solution.py:220
  118.2 3.4 bitcast_select_fusion.weights
  121.8 7.5 %multiply_convert_fusion.qkv = bf16[960,2048]{1,0:T(8,128)(2,1)} fusion(bf16[1280,960]{1,0:T(8,128)(2,1)S(1)} %bitcast_select_fusion.weights, bf16[2048,1280]{1,0:T(8,128)(2,1)S(1)} %copy-done.9, f32[960]{0:T(1024)S(1)} %bitcast.98), kind=kOutput, calls=%fused_computation | convolution fusion | flops 5037096960 | bytes 11636480 | tf_op jit(solution)/shard_map/dot_general | solution.py:243
  129.3 41.4 %attention_forward.1 = (bf16[320,2048]{1,0:T(8,128)(2,1)S(1)}, f32[4,2048]{1,0:T(4,128)S(1)}, bf16[1280,512]{1,0:T(8,128)(2,1)S(1)}) custom-call(s32[2]{0:T(128)S(1)} %broadcast_select_fusion.span, bf16[960,2048]{1,0:T(8,128)(2,1)} %multiply_convert_fusion.qkv), custom_call_target="tpu_custom_call" | custom-call | tf_op jit(solution)/shard_map/attention_forward/pallas_call | solution.py:347
  170.7 1.0 copy-done.2
  171.8 0.6 copy-done.3
  172.4 4.8 %slice_bitcast_fusion.1 = (bf16[4,8,40,1280]{3,2,0,1:T(8,128)(2,1)S(1)}, bf16[4,8,40,1280]{3,2,0,1:T(8,128)(2,1)S(1)}, bf16[4,8,40,1280]{3,2,0,1:T(8,128)(2,1)S(1)}) fusion(bf16[8,4,3,40,1280]{4,3,2,1,0:T(8,128)(2,1)} %bitcast.82), kind=kLoop, calls=%fused_computation.14 | loop fusion | bytes 19660800 | tf_op jit(solution)/shard_map/transpose | solution.py:1011
  177.9 2.2 multiply_reduce_fusion.2
  180.1 1.9 fusion.22
  182.0 3.3 fusion.3
  185.3 2.3 fusion.4
  187.6 2.1 multiply_reduce_fusion.1
  189.7 3.9 fusion.23
  193.6 0.7 multiply_add_fusion
  194.4 3.2 convolution_convert_fusion.2.split
  197.5 3.6 convolution_convert_fusion.1
  201.2 3.9 convolution_convert_fusion
  205.0 0.7 maximum_maximum_fusion.small
  205.7 169.3 %attention_backward.1 = (bf16[512,1280]{1,0:T(8,128)(2,1)}, bf16[8,3,80,640]{3,2,1,0:T(8,128)(2,1)}, bf16[5,4,64,960]{3,2,1,0:T(8,128)(2,1)}, f32[8,1280]{1,0:T(8,128)}) custom-call(s32[2]{0:T(128)} %copy-done.4, bf16[960,2048]{1,0:T(8,128)(2,1)} %multiply_convert_fusion.qkv, bf16[320,2048]{1,0:T(8,128)(2,1)} %copy-done.2, f32[4,2048]{1,0:T(4,128)} %copy-done.3, ...), custom_call_target="tpu_custom_call" | custom-call | tf_op jit(solution)/shard_map/attention_backward/pallas_call | solution.py:898
  375.0 1.0 slice_reduce_fusion
  376.0 0.7 slice_reduce_fusion.2
  376.7 2.0 fusion.6
  378.7 3.6 fusion.9
  382.3 0.6 div.45
  382.9 0.6 div.46
  383.6 0.5 fusion.20
  384.2 2.4 bitcast_convert_fusion
  386.5 2.7 fusion.24
  389.2 2.7 copy.70
  392.0 2.7 copy.71
  394.7 1.7 copy.72
  396.4 2.1 convert.3
  398.9 0.8 copy.67
  399.7 1.3 copy.73
  401.0 0.8 copy.68
  401.9 1.3 copy.74
  403.1 0.8 copy.69
  404.0 1.3 copy.75
  (57 shorter events, 2.7 us)
Async XLA Ops:
  7.2 1.2 copy-start
  7.2 35.5 %copy-start.11 = (bf16[1280,320]{0,1:T(8,128)(2,1)S(1)}, bf16[1280,320]{0,1:T(8,128)(2,1)}, u32[]{:S(2)}) copy-start(bf16[1280,320]{0,1:T(8,128)(2,1)} %param.20) | copy-start | bytes 2457604
  7.2 33.6 %all-gather.5.cloned.1.call-start = ((), (), s32[]{:S(2)}) async-start(), calls=%async_computation | async-start | bytes 1536000 | tf_op jit(solution)/shard_map/all_gather | solution.py:1007
  10.1 162.3 %all-gather.7.cloned.1.call-start = ((), (), s32[]{:S(2)}) async-start(), calls=%async_computation.1 | async-start | bytes 11059200 | tf_op jit(solution)/shard_map/all_gather | solution.py:1008
  42.2 87.0 %collective-permute-start = (s32[2]{0:T(128)S(1)}, s32[2]{0:T(128)S(1)}, u32[]{:S(2)}, u32[]{:S(2)}) collective-permute-start(s32[2]{0:T(128)S(1)} %pad_add_fusion), channel_id=1, source_target_pairs={{0,4},{4,0},{8,12},{12,8},{16,20},{20,16},{24,28},{28,24},{1,5},{5... | collective-permute-start | bytes 32 | tf_op jit(solution)/shard_map/ppermute | solution.py:1016
  42.7 4.4 %copy-start.14 = (f32[80]{0:T(128)S(1)}, f32[80]{0:T(128)}, u32[]{:S(2)}) copy-start(f32[80]{0:T(128)} %param.17) | copy-start | bytes 964
  42.7 5.4 %copy-start.5 = (bf16[512,1280]{1,0:T(8,128)(2,1)S(1)}, bf16[512,1280]{1,0:T(8,128)(2,1)}, u32[]{:S(2)}) copy-start(bf16[512,1280]{1,0:T(8,128)(2,1)} %param.13) | copy-start | bytes 3932164
  48.5 3.7 copy-start.12
  118.2 3.6 copy-start.9
  121.6 7.6 %copy-start.6 = (bf16[1280,960]{1,0:T(8,128)(2,1)}, bf16[1280,960]{1,0:T(8,128)(2,1)S(1)}, u32[]{:S(2)}) copy-start(bf16[1280,960]{1,0:T(8,128)(2,1)S(1)} %bitcast_select_fusion.weights) | copy-start | bytes 7372804
  129.3 47.9 %copy-start.4 = (s32[2]{0:T(128)}, s32[2]{0:T(128)S(1)}, u32[]{:S(2)}) copy-start(s32[2]{0:T(128)S(1)} %broadcast_select_fusion.span) | copy-start | bytes 28
  170.7 1.1 copy-start.2
  171.8 0.6 copy-start.3
  177.9 2.2 copy-start.13
  182.0 3.3 copy-start.10
  194.4 3.2 copy-start.7
  375.0 3.7 copy-start.8
  403.1 2.1 copy-start.1
Sparse Core Ops, SparseCore 0:
  10.2 30.5 all-gather.4
  42.7 72.1 all-gather.6

commit v4 on v3

--- a/solution.py
+++ b/solution.py
@@ -88,157 +88,6 @@
     )
 
 
-def gather_kernel(
-    own, native, out, foreign, send_z, send_c, recv, local_sem, send_w, spread_w, recv_w
-):
-    here = Place()
-    rows = own.shape[0]
-    part = rows // CHUNKS
-    pair_barrier(here, plane=True)
-    partner = here.partner()
-    members = native.shape[0]
-    line = lax.rem(here.t + 2, 4)
-    weight_copy = remote(
-        native.at[here.d],
-        foreign.at[here.d],
-        send_w,
-        recv_w.at[here.d],
-        (here.base + 1 - line // 2, line),
-    )
-    weight_copy.start()
-
-    def weight_arrived(member):
-        remote(native.at[0], foreign.at[member], send_w, recv_w.at[member], partner).wait_recv()
-
-    def spread(core, step):
-        member = here.base + core
-        return remote(
-            foreign.at[member],
-            foreign.at[member],
-            spread_w.at[core, step],
-            recv_w.at[member],
-            here.across(step),
-        )
-
-    def place(seq, k, ch):
-        block = jnp.where(seq == 0, k, 3 - k)
-        return out.at[pl.ds(pl.multiple_of(block * rows + ch * part, part), part)]
-
-    def own_part(ch):
-        return own.at[pl.ds(ch * part, part)]
-
-    def copy(src, k, ch, seq, device, send):
-        return remote(src, place(seq, k, ch), send.at[k, ch], recv.at[k, ch], device)
-
-    def arrived(k, ch, seq):
-        copy(place(seq, k, ch), k, ch, seq, partner, send_z).wait_recv()
-
-    for k in (2, 3):
-        @pl.when(here.pos == k)
-        def _(k=k):
-            target = here.device(here.c, 1)
-            for ch in range(CHUNKS):
-                copy(own_part(ch), k, ch, here.c, target, send_z).start()
-            for core in range(2):
-                weight_arrived(here.base + core)
-                for step in range(1, here.pairs):
-                    spread(core, step).start()
-            for step in range(1, here.pairs):
-                for core in range(2):
-                    weight_arrived(2 * lax.rem(here.pair + step, here.pairs) + core)
-            for ch in range(CHUNKS):
-                for kk in range(4):
-                    arrived(kk, ch, 1 - here.c)
-            for ch in range(CHUNKS):
-                copy(own_part(ch), k, ch, here.c, target, send_z).wait_send()
-            for core in range(2):
-                for step in range(1, here.pairs):
-                    spread(core, step).wait_send()
-
-    def keep(k):
-        return pltpu.make_async_copy(
-            own, out.at[pl.ds(pl.multiple_of(jnp.where(here.c == 0, k, 3 - k) * rows, rows), rows)], local_sem
-        )
-
-    @pl.when(here.pos == 1)
-    def _():
-        seq = here.c
-        near = here.device(seq, 0)
-        sent = []
-
-        def send(src, k, ch, device, sem):
-            copy(src, k, ch, seq, device, sem).start()
-            sent.append((src, k, ch, device, sem))
-
-        keep(1).start()
-        for ch in range(CHUNKS):
-            send(own_part(ch), 1, ch, near, send_z)
-            send(own_part(ch), 1, ch, partner, send_c)
-        for ch in range(CHUNKS):
-            for k in (2, 3):
-                arrived(k, ch, seq)
-                send(place(seq, k, ch), k, ch, near, send_z)
-                send(place(seq, k, ch), k, ch, partner, send_c)
-            arrived(0, ch, seq)
-            send(place(seq, 0, ch), 0, ch, partner, send_c)
-        for src, k, ch, device, sem in sent:
-            copy(src, k, ch, seq, device, sem).wait_send()
-        keep(1).wait()
-
-    @pl.when(here.pos == 0)
-    def _():
-        seq = here.c
-        far = here.device(seq, 1)
-        sent = []
-
-        def send(src, k, ch, device, sem):
-            copy(src, k, ch, seq, device, sem).start()
-            sent.append((src, k, ch, device, sem))
-
-        keep(0).start()
-        for ch in range(CHUNKS):
-            send(own_part(ch), 0, ch, far, send_z)
-            send(own_part(ch), 0, ch, partner, send_c)
-        for ch in range(CHUNKS):
-            arrived(1, ch, seq)
-            send(place(seq, 1, ch), 1, ch, partner, send_c)
-        for ch in range(CHUNKS):
-            for k in (2, 3):
-                arrived(k, ch, seq)
-                send(place(seq, k, ch), k, ch, partner, send_c)
-        for src, k, ch, device, sem in sent:
-            copy(src, k, ch, seq, device, sem).wait_send()
-        keep(0).wait()
-
-    weight_copy.wait_send()
-
-
-def gather_rows(own, native):
-    rows, width = own.shape
-    members = native.shape[0]
-    hbm = pl.BlockSpec(memory_space=pl.ANY)
-    return pl.pallas_call(
-        gather_kernel,
-        out_shape=(
-            jax.ShapeDtypeStruct((4 * rows, width), own.dtype),
-            jax.ShapeDtypeStruct(native.shape, native.dtype),
-        ),
-        in_specs=[hbm, hbm],
-        out_specs=(hbm, hbm),
-        scratch_shapes=[
-            pltpu.SemaphoreType.DMA((4, CHUNKS)),
-            pltpu.SemaphoreType.DMA((4, CHUNKS)),
-            pltpu.SemaphoreType.DMA((4, CHUNKS)),
-            pltpu.SemaphoreType.DMA,
-            pltpu.SemaphoreType.DMA,
-            pltpu.SemaphoreType.DMA((2, members // 2)),
-            pltpu.SemaphoreType.DMA((members,)),
-        ],
-        compiler_params=pltpu.CompilerParams(collective_id=0, has_side_effects=True),
-        name="gather_rows",
-    )(own, native)
-
-
 def dg(left, right, left_dim, right_dim):
     return lax.dot_general(
         left, right, (((left_dim,), (right_dim,)), ((), ())), preferred_element_type=jnp.float32
@@ -262,34 +111,242 @@
     return jnp.where((key >= span[1]) & (key < span[1] + span[0]), 0.0, MASKED)
 
 
-def forward_kernel(span, qkv, out, logsum, rows_out, highest, summed, total, send, recv, local_sem):
+def forward_kernel(
+    span, own, native, factor, mlp_native,
+    gathered, weights, qkv, out, logsum, rows_out, mlp_all,
+    highest, summed, total,
+    keep_sem, send_z, send_c, recv,
+    native_sem, weight_sent, spread_sent, weight_got,
+    rows_sent, rows_got, rows_local,
+    mlp_local, line_sent, line_got, plane_sent, share_sent, mlp_have,
+):
     heads = logsum.shape[0]
     width, slots = out.shape
     dim = width // heads
+    low, f32 = qkv.dtype, jnp.float32
     here = Place()
-    pair_barrier(here)
+    pairs = here.pairs
+    split = mlp_native.shape[1]
+    rows = own.shape[0]
+    part = rows // CHUNKS
+    columns = own.shape[1] // 2
+    tall = native.shape[0] // split
+    blocks = slots // TILE
+    partner = here.partner()
+    pair_barrier(here, plane=True)
+
+    def half(core):
+        return pl.ds(pl.multiple_of(core * columns, columns), columns)
+
+    def weight_piece(ref, pair, core):
+        return ref.at[pl.ds(pl.multiple_of(pair * tall, tall), tall), half(core)]
+
+    line = lax.rem(here.t + 2, 4)
+    weight_copy = remote(
+        weight_piece(native, here.pair, here.c),
+        weight_piece(weights, here.pair, here.c),
+        weight_sent,
+        weight_got.at[here.pair, here.c],
+        (here.base + 1 - line // 2, line),
+    )
+    sends = here.pair < split
+
+    @pl.when(sends)
+    def _():
+        weight_copy.start()
+
+    native_copy = pltpu.make_async_copy(native, weights, native_sem)
+
+    @pl.when(here.main)
+    def _():
+        native_copy.start()
+
+    def place(seq, k, ch):
+        block = jnp.where(seq == 0, k, 3 - k)
+        return gathered.at[pl.ds(pl.multiple_of(block * rows + ch * part, part), part)]
+
+    def copy(src, k, ch, seq, device, send):
+        return remote(src, place(seq, k, ch), send.at[k, ch], recv.at[k, ch], device)
+
+    def own_copy(k, ch, device, send):
+        return copy(own.at[pl.ds(ch * part, part)], k, ch, here.c, device, send)
+
+    def pass_copy(k, ch, device, send):
+        return copy(place(here.g, k, ch), k, ch, here.g, device, send)
+
+    def arrived(k, ch):
+        pass_copy(k, ch, partner, send_z).wait_recv()
+
+    keep = pltpu.make_async_copy(
+        own, gathered.at[pl.ds(pl.multiple_of(here.t * rows, rows), rows)], keep_sem
+    )
+    near = here.device(here.c, jnp.where(here.pos == 1, 0, 1))
+
+    @pl.when(here.main)
+    def _():
+        keep.start()
+        for ch in range(CHUNKS):
+            own_copy(here.pos, ch, near, send_z).start()
+            own_copy(here.pos, ch, partner, send_c).start()
+
+    @pl.when(jnp.logical_not(here.main))
+    def _():
+        for ch in range(CHUNKS):
+            own_copy(here.pos, ch, near, send_z).start()
+
+    def mlp_piece(quarter, pair, core):
+        return mlp_all.at[:, quarter, pair, :, half(core)]
+
+    def mlp_line(step):
+        return remote(
+            mlp_native.at[:, here.pair, :, half(here.c)],
+            mlp_piece(here.t, here.pair, here.c),
+            line_sent.at[step - 1],
+            line_got.at[here.t],
+            (here.d, lax.rem(here.t + step, 4)),
+        )
+
+    def mlp_plane(n, step):
+        quarter = lax.rem(here.t + n, 4)
+        piece = mlp_piece(quarter, here.pair, here.c)
+        return remote(
+            piece, piece, plane_sent.at[n - 1, step], mlp_have.at[quarter, here.pair, here.c], here.across(step)
+        )
+
+    def mlp_core(n, pair):
+        quarter = lax.rem(here.t + n, 4)
+        piece = mlp_piece(quarter, pair, here.c)
+        return remote(
+            piece, piece, share_sent.at[n - 1, pair], mlp_have.at[quarter, pair, here.c], partner
+        )
+
+    def mlp_arrived(n, pair, core):
+        quarter = lax.rem(here.t + n, 4)
+        piece = mlp_piece(quarter, pair, core)
+        remote(piece, piece, share_sent.at[0, 0], mlp_have.at[quarter, pair, core], partner).wait_recv()
+
+    mlp_keep = pltpu.make_async_copy(mlp_native, mlp_all.at[:, here.t], mlp_local)
+
+    @pl.when(sends)
+    def _():
+        for step in range(1, 4):
+            mlp_line(step).start()
+
+    mlp_keep.start()
+
+    def from_line():
+        @pl.when(sends)
+        def _():
+            for n in (1, 3, 2):
+                quarter = lax.rem(here.t + n, 4)
+                piece = mlp_piece(quarter, here.pair, here.c)
+                remote(piece, piece, share_sent.at[0, 0], line_got.at[quarter], partner).wait_recv()
+                for step in range(1, pairs):
+                    mlp_plane(n, step).start()
+                mlp_core(n, here.pair).start()
+
+    def spread(core, step):
+        piece = weight_piece(weights, here.pair, core)
+        return remote(
+            piece, piece, spread_sent.at[core, step - 1], weight_got.at[here.pair, core], here.across(step)
+        )
+
+    def weight_arrived(pair, core):
+        piece = weight_piece(weights, pair, core)
+        remote(piece, piece, weight_sent, weight_got.at[pair, core], partner).wait_recv()
+
+    @pl.when(jnp.logical_not(here.main))
+    def _():
+        @pl.when(sends)
+        def _():
+            for core in range(2):
+                weight_arrived(here.pair, core)
+                for step in range(1, pairs):
+                    spread(core, step).start()
+
+        for pair in range(split):
+            @pl.when(here.pair != pair)
+            def _(pair=pair):
+                for core in range(2):
+                    weight_arrived(pair, core)
+
+    @pl.when(here.main)
+    def _():
+        native_copy.wait()
+        keep.wait()
+
+    @pl.when(here.pos == 1)
+    def _():
+        for ch in range(CHUNKS):
+            arrived(2, ch)
+            pass_copy(2, ch, near, send_z).start()
+            pass_copy(2, ch, partner, send_c).start()
+            arrived(0, ch)
+            pass_copy(0, ch, partner, send_c).start()
+        for ch in range(CHUNKS):
+            arrived(3, ch)
+            pass_copy(3, ch, near, send_z).start()
+            pass_copy(3, ch, partner, send_c).start()
+
     quarter = here.quarter()
 
     def into(q):
         return rows_out.at[pl.ds(pl.multiple_of(q * width, width), width)]
 
-    def columns(i):
+    def done_columns(i):
         return out.at[:, pl.ds(pl.multiple_of(i * TILE, TILE), TILE)]
 
-    def copy(i):
-        return remote(columns(i), into(quarter), send.at[i], recv.at[quarter], (here.base + here.g, i))
-
-    keep = pltpu.make_async_copy(columns(here.t), into(here.t), local_sem)
-
-    @pl.loop(0, slots // TILE)
+    def rows_copy(i):
+        return remote(
+            done_columns(i), into(quarter), rows_sent.at[i], rows_got.at[quarter], (here.base + here.g, i)
+        )
+
+    rows_keep = pltpu.make_async_copy(done_columns(here.t), into(here.t), rows_local)
+
+    def finish(i):
+        qs = pl.ds(pl.multiple_of(i * TILE, TILE), TILE)
+        for h in range(heads):
+            hs = pl.ds(h * dim, dim)
+            sums = summed[h : h + 1, qs]
+            out[hs, qs] = (total[hs, qs] / sums).astype(out.dtype)
+            logsum[h : h + 1, qs] = highest[h : h + 1, qs] + jnp.log(sums)
+        stays = here.main & (here.t == i)
+
+        @pl.when(stays)
+        def _():
+            rows_keep.start()
+
+        @pl.when(jnp.logical_not(stays))
+        def _():
+            rows_copy(i).start()
+
+    highest[...] = jnp.full_like(highest, MASKED)
+    summed[...] = jnp.zeros_like(summed)
+    total[...] = jnp.zeros_like(total)
+
+    @pl.loop(0, blocks)
     def _(s):
-        i = slots // TILE - 1 - s
-        qs = pl.ds(pl.multiple_of(i * TILE, TILE), TILE)
-        highest[...] = jnp.full_like(highest, MASKED)
-        summed[...] = jnp.zeros_like(summed)
-        total[...] = jnp.zeros_like(total)
-
-        def tile(j, diagonal):
+        b = jnp.where(here.g == 0, s, blocks - 1 - s)
+        last = (here.g == 1) & (s == blocks - 1)
+
+        @pl.when((here.pos == 0) & (s >= 1))
+        def _():
+            for ch in range(CHUNKS):
+                arrived(s, ch)
+                pass_copy(s, ch, partner, send_c).start()
+
+        @pl.when(jnp.logical_not(here.main))
+        def _():
+            for ch in range(CHUNKS):
+                arrived(s, ch)
+
+        bs = pl.ds(pl.multiple_of(b * TILE, TILE), TILE)
+        for w in range(3):
+            at = pl.ds(w * width, width)
+            qkv[at, bs] = (dg(weights[at], gathered[bs], 1, 1) * factor[at]).astype(low)
+
+        def tile(i, j, diagonal):
+            qs = pl.ds(pl.multiple_of(i * TILE, TILE), TILE)
             ks = pl.ds(pl.multiple_of(j * TILE, TILE), TILE)
             if diagonal:
                 allowed = readable(span, j * TILE, i * TILE)
@@ -299,73 +356,153 @@
                 hs = pl.ds(h * dim, dim)
                 scores = dg(qkv[pl.ds(width + h * dim, dim), ks], qkv[hs, qs], 0, 0)
                 scores = jnp.where(allowed, scores, MASKED) if diagonal else scores + bias
-                before = highest[h : h + 1]
+                before = highest[h : h + 1, qs]
                 after = jnp.maximum(before, jnp.max(scores, axis=0, keepdims=True))
                 expo = jnp.exp(scores - after)
                 scale = jnp.exp(before - after)
-                summed[h : h + 1] = summed[h : h + 1] * scale + jnp.sum(expo, axis=0, keepdims=True)
-                highest[h : h + 1] = after
-                total[hs] = total[hs] * scale + dg(
-                    qkv[pl.ds(2 * width + h * dim, dim), ks], expo.astype(qkv.dtype), 1, 0
+                summed[h : h + 1, qs] = summed[h : h + 1, qs] * scale + jnp.sum(expo, axis=0, keepdims=True)
+                highest[h : h + 1, qs] = after
+                total[hs, qs] = total[hs, qs] * scale + dg(
+                    qkv[pl.ds(2 * width + h * dim, dim), ks], expo.astype(low), 1, 0
                 )
 
-        @pl.loop(0, i)
-        def _(j):
-            tile(j, False)
-
-        tile(i, True)
-        for h in range(heads):
-            hs = pl.ds(h * dim, dim)
-            out[hs, qs] = (total[hs] / summed[h : h + 1]).astype(out.dtype)
-            logsum[h : h + 1, qs] = highest[h : h + 1] + jnp.log(summed[h : h + 1])
-        stays = here.main & (here.t == i)
-
-        @pl.when(stays)
-        def _():
-            keep.start()
-
-        @pl.when(jnp.logical_not(stays))
-        def _():
-            copy(i).start()
+        tile(b, b, True)
+
+        @pl.when(last)
+        def _():
+            finish(b)
+
+        @pl.loop(0, s)
+        def _(n):
+            i = jnp.where(here.g == 0, b, b + 1 + n)
+            tile(i, jnp.where(here.g == 0, n, b), False)
+
+            @pl.when(last)
+            def _():
+                finish(i)
+
+        @pl.when(here.g == 0)
+        def _():
+            finish(b)
+
+        @pl.when(s == 2)
+        def _():
+            from_line()
+
+    for n in (1, 3, 2):
+        for pair in range(split):
+            @pl.when(here.pair != pair)
+            def _(n=n, pair=pair):
+                mlp_arrived(n, pair, here.c)
+                mlp_core(n, pair).start()
 
     for block in range(4):
         stays = here.main & (here.t == block)
 
         @pl.when(stays)
         def _():
-            keep.wait()
+            rows_keep.wait()
 
         @pl.when(jnp.logical_not(stays))
         def _(block=block):
-            copy(block).wait_send()
-            remote(columns(0), into(block), send.at[0], recv.at[block], here.partner()).wait_recv()
-
-
-def attention_forward(span, qkv, heads):
-    width, slots = qkv.shape[0] // 3, qkv.shape[1]
+            rows_copy(block).wait_send()
+            remote(
+                done_columns(0), into(block), rows_sent.at[0], rows_got.at[block], partner
+            ).wait_recv()
+
+    for n in range(1, 4):
+        for pair in range(split):
+            mlp_arrived(n, pair, 1 - here.c)
+            mlp_core(n, pair).wait_send()
+    mlp_keep.wait()
+
+    @pl.when(sends)
+    def _():
+        weight_copy.wait_send()
+        for step in range(1, 4):
+            mlp_line(step).wait_send()
+            for across in range(1, pairs):
+                mlp_plane(step, across).wait_send()
+
+    @pl.when(sends & jnp.logical_not(here.main))
+    def _():
+        for core in range(2):
+            for step in range(1, pairs):
+                spread(core, step).wait_send()
+
+    for ch in range(CHUNKS):
+        own_copy(here.pos, ch, near, send_z).wait_send()
+
+    @pl.when(here.main)
+    def _():
+        for ch in range(CHUNKS):
+            own_copy(here.pos, ch, partner, send_c).wait_send()
+
+    @pl.when(here.pos == 0)
+    def _():
+        for k in (1, 2, 3):
+            for ch in range(CHUNKS):
+                pass_copy(k, ch, partner, send_c).wait_send()
+
+    @pl.when(here.pos == 1)
+    def _():
+        for ch in range(CHUNKS):
+            pass_copy(0, ch, partner, send_c).wait_send()
+            for k in (2, 3):
+                pass_copy(k, ch, near, send_z).wait_send()
+                pass_copy(k, ch, partner, send_c).wait_send()
+
+
+def attention_forward(span, own, native, factor, mlp_native, heads):
+    rows, model = own.shape
+    slots = 4 * rows
+    width = native.shape[0] // 3
+    _, split, tall, _ = mlp_native.shape
+    pairs = lax.axis_size("dp") // 2
+    low, f32 = own.dtype, jnp.float32
     vmem = pl.BlockSpec(memory_space=pltpu.VMEM)
+    hbm = pl.BlockSpec(memory_space=pl.ANY)
+    dma = pltpu.SemaphoreType.DMA
     return pl.pallas_call(
         forward_kernel,
         out_shape=(
-            jax.ShapeDtypeStruct((width, slots), qkv.dtype),
-            jax.ShapeDtypeStruct((heads, slots), jnp.float32),
-            jax.ShapeDtypeStruct((4 * width, slots // 4), qkv.dtype),
+            jax.ShapeDtypeStruct((slots, model), low),
+            jax.ShapeDtypeStruct(native.shape, low),
+            jax.ShapeDtypeStruct((3 * width, slots), low),
+            jax.ShapeDtypeStruct((width, slots), low),
+            jax.ShapeDtypeStruct((heads, slots), f32),
+            jax.ShapeDtypeStruct((4 * width, rows), low),
+            jax.ShapeDtypeStruct((3, 4, split, tall, model), low),
         ),
-        in_specs=[pl.BlockSpec(memory_space=pltpu.SMEM), vmem],
-        out_specs=(vmem, vmem, pl.BlockSpec(memory_space=pl.ANY)),
+        in_specs=[pl.BlockSpec(memory_space=pltpu.SMEM), hbm, hbm, vmem, hbm],
+        out_specs=(vmem,) * 5 + (hbm, hbm),
         scratch_shapes=[
-            pltpu.VMEM((heads, TILE), jnp.float32),
-            pltpu.VMEM((heads, TILE), jnp.float32),
-            pltpu.VMEM((width, TILE), jnp.float32),
-            pltpu.SemaphoreType.DMA((4,)),
-            pltpu.SemaphoreType.DMA((4,)),
-            pltpu.SemaphoreType.DMA,
+            pltpu.VMEM((heads, slots), f32),
+            pltpu.VMEM((heads, slots), f32),
+            pltpu.VMEM((width, slots), f32),
+            dma,
+            dma((4, CHUNKS)),
+            dma((4, CHUNKS)),
+            dma((4, CHUNKS)),
+            dma,
+            dma,
+            dma((2, pairs - 1)),
+            dma((split, 2)),
+            dma((4,)),
+            dma((4,)),
+            dma,
+            dma,
+            dma((3,)),
+            dma((4,)),
+            dma((3, pairs)),
+            dma((3, split)),
+            dma((4, split, 2)),
         ],
         compiler_params=pltpu.CompilerParams(
             collective_id=1, has_side_effects=True, vmem_limit_bytes=50 * 1024 * 1024
         ),
         name="attention_forward",
-    )(span, qkv)
+    )(span, own, native, factor, mlp_native)
 
 
 def backward_kernel(
@@ -574,7 +711,7 @@
         result[pl.ds(0, width), bs] = (query_sum[:, bs] * factor[...]).astype(low)
         result[pl.ds(width, width), bs] = key_sum[:, bs].astype(low)
         result[pl.ds(2 * width, width), bs] = value_sum[:, bs].astype(low)
-        partial[bs] = dg(result[:, bs], weights[...], 0, 1).astype(low)
+        partial[bs] = dg(result[:, bs], weights[...], 0, 0).astype(low)
 
         @pl.when(jnp.logical_not(here.main))
         def _():
@@ -633,7 +770,7 @@
             weight_grad[i, p] = grads[p * share : (p + 1) * share].astype(low)
         for step in range(1, pairs):
             qkv_send(i, step).start()
-        weighted = grads * weights[at].astype(f32)
+        weighted = grads * jnp.transpose(weights[:, at]).astype(f32)
         by_row = jnp.sum(weighted, axis=1, keepdims=True)
         small_own[0:1, at] = jnp.transpose(jnp.broadcast_to(by_row, (depth, 128)))[0:1]
         small_own[2:3, pl.ds(0, 3 * width)] += jnp.sum(weighted, axis=0, keepdims=True)
@@ -886,7 +1023,7 @@
 ):
     width, slots = out.shape
     heads = logsum.shape[0]
-    rows, model = split.shape[1], weights.shape[0]
+    rows, model = split.shape[1], weights.shape[1]
     low, f32 = qkv.dtype, jnp.float32
     pairs, slice_rows = grad_out.shape[1], grad_out.shape[2]
     columns = model // 2
@@ -996,22 +1133,12 @@
     pairs = n_dp // 2
     swap_core = [(i, i ^ 1) for i in range(n_dp)]
 
-    slice_rows = w_out.shape[0] // n_dp
-    own_slice = jnp.stack(
-        [
-            lax.dynamic_slice_in_dim(w_out, here.d * slice_rows, slice_rows, 0),
-            jnp.transpose(lax.dynamic_slice_in_dim(w_up, here.d * slice_rows, slice_rows, 1)),
-            lax.dynamic_slice_in_dim(w_down, here.d * slice_rows, slice_rows, 0),
-        ]
-    )
-    line_w = lax.all_gather(own_slice, "tensor", axis=0, tiled=False)
-    mlp_w = lax.all_gather(line_w, "dp", axis=0, tiled=False)
-
-    def whole_weight(w):
-        return jnp.transpose(mlp_w[:, :, w], (1, 0, 2, 3)).reshape(model, model)
-
-    w_out_all, w_up_all, w_down_all = whole_weight(0), whole_weight(1), whole_weight(2)
-
+    split = min(pairs, 4)
+    mlp_native = jnp.stack([w_out, jnp.transpose(w_up), w_down])
+    mlp_native = mlp_native.reshape(3, split, width_local // split, model)
+    native = jnp.concatenate(
+        [jnp.transpose(w_query), jnp.transpose(w_key), jnp.transpose(w_value)]
+    )
     own_span = jnp.concatenate([lengths, offsets])
     other_span = lax.ppermute(own_span, "dp", swap_core)
     group_span = jnp.where(here.main, own_span, other_span)
@@ -1020,18 +1147,19 @@
 
     residual = inputs.astype(f32)
     normed, inverse_one = rms_forward(residual, gain_attn)
-    native_w = jnp.concatenate([w_query, w_key, w_value], axis=1)
-    gathered, foreign_w = gather_rows(
-        normed.astype(low), native_w.reshape(n_dp, model // n_dp, 3 * width_local)
-    )
-    stacked_w = jnp.where(here.main, native_w, foreign_w.reshape(model, 3 * width_local))
-
     scale_const = LOG_TWO_E / math.sqrt(head_dim)
     soft = jax.nn.softplus(query_scale)
     factor = jnp.tile(soft * scale_const, heads_local)[:, None]
-    projected = dg(stacked_w, gathered, 0, 1)
-    qkv = (projected * jnp.concatenate([factor, jnp.ones((2 * width_local, 1), f32)])).astype(low)
-    attended, logsum, attended_rows = attention_forward(group_span, qkv, heads_local)
+    gathered, stacked_w, qkv, attended, logsum, attended_rows, mlp_w = attention_forward(
+        group_span,
+        normed.astype(low),
+        native,
+        jnp.concatenate([factor, jnp.ones((2 * width_local, 1), f32)]),
+        mlp_native,
+        heads_local,
+    )
+    mlp_w = mlp_w.reshape(3, model, model)
+    w_out_all, w_up_all, w_down_all = mlp_w[0], mlp_w[1], mlp_w[2]
 
     hidden_one = residual + contract_rows(attended_rows, w_out_all)
     second, inverse_two = rms_forward(hidden_one, gain_mlp)

time: 417 us -> 374 us (0.90)
  waiting for transfers between devices: 30.7 us -> 0.01 us
  Pallas kernels: 275 us -> 291 us
  between operations: 15.9 us -> 2.59 us
  local copies, waits for them, and re-layouts: 33.1 us -> 24.5 us
  matrix products: 33.8 us -> 26.3 us
    all_gather x2 -> x0, waiting for transfers between devices: 30.7 us -> none  [the longest x1 30.7 us: per_device(): line_w = lax.all_gather(own_slice, 'tensor', axis=0, tiled=False)]
    pallas_call x2 -> x1, Pallas kernels: 106 us -> 132 us  [attention_forward(): pl.pallas_call(forward_kernel, out_shape=(jax.ShapeDtypeStruct((slots, mo...]
    pallas_call x1, Pallas kernels: 169 us -> 159 us  [attention_backward(): pl.pallas_call(backward_kernel, out_shape=(jax.ShapeDtypeStruct((rows, mo...]
    dot_general x1 -> x0, matrix products: 7.46 us -> none  [dg(): lax.dot_general(left, right, (((left_dim,), (right_dim,)), ((), ())), pre...]
    unnamed x39 -> x40, local copies, waits for them, and re-layouts: 18.3 us -> 11.9 us
    transpose x4 -> x0, local copies, waits for them, and re-layouts: 5.43 us -> none  [whole_weight(): return jnp.transpose(mlp_w[:, :, w], (1, 0, 2, 3)).reshape(model, model)]
    slice x0 -> x1, local copies, waits for them, and re-layouts: none -> 4.92 us  [per_device(): w_out_all, w_up_all, w_down_all = (mlp_w[0], mlp_w[1], mlp_w[2])]
  transfers between devices with their start and end apart: 3 -> 1, of which waited for: 1 -> 0; matrix products, arithmetic and copies ran while one was open for 5% -> 2% of each run, Pallas kernels for 26% -> 0%
where the time goes in v4:
time: 374 us; the launch traced here: 367 us
  Pallas kernels  291 us (78%)
  matrix products  26.3 us (7%)
  local copies, waits for them, and re-layouts  24.5 us (7%)
  other arithmetic  21.7 us (6%)
    pallas_call x1, Pallas kernels, attention_backward(): pl.pallas_call(backward_kernel, out_shape=(jax.ShapeDtypeStruct((rows, mo...  159 us
    pallas_call x1, Pallas kernels, attention_forward(): pl.pallas_call(forward_kernel, out_shape=(jax.ShapeDtypeStruct((slots, mo...  132 us
    unnamed x40, local copies, waits for them, and re-layouts  11.9 us
    dot_general x3, matrix products, contract_rows(): lax.dot_general(left, right, (((0,), (0,)), ((), ())), preferred_element_...  9.73 us
    dot_general x3, matrix products, contract_cols(): lax.dot_general(left, right, (((1,), (1,)), ((), ())), preferred_element_...  7.62 us
  transfers between devices with their start and end apart: 1, of which 0 were waited for; matrix products, arithmetic and copies ran while one was open for 2% of the time, Pallas kernels for 0%

profile of v4, /device:TPU:27, one launch (start us, length us, event | category | flops | bytes accessed | tf_op | source)
XLA Modules:
  0.0 366.5 jit_solution(10996456353109310066)
XLA Ops:
  2.1 0.1 pad_add_fusion
  2.2 0.7 collective-permute-start
  2.9 1.6 fusion.10
  4.5 0.7 broadcast_multiply_fusion.2
  5.2 0.2 broadcast_in_dim_tile.4.factor
  5.4 0.0 copy-start.6
  5.4 0.1 pad.3.clone
  5.5 2.7 fusion.5.own
  8.3 1.6 pad_maximum_fusion.native
  9.9 0.4 copy-done.12
  10.3 0.5 copy-done.13
  10.8 1.7 pad_maximum_fusion.1.mlp_native
  12.5 0.1 broadcast_select_fusion.span
  12.5 131.9 %attention_forward.1 = (bf16[2048,1280]{1,0:T(8,128)(2,1)}, bf16[960,1280]{1,0:T(8,128)(2,1)}, bf16[960,2048]{1,0:T(8,128)(2,1)}, bf16[320,2048]{1,0:T(8,128)(2,...) custom-call(s32[2]{0:T(128)S(1)} %broadcast_select_fusion.span, ...), custom_call_target="tpu_custom_call" | custom-call | tf_op jit(solution)/shard_map/attention_forward/pallas_call | solution.py:466
  144.5 4.9 %fusion.23 = (bf16[1,4,4,80,1280]{4,3,2,1,0:T(8,128)(2,1)S(1)}, bf16[1,4,4,80,1280]{4,3,2,1,0:T(8,128)(2,1)S(1)}, bf16[1,4,4,80,1280]{4,3,2,1,0:T(8,128)(2,1)S(1)}) fusion(bf16[3,4,4,80,1280]{4,3,2,1,0:T(8,128)(2,1)} %get-tuple-element.23), kind=kLoop, calls=%fused_computation.59 | loop fusion | bytes 19660800 | tf_op jit(solution)/shard_map/slice | solution.py:1162
  149.5 2.1 multiply_reduce_fusion.2
  151.6 1.9 fusion.22
  153.5 3.3 fusion.3
  156.8 2.3 fusion.4
  159.2 2.1 multiply_reduce_fusion.1
  161.3 3.8 %fusion.24 = (bf16[1280,1280]{1,0:T(8,128)(2,1)}, f32[1280]{0:T(1024)S(1)}) fusion(bf16[1,4,4,80,1280]{4,3,2,1,0:T(8,128)(2,1)S(1)} %get-tuple-element.35, bf16[512,1280]{1,0:T(8,128)(2,1)S(1)} %fusion.4, f32[512,1280]{1,0:T(8,128)S(1)} %get-tuple-element.47, f32[1280]{0:T(1024)S(1)} %copy-done.15, f32[512]{0:T(512)S(1)} %add_rsqrt_fusion), kind=kOutput, calls=%fused_computation.60 | convolution fusion | flops 1686240000 | bytes 10498048 | tf_op jit(solution)/shard_map/dot_general | solution.py:31
  165.1 0.8 multiply_add_fusion
  165.8 3.4 convolution_convert_fusion.2.split
  169.2 3.6 convolution_convert_fusion.1
  172.8 3.9 %convolution_convert_fusion = bf16[1280,1280]{1,0:T(8,128)(2,1)} fusion(bf16[512,1280]{1,0:T(8,128)(2,1)S(1)} %copy-done.7, f32[512]{0:T(512)S(1)} %fusion.19, f32[512,1280]{1,0:T(8,128)S(1)} %fusion.22), kind=kOutput, calls=%fused_computation | convolution fusion | flops 1684602880 | bytes 7211008 | tf_op jit(solution)/shard_map/dot_general | solution.py:31
  176.7 0.7 maximum_maximum_fusion.small
  177.4 158.8 %attention_backward.1 = (bf16[512,1280]{1,0:T(8,128)(2,1)}, bf16[8,3,80,640]{3,2,1,0:T(8,128)(2,1)}, bf16[5,4,64,960]{3,2,1,0:T(8,128)(2,1)}, f32[8,1280]{1,0:T(8,128)}) custom-call(s32[2]{0:T(128)} %copy-done.2, bf16[960,2048]{1,0:T(8,128)(2,1)} %get-tuple-element.24.qkv, bf16[320,2048]{1,0:T(8,128)(2,1)} %copy-done, f32[4,2048]{1,0:T(4,128)} %copy-done.1, ...), custom_call_target="tpu_custom_call" | custom-call | tf_op jit(solution)/shard_map/attention_backward/pallas_call | solution.py:1035
  336.2 1.0 slice_reduce_fusion
  337.1 0.7 slice_reduce_fusion.2
  337.9 1.9 fusion.6
  339.9 3.5 fusion.9
  343.4 0.6 div.45
  344.0 0.6 div.46
  344.6 0.1 reshape_squeeze.3
  344.7 0.5 fusion.20
  345.2 2.4 bitcast_convert_fusion
  347.6 2.7 fusion.25
  350.3 2.7 copy.38
  353.0 2.7 copy.39
  355.8 1.7 copy.40
  357.5 2.1 convert.3
  359.5 0.4 slice_bitcast_fusion
  360.0 0.8 copy.35
  360.8 1.3 copy.41
  362.1 0.8 copy.36
  362.9 1.3 copy.42
  364.2 0.8 copy.37
  365.1 1.3 copy.43
  (43 shorter events, 0.2 us)
Async XLA Ops:
  0.6 7.6 %copy-start.8 = (bf16[1280,320]{0,1:T(8,128)(2,1)S(1)}, bf16[1280,320]{0,1:T(8,128)(2,1)}, u32[]{:S(2)}) copy-start(bf16[1280,320]{0,1:T(8,128)(2,1)} %param.20) | copy-start | bytes 2457604
  0.7 7.6 %copy-start.9 = (bf16[1280,320]{0,1:T(8,128)(2,1)S(1)}, bf16[1280,320]{0,1:T(8,128)(2,1)}, u32[]{:S(2)}) copy-start(bf16[1280,320]{0,1:T(8,128)(2,1)} %param.19) | copy-start | bytes 2457604
  0.7 7.6 %copy-start.10 = (bf16[1280,320]{0,1:T(8,128)(2,1)S(1)}, bf16[1280,320]{0,1:T(8,128)(2,1)}, u32[]{:S(2)}) copy-start(bf16[1280,320]{0,1:T(8,128)(2,1)} %param.18) | copy-start | bytes 2457604
  2.2 10.3 %collective-permute-start = (s32[2]{0:T(128)S(1)}, s32[2]{0:T(128)S(1)}, u32[]{:S(2)}, u32[]{:S(2)}) collective-permute-start(s32[2]{0:T(128)S(1)} %pad_add_fusion), channel_id=1, source_target_pairs={{0,4},{4,0},{8,12},{12,8},{16,20},{20,16},{24,28},{28,24},{1,5},{5... | collective-permute-start | bytes 32 | tf_op jit(solution)/shard_map/ppermute | solution.py:1143
  5.4 4.5 %copy-start.6 = (f32[320,1]{1,0:T(8,128)}, f32[320,1]{1,0:T(8,128)S(1)}, u32[]{:S(2)}) copy-start(f32[320,1]{1,0:T(8,128)S(1)} %broadcast_in_dim_tile.4.factor) | copy-start | bytes 3844
  8.3 1.7 copy-start.11
  8.3 2.0 copy-start.12
  8.3 2.5 copy-start.13
  12.5 132.0 %copy-start.2 = (s32[2]{0:T(128)}, s32[2]{0:T(128)S(1)}, u32[]{:S(2)}) copy-start(s32[2]{0:T(128)S(1)} %broadcast_select_fusion.span) | copy-start | bytes 28
  144.5 5.0 %copy-start = (bf16[320,2048]{1,0:T(8,128)(2,1)}, bf16[320,2048]{1,0:T(8,128)(2,1)S(1)}, u32[]{:S(2)}) copy-start(bf16[320,2048]{1,0:T(8,128)(2,1)S(1)} %get-tuple-element.25.out) | copy-start | bytes 3932164
  144.5 5.0 %copy-start.1 = (f32[4,2048]{1,0:T(4,128)}, f32[4,2048]{1,0:T(4,128)S(1)}, u32[]{:S(2)}) copy-start(f32[4,2048]{1,0:T(4,128)S(1)} %get-tuple-element.26.logsum) | copy-start | bytes 98308
  144.5 5.0 %copy-start.3 = (bf16[512,1280]{1,0:T(8,128)(2,1)S(1)}, bf16[512,1280]{1,0:T(8,128)(2,1)}, u32[]{:S(2)}) copy-start(bf16[512,1280]{1,0:T(8,128)(2,1)} %param.13) | copy-start | bytes 3932164
  149.5 2.1 copy-start.15
  153.5 3.3 copy-start.7
  165.8 3.4 copy-start.4
  177.4 160.5 %copy-start.14 = (f32[1280]{0:T(1024)S(1)}, f32[1280]{0:T(1024)}, u32[]{:S(2)}) copy-start(f32[1280]{0:T(1024)} %param.15) | copy-start | bytes 15364
  336.1 3.7 %copy-start.5 = (f32[512,1280]{1,0:T(8,128)S(1)}, f32[512,1280]{1,0:T(8,128)}, u32[]{:S(2)}) copy-start(f32[512,1280]{1,0:T(8,128)} %copy-done.4) | copy-start | bytes 7864324
  339.8 4.9 %copy-start.16 = (f32[80]{0:T(128)S(1)}, f32[80]{0:T(128)}, u32[]{:S(2)}) copy-start(f32[80]{0:T(128)} %param.17) | copy-start | bytes 964
